TPU v7x, 32 devices: a whole 2x2x4 slice. The times are simulated.
32 devices in a mesh: groups: 2 (over x), ctx: 16 (over z, y, core).
Axes of the slice: x: 2, y: 2, z: 4, core: 2. Of those that a mesh axis runs over, the one named last changes fastest.
Arguments:
- queries: bfloat16 [4096, 2048], P(('groups', 'ctx')), parts along dimension 0, may hold values from -64 to 64
- keys: bfloat16 [4096, 512], P(('groups', 'ctx')), parts along dimension 0, may hold values from -6 to 6
- values: bfloat16 [4096, 512], P(('groups', 'ctx')), parts along dimension 0, may hold values from -6 to 6
- block_ids: int32 [4096], P(('groups', 'ctx')), parts along dimension 0, may hold values from 0 to 3, as said below
- out_weight: bfloat16 [2048, 2048], P('ctx'), may hold values from -0.59765625 to 0.59765625
- summary_gain: float32 [128], replicated, may hold values from 0.1 to 1.9
- norm_gain: float32 [2048], replicated, may hold values from 0.1 to 1.9
- routes: int32 [4096, 8], P(('groups', 'ctx')), parts along dimension 0, may hold values from 0 to 15, all different within a row; in each aligned block of 128 rows (0 to 127, 128 to 255, ...) at most 80 rows name the same one
- route_scores: float32 [4096, 8], P(('groups', 'ctx')), parts along dimension 0, may hold values from 0.02 to 1
- expert_gate: bfloat16 [16, 2048, 768], P('ctx'), may hold values from -0.125 to 0.125
- expert_up: bfloat16 [16, 2048, 768], P('ctx'), may hold values from -0.125 to 0.125
- expert_down: bfloat16 [16, 768, 2048], P('ctx'), may hold values from -0.21875 to 0.21875
Outputs:
- projected: bfloat16 [4096, 2048], P(('groups', 'ctx')), parts along dimension 0
- mixed: bfloat16 [4096, 2048], P(('groups', 'ctx')), parts along dimension 0
There are 2 independent parts, one for each index of `groups`. A program takes and returns all parts, laid end to end along the dimension named above; an argument that names none is the same for every part. Nothing has to cross between parts.
Inputs may be any that keep to these rules, and one draw needn't show every extreme that they name: `block_ids`: within each context shard's 128 tokens the block numbers never fall, start at 0 and take every value up to 3. `routes`: among the 128 tokens of one context shard no expert is chosen more than 80 times, and in every draw some expert is chosen exactly 80 times by some shard. A token's 8 experts differ.
All inputs are finite; a program needn't handle non-finite values.
Results may differ from a plain program's by a relative error of at most 0.0077.
Values may be sent and summed in bfloat16 or wider, within the bound.
No kernel may reach another device: no remote copies, remote signals or barrier semaphores. Data moves between devices by JAX's collectives and lax.ppermute only.
A program may use at most 128 MiB of HBM per device.

v0:
```python
import math

import jax
import jax.numpy as jnp
from jax import lax
from jax.sharding import PartitionSpec as P

D = 2048
HQ = 16
KVH = 4
HD = 128
TOP = 8
EXP_DEV = 1
NB = 4


def normalize(x):
    return x * lax.rsqrt(jnp.mean(x * x, axis=-1, keepdims=True) + 1e-06)


def body(
    queries,
    keys,
    values,
    block_ids,
    out_weight,
    summary_gain,
    norm_gain,
    routes,
    route_scores,
    expert_gate,
    expert_up,
    expert_down,
):
    tokens_here = queries.shape[0]
    group = HQ // KVH
    scale = 1.0 / math.sqrt(HD)
    member = block_ids[None, :] == jnp.arange(NB, dtype=jnp.int32)[:, None]
    count = jnp.sum(member.astype(jnp.float32), axis=-1)
    indicator = member.astype(jnp.bfloat16)
    kmean = jnp.dot(indicator, keys, preferred_element_type=jnp.float32) / count[:, None]
    vmean = jnp.dot(indicator, values, preferred_element_type=jnp.float32) / count[:, None]
    summary_keys = (
        (normalize(kmean.reshape(NB, KVH, HD)) * summary_gain)
        .astype(jnp.bfloat16)
        .reshape(NB, KVH * HD)
    )
    summary_values = (
        normalize(vmean.reshape(NB, KVH, HD)).astype(jnp.bfloat16).reshape(NB, KVH * HD)
    )
    all_keys, all_values = (
        lax.all_gather(summary_keys, "ctx", axis=0, tiled=True),
        lax.all_gather(summary_values, "ctx", axis=0, tiled=True),
    )
    index = lax.axis_index("ctx")
    query = queries.reshape(tokens_here, KVH, group, HD)
    key_loc = keys.reshape(tokens_here, KVH, HD)
    remote_keys = all_keys.reshape(-1, KVH, HD)
    causal = jnp.arange(tokens_here)[:, None] >= jnp.arange(tokens_here)[None, :]
    owner = jnp.arange(remote_keys.shape[0], dtype=jnp.int32) // NB
    local = jnp.einsum("tkgd,skd->kgts", query, key_loc, preferred_element_type=jnp.float32) * scale
    local = jnp.where(causal[None, None], local, -jnp.inf)
    remote = (
        jnp.einsum("tkgd,skd->kgts", query, remote_keys, preferred_element_type=jnp.float32) * scale
    )
    remote = jnp.where((owner < index)[None, None, None, :], remote, -jnp.inf)
    scores = jnp.concatenate([local, remote], axis=-1)
    top = jnp.max(scores, axis=-1, keepdims=True)
    expo = jnp.exp(scores - top)
    weights = (expo / jnp.sum(expo, axis=-1, keepdims=True)).astype(jnp.bfloat16)
    every_value = jnp.concatenate(
        [values.reshape(tokens_here, KVH, HD), all_values.reshape(-1, KVH, HD)], axis=0
    )
    attended = jnp.einsum(
        "kgts,skd->tkgd", weights, every_value, preferred_element_type=jnp.float32
    )
    attended = attended.reshape(tokens_here, HQ * HD).astype(jnp.bfloat16)
    hidden = jnp.dot(
        attended,
        lax.all_gather(out_weight, "ctx", axis=0, tiled=True),
        preferred_element_type=jnp.float32,
    )
    normed = (normalize(hidden) * norm_gain).astype(jnp.bfloat16)
    combine = route_scores / jnp.sum(route_scores, axis=-1, keepdims=True)
    experts_all = EXP_DEV * lax.axis_size("ctx")
    capacity = max(2, 5 * tokens_here * TOP // (4 * experts_all))
    flat_routes = routes.reshape(-1)
    hits = (flat_routes[:, None] == jnp.arange(experts_all, dtype=jnp.int32)[None, :]).astype(
        jnp.int32
    )
    slot = jnp.sum(hits * (jnp.cumsum(hits, axis=0) - 1), axis=-1)
    target = flat_routes * capacity + slot
    source = jnp.arange(tokens_here * TOP, dtype=jnp.int32) // TOP
    outgoing = jnp.zeros((experts_all * capacity, D), jnp.bfloat16).at[target].set(normed[source])
    outgoing = outgoing.reshape(experts_all, capacity, D)
    arrived = lax.all_to_all(outgoing, "ctx", split_axis=0, concat_axis=0, tiled=True)
    senders = arrived.shape[0] // EXP_DEV
    width = arrived.shape[1]
    inputs = (
        arrived.reshape(senders, EXP_DEV, width, D)
        .transpose(1, 0, 2, 3)
        .reshape(EXP_DEV, senders * width, D)
    )
    gate = jnp.einsum("erd,edf->erf", inputs, expert_gate, preferred_element_type=jnp.float32)
    upper = jnp.einsum("erd,edf->erf", inputs, expert_up, preferred_element_type=jnp.float32)
    act = (jax.nn.silu(gate) * upper).astype(jnp.bfloat16)
    result = jnp.einsum(
        "erf,efd->erd", act, expert_down, preferred_element_type=jnp.float32
    ).astype(jnp.bfloat16)
    result = (
        result.reshape(EXP_DEV, senders, width, D)
        .transpose(1, 0, 2, 3)
        .reshape(senders * EXP_DEV, width, D)
    )
    returned = lax.all_to_all(result, "ctx", split_axis=0, concat_axis=0, tiled=True)
    returned = returned.reshape(experts_all * capacity, D)
    picked = jnp.take(returned, target, axis=0).reshape(tokens_here, TOP, D)
    blended = jnp.sum(combine[:, :, None] * picked.astype(jnp.float32), axis=1)
    return (hidden.astype(jnp.bfloat16), (hidden + blended).astype(jnp.bfloat16))


def solution(mesh):
    in_specs = (
        P(("groups", "ctx"), None),
        P(("groups", "ctx"), None),
        P(("groups", "ctx"), None),
        P(("groups", "ctx")),
        P("ctx", None),
        P(),
        P(),
        P(("groups", "ctx"), None),
        P(("groups", "ctx"), None),
        P("ctx", None, None),
        P("ctx", None, None),
        P("ctx", None, None),
    )
    out_specs = (P(("groups", "ctx"), None), P(("groups", "ctx"), None))
    return jax.shard_map(body, mesh=mesh, in_specs=in_specs, out_specs=out_specs, check_vma=False)
```

profile of v0, /device:TPU:13, one launch (start us, length us, event | category | flops | bytes accessed | tf_op | source)
XLA Modules:
  0.0 398.0 jit_solution(11848034568985104021)
XLA Ops:
  7.2 0.7 all-gather.4.cloned.1.call-update
  7.9 0.9 copy.81
  8.9 0.1 eq.42
  8.9 0.1 reshape.239
  9.0 0.9 reshape.236
  10.0 0.8 convert_reduce_fusion
  10.8 1.0 fusion.33
  11.8 0.1 reduce_sum.78
  11.9 0.7 broadcast_bitcast_fusion.2
  12.6 0.1 broadcast_bitcast_fusion
  12.7 15.9 %all-gather.1 = bf16[16,4,512]{2,1,0:T(4,128)(2,1)S(1)} all-gather(bf16[1,4,512]{2,1,0:T(4,128)(2,1)S(1)} %fusion.27), channel_id=1, replica_groups=mesh['groups'=2,'ctx'=16] {'ctx'}, dimensions={0}, use_global_device_ids=true | all-gather | bytes 69632 | tf_op jit(solution)/shard_map/all_gather | solution.py:52
  28.6 2.2 reshape.237
  30.8 1.0 copy.73
  31.8 1.1 fusion.36
  32.9 0.1 reduce_sum.77
  33.0 0.1 broadcast_bitcast_fusion.1
  33.1 21.9 %all-gather = bf16[16,4,512]{2,1,0:T(4,128)(2,1)S(1)} all-gather(bf16[1,4,512]{2,1,0:T(4,128)(2,1)S(1)} %fusion.26), channel_id=1, replica_groups=mesh['groups'=2,'ctx'=16] {'ctx'}, dimensions={0}, use_global_device_ids=true | all-gather | bytes 69632 | tf_op jit(solution)/shard_map/all_gather | solution.py:53
  55.0 0.7 reshape.235
  55.7 0.8 copy.75
  56.6 0.8 copy.74
  57.3 4.5 %reduce-window.6 = s32[16,8,128]{2,1,0:T(8,128)S(1)} reduce-window(s32[16,8,128]{2,1,0:T(8,128)S(1)} %fusion.22, s32[]{:T(128)} %constant.73.clone.1), window={size=1x1x128 pad=0_0x0_0x127_0}, to_apply=%region_7.8 | reduce-window | flops 2080768 | bytes 131076 | tf_op jit(solution)/shard_map/reduce-window
  61.8 0.1 slice.12
  61.9 0.1 copy.83
  62.2 0.6 broadcast_multiply_fusion
  62.8 0.8 copy.87
  63.5 0.7 mul.144
  64.3 1.4 fusion.35
  65.7 1.4 fusion.34
  67.1 0.1 add_add_fusion
  67.2 0.2 fusion.13
  67.5 1.3 convolution_convert_fusion.1
  68.8 16.9 %all-gather.4.cloned.1.call-done = bf16[2048,2048]{1,0:T(8,128)(2,1)} async-done(((bf16[128,2048]{1,0:T(8,128)(2,1)}), bf16[2048,2048]{1,0:T(8,128)(2,1)}) %all-gather.4.cloned.1.call-update) | async-done | bytes 8388624 | tf_op jit(solution)/shard_map/all_gather | solution.py:80
  85.7 4.9 %multiply_reduce_fusion.1 = (f32[128]{0:T(128)S(1)}, f32[128,2048]{1,0:T(8,128)S(1)}) fusion(bf16[128,2048]{0,1:T(8,128)(2,1)} %bitcast.86, bf16[2048,2048]{1,0:T(8,128)(2,1)} %all-gather.4.cloned.1.call-done), kind=kOutput, calls=%fused_computation.30 | convolution fusion | flops 1074265984 | bytes 9961984 | tf_op jit(solution)/shard_map/dot_general | solution.py:78
  90.6 1.0 copy-done.1
  91.6 1.0 multiply_convert_fusion
  92.5 24.0 %scatter_custom_fusion = bf16[1280,2048]{1,0:T(8,128)(2,1)} fusion(s32[1024]{0:T(1024)S(1)} %bitcast.93, bf16[128,2048]{1,0:T(8,128)(2,1)} %multiply_convert_fusion, s32[1024]{0:T(1024)S(1)} %broadcast_clamp_fusion.1, bf16[]{:T(256)} %constant.80.clone.1), kind=kCustom, calls=%fused_computation.6 | custom fusion | bytes 5243392 | tf_op jit(solution)/shard_map/scatter | solution.py:94
  116.6 120.3 %all_to_all.10 = bf16[16,80,2048]{2,1,0:T(8,128)(2,1)S(1)} all-to-all(bf16[16,80,2048]{2,1,0:T(8,128)(2,1)} %bitcast.82), channel_id=1, replica_groups=mesh['groups'=2,'ctx'=16] {'ctx'}, dimensions={0} | all-to-all | bytes 10485760 | tf_op jit(solution)/shard_map/all_to_all | solution.py:96
  236.9 4.3 %fusion.5 = f32[1280,768]{1,0:T(8,128)S(1)} fusion(bf16[1280,2048]{1,0:T(8,128)(2,1)S(1)} %bitcast.84, bf16[1,2048,768]{2,1,0:T(8,128)(2,1)S(1)} %copy-done.8), kind=kOutput, calls=%fused_computation.12 | convolution fusion | flops 4026531840 | bytes 12320768 | tf_op jit(solution)/shard_map/erd,edf->erf/dot_general | solution.py:104
  241.3 4.8 %fusion.2 = bf16[1280,768]{1,0:T(8,128)(2,1)S(1)} fusion(bf16[1280,2048]{1,0:T(8,128)(2,1)S(1)} %bitcast.85, f32[1280,768]{1,0:T(8,128)S(1)} %fusion.5, bf16[1,2048,768]{2,1,0:T(8,128)(2,1)S(1)} %copy-done.9), kind=kOutput, calls=%fused_computation.9 | convolution fusion | flops 4032430080 | bytes 14286848 | tf_op jit(solution)/shard_map/erd,edf->erf/dot_general | solution.py:105
  246.1 6.0 %convolution_convert_fusion = bf16[1280,2048]{1,0:T(8,128)(2,1)} fusion(bf16[1280,768]{1,0:T(8,128)(2,1)S(1)} %fusion.2, bf16[1,768,2048]{2,1,0:T(8,128)(2,1)S(1)} %copy-done), kind=kOutput, calls=%fused_computation.4 | convolution fusion | flops 4029153280 | bytes 10354688 | tf_op jit(solution)/shard_map/erf,efd->erd/dot_general | solution.py:107
  252.1 5.2 %all-to-all-start.1 = ((bf16[16,80,2048]{2,1,0:T(8,128)(2,1)}), bf16[16,80,2048]{2,1,0:T(8,128)(2,1)}, u32[]{:S(2)}, u32[]{:S(2)}) async-start(bf16[16,80,2048]{2,1,0:T(8,128)(2,1)} %bitcast.83), calls=%async_computation.1 | async-start | bytes 10485760 | tf_op jit(solution)/shard_map/all_to_all | solution.py:115
  257.3 0.1 reduce_sum.82
  257.5 0.1 copy.86
  257.7 0.1 copy.80
  257.8 114.5 %all-to-all-done.1 = bf16[16,80,2048]{2,1,0:T(8,128)(2,1)} async-done(((bf16[16,80,2048]{2,1,0:T(8,128)(2,1)}), bf16[16,80,2048]{2,1,0:T(8,128)(2,1)}, u32[]{:S(2)}, u32[]{:S(2)}) %all-to-all-start.1) | async-done | bytes 5242912 | tf_op jit(solution)/shard_map/all_to_all | solution.py:115
  372.3 12.0 %gather_fusion = bf16[1024,2048]{1,0:T(8,128)(2,1)} fusion(bf16[1280,2048]{1,0:T(8,128)(2,1)} %bitcast.23, s32[1024]{0:T(1024)S(1)} %broadcast_clamp_fusion), kind=kCustom, calls=%fused_computation.1 | custom fusion | bytes 8392704 | tf_op jit(solution)/shard_map/jit(_take)/gather | solution.py:117
  384.3 5.7 %multiply_reduce_fusion = f32[128,2048]{1,0:T(8,128)S(1)} fusion(bf16[1024,2048]{1,0:T(8,128)(2,1)} %gather_fusion, f32[128,8]{1,0:T(8,128)S(1)} %copy.80, pred[128,8]{1,0:T(8,128)(4,1)S(1)} %copy.86), kind=kLoop, calls=%fused_computation.3 | loop fusion | flops 8126464 | bytes 5248000 | tf_op jit(solution)/shard_map/reduce_sum | solution.py:118
  390.0 1.1 add_convert_fusion
  (44 shorter events, 0.5 us)
Async XLA Ops:
  7.2 238.9 %copy-start = (bf16[1,768,2048]{2,1,0:T(8,128)(2,1)S(1)}, bf16[1,768,2048]{2,1,0:T(8,128)(2,1)}, u32[]{:S(2)}) copy-start(bf16[1,768,2048]{2,1,0:T(8,128)(2,1)} %param.23) | copy-start | bytes 9437188
  7.2 55.0 %copy-start.4 = (s32[128,8]{0,1:T(8,128)S(1)}, s32[128,8]{0,1:T(8,128)}, u32[]{:S(2)}) copy-start(s32[128,8]{0,1:T(8,128)} %param.19) | copy-start | bytes 12292
  7.2 78.5 %all-gather.4.cloned.1.call-start = ((), (), s32[]{:S(2)}) async-start(), calls=%async_computation.2 | async-start | bytes 8912896 | tf_op jit(solution)/shard_map/all_gather | solution.py:80
  64.2 3.2 copy-start.5
  64.2 3.2 copy-start.3
  85.7 5.9 %copy-start.7 = (f32[2048]{0:T(1024)S(1)}, f32[2048]{0:T(1024)}, u32[]{:S(2)}) copy-start(f32[2048]{0:T(1024)} %param.18) | copy-start | bytes 24580
  90.6 1.0 copy-start.1
  116.6 120.4 %copy-start.8 = (bf16[1,2048,768]{2,1,0:T(8,128)(2,1)S(1)}, bf16[1,2048,768]{2,1,0:T(8,128)(2,1)}, u32[]{:S(2)}) copy-start(bf16[1,2048,768]{2,1,0:T(8,128)(2,1)} %param.21) | copy-start | bytes 9437188
  236.9 4.3 %copy-start.9 = (bf16[1,2048,768]{2,1,0:T(8,128)(2,1)S(1)}, bf16[1,2048,768]{2,1,0:T(8,128)(2,1)}, u32[]{:S(2)}) copy-start(bf16[1,2048,768]{2,1,0:T(8,128)(2,1)} %param.22) | copy-start | bytes 9437188
  252.1 5.5 %copy-start.6 = (f32[128,8]{0,1:T(8,128)S(1)}, f32[128,8]{0,1:T(8,128)}, u32[]{:S(2)}) copy-start(f32[128,8]{0,1:T(8,128)} %param.20) | copy-start | bytes 12292
  252.1 120.1 %all-to-all-start.1 = ((bf16[16,80,2048]{2,1,0:T(8,128)(2,1)}), bf16[16,80,2048]{2,1,0:T(8,128)(2,1)}, u32[]{:S(2)}, u32[]{:S(2)}) async-start(bf16[16,80,2048]{2,1,0:T(8,128)(2,1)} %bitcast.83), calls=%async_computation.1 | async-start | bytes 10485760 | tf_op jit(solution)/shard_map/all_to_all | solution.py:115
  384.3 5.7 %copy-start.2 = (f32[128,2048]{1,0:T(8,128)S(1)}, f32[128,2048]{1,0:T(8,128)}, u32[]{:S(2)}) copy-start(f32[128,2048]{1,0:T(8,128)} %copy-done.1) | copy-start | bytes 3145732
Sparse Core Ops, SparseCore 0:
  10.2 75.4 all-gather.3
where the time goes:
time: 399 us; the launch traced here: 398 us
  blocking collectives  158 us (40%)
  waiting for transfers between devices  132 us (33%)
  local copies, waits for them, and re-layouts  47.6 us (12%)
  matrix products  26.2 us (7%)
  other arithmetic  14.3 us (4%)
  between operations  14.3 us (4%)
  starting transfers between devices  5.22 us (1%)
    all_to_all x1, blocking collectives, body(): lax.all_to_all(outgoing, 'ctx', split_axis=0, concat_axis=0, tiled=True)  120 us
    all_to_all x1, waiting for transfers between devices, body(): lax.all_to_all(result, 'ctx', split_axis=0, concat_axis=0, tiled=True)  114 us
    scatter x1, local copies, waits for them, and re-layouts, body(): jnp.zeros((experts_all * capacity, D), jnp.bfloat16).at[target]  24 us
    all_gather x1, blocking collectives, body(): lax.all_gather(summary_values, 'ctx', axis=0, tiled=True)  21.9 us
    all_gather x1, waiting for transfers between devices, body(): lax.all_gather(out_weight, 'ctx', axis=0, tiled=True)  16.9 us
    all_gather x1, blocking collectives, body(): lax.all_gather(summary_keys, 'ctx', axis=0, tiled=True)  15.9 us
    gather x1, local copies, waits for them, and re-layouts, body(): picked = jnp.take(returned, target, axis=0).reshape(tokens_here, TOP, D)  12 us
  transfers between devices with their start and end apart: 2, of which 2 were waited for; matrix products, arithmetic and copies ran while one was open for 6% of the time, Pallas kernels for 0%

commit v1 on v0

v1 whole, which is shorter than its diff:
```python
import functools
import math

import jax
import jax.numpy as jnp
from jax import lax
from jax.experimental import pallas as pl
from jax.experimental.pallas import tpu as pltpu
from jax.sharding import PartitionSpec as P

D = 2048
HQ = 16
KVH = 4
HD = 128
TOP = 8
NB = 4
CORES = 2
VMEM_BYTES = 48 * 1024 * 1024
F32 = jnp.float32
BF16 = jnp.bfloat16


def normalize(x):
    return x * lax.rsqrt(jnp.mean(x * x, axis=-1, keepdims=True) + 1e-06)


def params():
    return pltpu.CompilerParams(vmem_limit_bytes=VMEM_BYTES)


def whole(*shape):
    return pl.BlockSpec(shape, lambda *_: (0,) * len(shape))


def summary_kernel(experts, ids, keys, values, gain, routes, scores, out, rows):
    tokens = ids.shape[1]
    block = lax.broadcasted_iota(jnp.int32, (8, tokens), 0)
    member = (ids[...] == block) & (block < NB)
    ones = jnp.where(member, 1.0, 0.0).astype(F32)
    count = jnp.maximum(jnp.sum(ones, axis=-1, keepdims=True), 1.0)
    indicator = ones.astype(BF16)
    kmean = jnp.dot(indicator, keys[...], preferred_element_type=F32) / count
    vmean = jnp.dot(indicator, values[...], preferred_element_type=F32) / count
    for g in range(KVH):
        cols = slice(g * HD, (g + 1) * HD)
        rows[8 * g : 8 * g + NB, :] = (normalize(kmean[:, cols]) * gain[...])[:NB]
        rows[8 * g + NB : 8 * g + 2 * NB, :] = normalize(vmean[:, cols])[:NB]
    base = 8 * KVH
    if experts:
        combine = scores[...] / jnp.sum(scores[...], axis=0, keepdims=True)
        expert = lax.broadcasted_iota(jnp.int32, (experts, tokens), 0)
        table = jnp.zeros((experts, tokens), F32)
        for k in range(TOP):
            table += jnp.where(routes[k : k + 1, :] == expert, combine[k : k + 1, :], 0.0)
        high = table.astype(BF16).astype(F32)
        rows[base : base + experts, :] = high
        rows[base + experts : base + 2 * experts, :] = table - high
    out[...] = rows[...].astype(BF16)


def summarize(ids, keys, values, gain, routes, scores, experts):
    tokens = ids.shape[0]
    height = 8 * KVH + 2 * experts
    return pl.pallas_call(
        functools.partial(summary_kernel, experts),
        out_shape=jax.ShapeDtypeStruct((height, HD), BF16),
        scratch_shapes=[pltpu.VMEM((height, HD), F32)],
        compiler_params=params(),
        name="summaries",
    )(ids.reshape(1, tokens), keys, values, gain.reshape(1, HD), routes.T, scores.T)


def attention_kernel(me, queries, keys, values, gathered, attended):
    tokens = queries.shape[0]
    group = HQ // KVH
    scale = 1.0 / math.sqrt(HD)
    shards = gathered.shape[0]
    wide = shards * 2 * NB
    row = lax.broadcasted_iota(jnp.int32, (tokens, tokens), 0)
    col = lax.broadcasted_iota(jnp.int32, (tokens, tokens), 1)
    causal = row >= col
    place = lax.broadcasted_iota(jnp.int32, (tokens, wide), 1)
    owner = (place // (2 * NB)) ^ me[1]
    earlier = (owner < me[0]) & (place % (2 * NB) < NB)
    seen = jnp.concatenate([causal, earlier], axis=1)
    for g in range(KVH):
        cols = slice(g * HD, (g + 1) * HD)
        pairs = gathered[:, 16 * (g // 2) : 16 * (g // 2) + 16, :].astype(F32)
        half = 8 * (g % 2)
        remote = pairs[:, half : half + 8, :].reshape(wide, HD)
        key_all = jnp.concatenate([keys[:, cols], remote.astype(BF16)], axis=0)
        shifted = pltpu.roll(remote, wide - NB, 0)
        value_all = jnp.concatenate([values[:, cols], shifted.astype(BF16)], axis=0)
        for i in range(group):
            h = g * group + i
            head = slice(h * HD, (h + 1) * HD)
            scores = (
                lax.dot_general(
                    queries[:, head],
                    key_all,
                    (((1,), (1,)), ((), ())),
                    preferred_element_type=F32,
                )
                * scale
            )
            scores = jnp.where(seen, scores, -jnp.inf)
            top = jnp.max(scores, axis=-1, keepdims=True)
            expo = jnp.exp(scores - top)
            weights = (expo / jnp.sum(expo, axis=-1, keepdims=True)).astype(BF16)
            attended[:, head] = jnp.dot(
                weights, value_all, preferred_element_type=F32
            ).astype(BF16)


def attend(me, queries, keys, values, gathered):
    tokens = queries.shape[0]
    return pl.pallas_call(
        attention_kernel,
        grid_spec=pltpu.PrefetchScalarGridSpec(
            num_scalar_prefetch=1,
            grid=(1,),
            in_specs=[whole(*a.shape) for a in (queries, keys, values, gathered)],
            out_specs=whole(tokens, HQ * HD),
        ),
        out_shape=jax.ShapeDtypeStruct((tokens, HQ * HD), BF16),
        compiler_params=params(),
        cost_estimate=pl.CostEstimate(
            flops=4 * HQ * HD * tokens * 2 * tokens,
            bytes_accessed=2 * 4 * tokens * HQ * HD,
            transcendentals=HQ * tokens * 2 * tokens,
        ),
        name="attention",
    )(me, queries, keys, values, gathered)


def project_first_kernel(chips, attended, *refs):
    blocks, acc, pair = refs[:-2], refs[-2], refs[-1]
    rows = blocks[0].shape[0]
    mine = chips[0]
    total = None
    for i in range(len(blocks) // 2):
        pair[pl.ds(pl.multiple_of(mine * rows, rows), rows), :] = blocks[2 * i][...]
        pair[pl.ds(pl.multiple_of((1 - mine) * rows, rows), rows), :] = blocks[2 * i + 1][...]
        at = pl.multiple_of(chips[i + 1] * 2 * rows, 2 * rows)
        part = jnp.dot(
            attended[:, pl.ds(at, 2 * rows)], pair[...], preferred_element_type=F32
        )
        if i == 0:
            acc[...] = part
        else:
            acc[...] += part


def project_first(chips, attended, blocks):
    tokens = attended.shape[0]
    rows, width = blocks[0].shape
    return pl.pallas_call(
        project_first_kernel,
        grid_spec=pltpu.PrefetchScalarGridSpec(
            num_scalar_prefetch=1,
            grid=(1,),
            in_specs=[whole(*attended.shape)] + [whole(rows, width)] * len(blocks),
            out_specs=whole(tokens, width),
            scratch_shapes=[pltpu.VMEM((2 * rows, width), BF16)],
        ),
        out_shape=jax.ShapeDtypeStruct((tokens, width), F32),
        compiler_params=params(),
        cost_estimate=pl.CostEstimate(
            flops=2 * tokens * rows * width * len(blocks),
            bytes_accessed=2 * rows * width * len(blocks),
            transcendentals=0,
        ),
        name="project_first",
    )(chips, attended, *blocks)


def project_last_kernel(chips, attended, acc, gain, a, b, c, d, hidden, projected, normed, pair):
    half = a.shape[0]
    rows = 2 * half
    mine = chips[0]
    own = pl.multiple_of(mine * rows, rows)
    other = pl.multiple_of((1 - mine) * rows, rows)
    pair[pl.ds(own, half), :] = a[...]
    pair[pl.ds(own + half, half), :] = b[...]
    pair[pl.ds(other, half), :] = c[...]
    pair[pl.ds(other + half, half), :] = d[...]
    at = pl.multiple_of(chips[1] * 2 * rows, 2 * rows)
    total = acc[...] + jnp.dot(
        attended[:, pl.ds(at, 2 * rows)], pair[...], preferred_element_type=F32
    )
    hidden[...] = total
    projected[...] = total.astype(BF16)
    normed[...] = (normalize(total) * gain[...]).astype(BF16)


def project_last(chips, attended, acc, gain, halves):
    tokens, width = acc.shape
    half = halves[0].shape[0]
    return pl.pallas_call(
        project_last_kernel,
        grid_spec=pltpu.PrefetchScalarGridSpec(
            num_scalar_prefetch=1,
            grid=(1,),
            in_specs=[whole(*attended.shape), whole(tokens, width), whole(1, width)]
            + [whole(half, width)] * 4,
            out_specs=[whole(tokens, width)] * 3,
            scratch_shapes=[pltpu.VMEM((4 * half, width), BF16)],
        ),
        out_shape=[
            jax.ShapeDtypeStruct((tokens, width), F32),
            jax.ShapeDtypeStruct((tokens, width), BF16),
            jax.ShapeDtypeStruct((tokens, width), BF16),
        ],
        compiler_params=params(),
        cost_estimate=pl.CostEstimate(
            flops=8 * tokens * half * width, bytes_accessed=12 * tokens * width, transcendentals=0
        ),
        name="project_last",
    )(chips, attended, acc, gain.reshape(1, width), *halves)


def expert_kernel(count, at, table, *refs):
    blocks, (gate, up, down) = refs[:count], refs[count : count + 3]
    outs = refs[count + 3 : 2 * count + 3]
    tokens, acc = refs[2 * count + 3 :]
    rows = blocks[0].shape[0]
    step = pl.program_id(0)

    @pl.when(step == 0)
    def _():
        for i in range(count):
            tokens[i * rows : (i + 1) * rows, :] = blocks[i][...]

    g = jnp.dot(tokens[...], gate[0], preferred_element_type=F32)
    u = jnp.dot(tokens[...], up[0], preferred_element_type=F32)
    act = (g / (1.0 + jnp.exp(-g)) * u).astype(BF16)
    part = jnp.dot(act, down[0], preferred_element_type=F32)

    @pl.when(step == 0)
    def _():
        acc[...] = part

    @pl.when(step != 0)
    def _():
        acc[...] += part

    @pl.when(step == pl.num_programs(0) - 1)
    def _():
        for i in range(count):
            weight = table[pl.ds(at[i], 1), :]
            weight = jnp.transpose(jnp.broadcast_to(weight, (rows, rows)))
            for j in range(acc.shape[1] // rows):
                cols = slice(j * rows, (j + 1) * rows)
                outs[i][:, cols] = (acc[i * rows : (i + 1) * rows, cols] * weight).astype(BF16)


def expert_blocks(at, table, blocks, gate, up, down):
    count = len(blocks)
    rows, width = blocks[0].shape
    ff = gate.shape[2]
    tile = 256
    return pl.pallas_call(
        functools.partial(expert_kernel, count),
        grid_spec=pltpu.PrefetchScalarGridSpec(
            num_scalar_prefetch=1,
            grid=(ff // tile,),
            in_specs=[whole(*table.shape)]
            + [whole(rows, width)] * count
            + [
                pl.BlockSpec((1, width, tile), lambda f, _: (0, 0, f)),
                pl.BlockSpec((1, width, tile), lambda f, _: (0, 0, f)),
                pl.BlockSpec((1, tile, width), lambda f, _: (0, f, 0)),
            ],
            out_specs=[whole(rows, width)] * count,
            scratch_shapes=[
                pltpu.VMEM((count * rows, width), BF16),
                pltpu.VMEM((count * rows, width), F32),
            ],
        ),
        out_shape=[jax.ShapeDtypeStruct((rows, width), BF16)] * count,
        compiler_params=params(),
        cost_estimate=pl.CostEstimate(
            flops=6 * count * rows * width * ff,
            bytes_accessed=6 * width * ff,
            transcendentals=count * rows * ff,
        ),
        name="experts",
    )(at, table, *blocks, gate, up, down)


class Ring:
    def __init__(self, n):
        self.chips = n // CORES
        self.cycle = [*range(0, self.chips, 2), *range(self.chips - 1, 0, -2)]
        self.far = self.chips // 2

    def step(self, x, by):
        pairs = []
        for p, chip in enumerate(self.cycle):
            to = self.cycle[(p + by) % self.chips]
            pairs += [(chip * CORES + c, to * CORES + c) for c in range(CORES)]
        return lax.ppermute(x, "ctx", pairs)

    def swap(self, x):
        n = self.chips * CORES
        return lax.ppermute(x, "ctx", [(i, i ^ 1) for i in range(n)])

    def table(self, n):
        place = {chip: p for p, chip in enumerate(self.cycle)}
        rows = []
        for i in range(n):
            p = place[i // CORES]
            row = [self.cycle[p]]
            for k in range(1, self.far):
                row += [self.cycle[(p - k) % self.chips], self.cycle[(p + k) % self.chips]]
            rows.append(row + [self.cycle[(p + self.far) % self.chips]])
        return rows

    def gather(self, x):
        half = x.shape[0] // 2
        levels = [[x]]
        up = down = x
        for _ in range(1, self.far):
            up, down = self.step(up, 1), self.step(down, -1)
            levels.append([up, down])
        levels.append([self.step(up[:half], 1), self.step(down[half:], -1)])
        return levels


def xor_gather(x, n):
    x = x[None]
    bit = 1
    while bit < n:
        other = lax.ppermute(x, "ctx", [(i, i ^ bit) for i in range(n)])
        x = jnp.concatenate([x, other], axis=0)
        bit *= 2
    return x


def add(*xs):
    total = xs[0].astype(F32)
    for x in xs[1:]:
        total = total + x.astype(F32)
    return total


def ring_body(
    n,
    queries,
    keys,
    values,
    block_ids,
    out_weight,
    summary_gain,
    norm_gain,
    routes,
    route_scores,
    expert_gate,
    expert_up,
    expert_down,
):
    index = lax.axis_index("ctx")
    core = index % CORES
    ring = Ring(n)
    near = jnp.asarray(ring.table(n), jnp.int32)[index]

    rows_of_weight = ring.gather(out_weight)
    sibling_rows = [[ring.swap(b) for b in level] for level in rows_of_weight]

    small = summarize(block_ids, keys, values, summary_gain, routes, route_scores, n)
    small = xor_gather(small, n)
    attended = attend(jnp.stack([index, index]), queries, keys, values, small[:, : 8 * KVH])
    base = 8 * KVH
    parts = lax.dynamic_index_in_dim(
        small[:, base:].reshape(n, 2, n, HD), index, axis=2, keepdims=False
    ).astype(F32)
    table = parts[:, 0] + parts[:, 1]

    blocks = []
    for mine, theirs in zip(rows_of_weight[:-1], sibling_rows[:-1]):
        for a, b in zip(mine, theirs):
            blocks += [a, b]
    first = jnp.concatenate([core[None], near[:-1]])
    acc = project_first(first, attended, blocks)
    last = jnp.stack([core, near[-1]])
    hidden, projected, normed = project_last(
        last, attended, acc, norm_gain, [*rows_of_weight[-1], *sibling_rows[-1]]
    )

    levels = ring.gather(normed)
    levels[-1] = [jnp.concatenate(levels[-1], axis=0)]
    partial = []
    at = 0
    for level in levels:
        others = [ring.swap(b) for b in level]
        chips = near[at : at + len(level)]
        at += len(level)
        places = jnp.concatenate([chips * CORES + core, chips * CORES + 1 - core]) ^ index
        done = expert_blocks(
            places, table, [*level, *others], expert_gate, expert_up, expert_down
        )
        kept, sent = done[: len(level)], done[len(level) :]
        partial.append([(a, ring.swap(b)) for a, b in zip(kept, sent)])

    half = queries.shape[0] // 2
    [(mine, theirs)] = partial[-1]
    far = add(mine, theirs).astype(BF16)
    up, down = ring.step(far[:half], 1), ring.step(far[half:], -1)
    for k in range(ring.far - 1, 0, -1):
        (behind, behind2), (ahead, ahead2) = partial[k]
        if k == ring.far - 1:
            zero = jnp.zeros_like(up)
            up = jnp.concatenate([up, zero], axis=0)
            down = jnp.concatenate([zero, down], axis=0)
        up = ring.step(add(ahead, ahead2, up).astype(BF16), 1)
        down = ring.step(add(behind, behind2, down).astype(BF16), -1)
    [(mine, theirs)] = partial[0]
    return projected, add(hidden, mine, theirs, up, down).astype(BF16)


def exchange_body(
    n,
    queries,
    keys,
    values,
    block_ids,
    out_weight,
    summary_gain,
    norm_gain,
    routes,
    route_scores,
    expert_gate,
    expert_up,
    expert_down,
):
    tokens_here = queries.shape[0]
    index = lax.axis_index("ctx")
    small = summarize(block_ids, keys, values, summary_gain, routes, route_scores, 0)
    small = lax.all_gather(small, "ctx", axis=0, tiled=False)
    attended = attend(jnp.stack([index, 0 * index]), queries, keys, values, small)
    hidden = jnp.dot(
        attended,
        lax.all_gather(out_weight, "ctx", axis=0, tiled=True),
        preferred_element_type=F32,
    )
    normed = (normalize(hidden) * norm_gain).astype(BF16)
    combine = route_scores / jnp.sum(route_scores, axis=-1, keepdims=True)
    held = expert_gate.shape[0]
    experts_all = held * n
    capacity = capacity_of(tokens_here, experts_all)
    flat_routes = routes.reshape(-1)
    count = tokens_here * TOP
    hits = flat_routes[:, None] == jnp.arange(experts_all, dtype=jnp.int32)[None, :]
    before = jnp.arange(count)[:, None] > jnp.arange(count)[None, :]
    ahead = jnp.dot(before.astype(BF16), hits.astype(BF16), preferred_element_type=F32)
    slot = jnp.sum(jnp.where(hits, ahead, 0.0), axis=-1).astype(jnp.int32)
    target = flat_routes * capacity + slot
    source = jnp.arange(count, dtype=jnp.int32) // TOP
    outgoing = jnp.zeros((experts_all * capacity, D), BF16).at[target].set(normed[source])
    outgoing = outgoing.reshape(experts_all, capacity, D)
    arrived = lax.all_to_all(outgoing, "ctx", split_axis=0, concat_axis=0, tiled=True)
    inputs = (
        arrived.reshape(n, held, capacity, D).transpose(1, 0, 2, 3).reshape(held, n * capacity, D)
    )
    gate = jnp.einsum("erd,edf->erf", inputs, expert_gate, preferred_element_type=F32)
    upper = jnp.einsum("erd,edf->erf", inputs, expert_up, preferred_element_type=F32)
    act = (jax.nn.silu(gate) * upper).astype(BF16)
    result = jnp.einsum("erf,efd->erd", act, expert_down, preferred_element_type=F32)
    result = (
        result.astype(BF16)
        .reshape(held, n, capacity, D)
        .transpose(1, 0, 2, 3)
        .reshape(n * held, capacity, D)
    )
    returned = lax.all_to_all(result, "ctx", split_axis=0, concat_axis=0, tiled=True)
    returned = returned.reshape(experts_all * capacity, D)
    picked = jnp.take(returned, target, axis=0).reshape(tokens_here, TOP, D)
    blended = jnp.sum(combine[:, :, None] * picked.astype(F32), axis=1)
    return (hidden.astype(BF16), (hidden + blended).astype(BF16))


def capacity_of(tokens, experts):
    return max(2, 5 * tokens * TOP // (4 * experts))


def solution(mesh):
    n = mesh.shape["ctx"]

    def body(*args):
        tokens, held = args[0].shape[0], args[9].shape[0]
        dense = tokens <= 2 * capacity_of(tokens, held * n) and held == 1
        fits = n % 4 == 0 and n & (n - 1) == 0
        return (ring_body if dense and fits else exchange_body)(n, *args)

    in_specs = (
        P(("groups", "ctx"), None),
        P(("groups", "ctx"), None),
        P(("groups", "ctx"), None),
        P(("groups", "ctx")),
        P("ctx", None),
        P(),
        P(),
        P(("groups", "ctx"), None),
        P(("groups", "ctx"), None),
        P("ctx", None, None),
        P("ctx", None, None),
        P("ctx", None, None),
    )
    out_specs = (P(("groups", "ctx"), None), P(("groups", "ctx"), None))
    return jax.shard_map(body, mesh=mesh, in_specs=in_specs, out_specs=out_specs, check_vma=False)
```

time: 399 us -> 219 us (0.55)
  the two profiles are of different devices: /device:TPU:13 before, /device:TPU:0 now
where the time goes in v1:
time: 219 us; the launch traced here: 218 us
  waiting for transfers between devices  113 us (52%)
  Pallas kernels  50.8 us (23%)
  starting transfers between devices  34.7 us (16%)
  local copies, waits for them, and re-layouts  12.9 us (6%)
  other arithmetic  4.02 us (2%)
  between operations  2.52 us (1%)
    ppermute x24, waiting for transfers between devices, step(): return lax.ppermute(x, 'ctx', pairs)  94.8 us
    pallas_call x5, Pallas kernels, expert_blocks(): pl.pallas_call(functools.partial(expert_kernel, count), grid_spec=pltpu.P...  41.9 us
    ppermute x24, starting transfers between devices, step(): return lax.ppermute(x, 'ctx', pairs)  26 us
    ppermute x4, waiting for transfers between devices, xor_gather(): other = lax.ppermute(x, 'ctx', [(i, i ^ bit) for i in range(n)])  17.4 us
    unnamed x39, local copies, waits for them, and re-layouts  10.4 us
    pallas_call x1, Pallas kernels, project_first(): pl.pallas_call(project_first_kernel, grid_spec=pltpu.PrefetchScalarGridSp...  4.78 us
    ppermute x25, starting transfers between devices, swap(): return lax.ppermute(x, 'ctx', [(i, i ^ 1) for i in range(n)])  4.72 us
  transfers between devices with their start and end apart: 53, of which 21 were waited for; matrix products, arithmetic and copies ran while one was open for 2% of the time, Pallas kernels for 22%

profile of v1, /device:TPU:0, one launch (start us, length us, event | category | flops | bytes accessed | tf_op | source)
XLA Modules:
  0.0 218.4 jit_solution(521023971025756012)
XLA Ops:
  0.6 3.1 %collective-permute-start.5 = (bf16[128,2048]{1,0:T(8,128)(2,1)}, bf16[128,2048]{1,0:T(8,128)(2,1)S(1)}, u32[]{:S(2)}, u32[]{:S(2)}) collective-permute-start(bf16[128,2048]{1,0:T(8,128)(2,1)} %refs_0_.1), channel_id=1, source_target_pairs={{0,4},{1,5},{4,8},{5,9},{8,12},{9,13},{12,14},{13,15},{14,10},{15,... | collective-permute-start | bytes 1572872 | tf_op jit(solution)/shard_map/ppermute | solution.py:302
  3.7 12.1 %collective-permute-done.5.refs_2_ = bf16[128,2048]{1,0:T(8,128)(2,1)S(1)} collective-permute-done((bf16[128,2048]{1,0:T(8,128)(2,1)}, bf16[128,2048]{1,0:T(8,128)(2,1)S(1)}, u32[]{:S(2)}, u32[]{:S(2)}) %collective-permute-start.5) | collective-permute-done | bytes 524320 | tf_op jit(solution)/shard_map/ppermute | solution.py:302
  15.8 1.8 collective-permute-start.9
  17.6 0.9 copy-done.5
  18.5 0.9 copy-done.7
  23.8 5.1 %collective-permute-done.9.refs_6_ = bf16[128,2048]{1,0:T(8,128)(2,1)S(1)} collective-permute-done((bf16[128,2048]{1,0:T(8,128)(2,1)S(1)}, bf16[128,2048]{1,0:T(8,128)(2,1)S(1)}, u32[]{:S(2)}, u32[]{:S(2)}) %collective-permute-start.9) | collective-permute-done | bytes 524320 | tf_op jit(solution)/shard_map/ppermute | solution.py:302
  28.9 1.5 collective-permute-start.13
  31.8 5.7 %collective-permute-done.11.refs_8_ = bf16[128,2048]{1,0:T(8,128)(2,1)S(1)} collective-permute-done((bf16[128,2048]{1,0:T(8,128)(2,1)S(1)}, bf16[128,2048]{1,0:T(8,128)(2,1)S(1)}, u32[]{:S(2)}, u32[]{:S(2)}) %collective-permute-start.11) | collective-permute-done | bytes 524320 | tf_op jit(solution)/shard_map/ppermute | solution.py:302
  38.1 3.7 %collective-permute-done.1 = bf16[2,64,128]{2,1,0:T(8,128)(2,1)S(1)} collective-permute-done((bf16[2,64,128]{2,1,0:T(8,128)(2,1)S(1)}, bf16[2,64,128]{2,1,0:T(8,128)(2,1)S(1)}, u32[]{:S(2)}, u32[]{:S(2)}) %collective-permute-start.1) | collective-permute-done | bytes 32800 | tf_op jit(solution)/shard_map/ppermute | solution.py:334
  42.0 10.0 %collective-permute-done.2 = bf16[4,64,128]{2,1,0:T(8,128)(2,1)S(1)} collective-permute-done((bf16[4,64,128]{2,1,0:T(8,128)(2,1)S(1)}, bf16[4,64,128]{2,1,0:T(8,128)(2,1)S(1)}, u32[]{:S(2)}, u32[]{:S(2)}) %collective-permute-start.2) | collective-permute-done | bytes 65568 | tf_op jit(solution)/shard_map/ppermute | solution.py:334
  52.5 2.7 %collective-permute-start.3 = (bf16[8,64,128]{2,1,0:T(8,128)(2,1)S(1)}, bf16[8,64,128]{2,1,0:T(8,128)(2,1)S(1)}, u32[]{:S(2)}, u32[]{:S(2)}) collective-permute-start(bf16[8,64,128]{2,1,0:T(8,128)(2,1)S(1)} %pad_maximum_fusion), channel_id=1, source_target_pairs={{0,8},{1,9},{2,10},{3,11},{4,12},{5,13},{6,14},{7,15},{8,0},{9,1},... | collective-permute-start | bytes 393224 | tf_op jit(solution)/shard_map/ppermute | solution.py:334
  56.0 1.0 slice.78
  57.0 3.7 %collective-permute-done.3 = bf16[8,64,128]{2,1,0:T(8,128)(2,1)S(1)} collective-permute-done((bf16[8,64,128]{2,1,0:T(8,128)(2,1)S(1)}, bf16[8,64,128]{2,1,0:T(8,128)(2,1)S(1)}, u32[]{:S(2)}, u32[]{:S(2)}) %collective-permute-start.3) | collective-permute-done | bytes 131104 | tf_op jit(solution)/shard_map/ppermute | solution.py:334
  60.7 2.0 collective-permute-start.18
  63.3 6.1 %collective-permute-done.17.a = bf16[64,2048]{1,0:T(8,128)(2,1)S(1)} collective-permute-done((bf16[64,2048]{1,0:T(8,128)(2,1)S(1)}, bf16[64,2048]{1,0:T(8,128)(2,1)S(1)}, u32[]{:S(2)}, u32[]{:S(2)}) %collective-permute-start.17) | collective-permute-done | bytes 262176 | tf_op jit(solution)/shard_map/ppermute | solution.py:302
  70.0 1.0 copy-done.4
  71.0 0.9 copy-done.6
  71.9 0.9 copy-done.8
  72.8 2.1 attention.1.attended
  76.6 4.8 %project_first.1.acc = f32[128,2048]{1,0:T(8,128)} custom-call(s32[8]{0:T(128)S(1)} %pad_add_fusion.2.chips, bf16[128,2048]{1,0:T(8,128)(2,1)S(1)} %attention.1.attended, bf16[128,2048]{1,0:T(8,128)(2,1)S(1)} %copy-done.3, bf16[128,2048]{1,0:T(8,128)(2,1)S(1)} %collective-permute-done.4.refs_1_, bf16[128,2048]{1,0:T(8,128)(2,1)S(1)} %collective-permute-done.5.refs_2_, ...), custom_call_target="tpu_custom_call" | custom-call | flops 939524096 | bytes 7340032 | tf_op jit(solution)/shard_map/project_first/pallas_call | solution.py:157
  81.4 1.4 copy-done.2
  82.8 1.7 project_last.1
  84.5 1.2 collective-permute-start.23
  85.7 0.8 collective-permute-start.24
  86.6 11.9 %collective-permute-done.23.refs_0_ = bf16[128,2048]{1,0:T(8,128)(2,1)S(1)} collective-permute-done((bf16[128,2048]{1,0:T(8,128)(2,1)S(1)}, bf16[128,2048]{1,0:T(8,128)(2,1)S(1)}, u32[]{:S(2)}, u32[]{:S(2)}) %collective-permute-start.23) | collective-permute-done | bytes 524320 | tf_op jit(solution)/shard_map/ppermute | solution.py:302
  98.4 1.6 collective-permute-start.28
  100.4 11.5 %collective-permute-done.28.refs_0_ = bf16[128,2048]{1,0:T(8,128)(2,1)S(1)} collective-permute-done((bf16[128,2048]{1,0:T(8,128)(2,1)S(1)}, bf16[128,2048]{1,0:T(8,128)(2,1)S(1)}, u32[]{:S(2)}, u32[]{:S(2)}) %collective-permute-start.28) | collective-permute-done | bytes 524320 | tf_op jit(solution)/shard_map/ppermute | solution.py:302
  111.9 1.7 collective-permute-start.33
  114.9 9.7 %collective-permute-done.33.refs_0_ = bf16[128,2048]{1,0:T(8,128)(2,1)S(1)} collective-permute-done((bf16[128,2048]{1,0:T(8,128)(2,1)S(1)}, bf16[128,2048]{1,0:T(8,128)(2,1)S(1)}, u32[]{:S(2)}, u32[]{:S(2)}) %collective-permute-start.33) | collective-permute-done | bytes 524320 | tf_op jit(solution)/shard_map/ppermute | solution.py:302
  124.6 1.7 collective-permute-start.38
  127.9 3.1 %collective-permute-done.38 = bf16[64,2048]{1,0:T(8,128)(2,1)S(1)} collective-permute-done((bf16[64,2048]{1,0:T(8,128)(2,1)S(1)}, bf16[64,2048]{1,0:T(8,128)(2,1)S(1)}, u32[]{:S(2)}, u32[]{:S(2)}) %collective-permute-start.38) | collective-permute-done | bytes 262176 | tf_op jit(solution)/shard_map/ppermute | solution.py:302
  131.0 2.1 collective-permute-done.39
  134.0 1.2 collective-permute-done.40.refs_1_
  135.2 6.6 %experts.9 = (bf16[128,2048]{1,0:T(8,128)(2,1)S(1)}, bf16[128,2048]{1,0:T(8,128)(2,1)S(1)}) custom-call(s32[2]{0:T(128)S(1)} %add_xor_fusion.4.at, f32[16,128]{1,0:T(8,128)S(1)} %fusion.table, bf16[128,2048]{1,0:T(8,128)(2,1)S(1)} %constant_dynamic-update-slice_fusion.5.refs_0_, bf16[128,2048]{1,0:T(8,128)(2,1)S(1)} %collective-permute-done.40.refs_1_, ...), custom_call_target="tpu_custom_call" | custom-call | flops 2415919104 | bytes 9437184 | tf_op jit(solution)/shard_map/experts/pallas_call | solution.py:262
  143.1 9.5 %experts.8 = (bf16[128,2048]{1,0:T(8,128)(2,1)S(1)}, bf16[128,2048]{1,0:T(8,128)(2,1)S(1)}, bf16[128,2048]{1,0:T(8,128)(2,1)S(1)}, bf16[128,2048]{1,0:T(8,128)(2,1)S(1)}) custom-call(s32[4]{0:T(128)S(1)} %add_xor_fusion.3.at, f32[16,128]{1,0:T(8,128)S(1)} %fusion.table, bf16[128,2048]{1,0:T(8,128)(2,1)S(1)} %collective-permute-done.33.refs_0_, ...), custom_call_target="tpu_custom_call" | custom-call | flops 4831838208 | bytes 9437184 | tf_op jit(solution)/shard_map/experts/pallas_call | solution.py:262
  153.5 1.9 collective-permute-start.42
  155.4 9.5 %experts.7 = (bf16[128,2048]{1,0:T(8,128)(2,1)S(1)}, bf16[128,2048]{1,0:T(8,128)(2,1)S(1)}, bf16[128,2048]{1,0:T(8,128)(2,1)S(1)}, bf16[128,2048]{1,0:T(8,128)(2,1)S(1)}) custom-call(s32[4]{0:T(128)S(1)} %add_xor_fusion.2.at, f32[16,128]{1,0:T(8,128)S(1)} %fusion.table, bf16[128,2048]{1,0:T(8,128)(2,1)S(1)} %collective-permute-done.28.refs_0_, ...), custom_call_target="tpu_custom_call" | custom-call | flops 4831838208 | bytes 9437184 | tf_op jit(solution)/shard_map/experts/pallas_call | solution.py:262
  165.8 7.9 %collective-permute-done.49 = bf16[64,2048]{1,0:T(8,128)(2,1)S(1)} collective-permute-done((bf16[64,2048]{1,0:T(8,128)(2,1)S(1)}, bf16[64,2048]{1,0:T(8,128)(2,1)S(1)}, u32[]{:S(2)}, u32[]{:S(2)}) %collective-permute-start.49) | collective-permute-done | bytes 262176 | tf_op jit(solution)/shard_map/ppermute | solution.py:302
  173.7 1.4 collective-permute-start.43
  176.1 9.5 %experts.6 = (bf16[128,2048]{1,0:T(8,128)(2,1)S(1)}, bf16[128,2048]{1,0:T(8,128)(2,1)S(1)}, bf16[128,2048]{1,0:T(8,128)(2,1)S(1)}, bf16[128,2048]{1,0:T(8,128)(2,1)S(1)}) custom-call(s32[4]{0:T(128)S(1)} %add_xor_fusion.1.at, f32[16,128]{1,0:T(8,128)S(1)} %fusion.table, bf16[128,2048]{1,0:T(8,128)(2,1)S(1)} %collective-permute-done.23.refs_0_, ...), custom_call_target="tpu_custom_call" | custom-call | flops 4831838208 | bytes 9437184 | tf_op jit(solution)/shard_map/experts/pallas_call | solution.py:262
  185.9 1.3 collective-permute-done.43
  187.5 1.5 collective-permute-start.44
  190.7 6.6 %experts.5 = (bf16[128,2048]{1,0:T(8,128)(2,1)S(1)}, bf16[128,2048]{1,0:T(8,128)(2,1)S(1)}) custom-call(s32[2]{0:T(128)S(1)} %add_xor_fusion.at, f32[16,128]{1,0:T(8,128)S(1)} %fusion.table, bf16[128,2048]{1,0:T(8,128)(2,1)S(1)} %get-tuple-element.23.refs_0_, bf16[128,2048]{1,0:T(8,128)(2,1)S(1)} %collective-permute-done.21.refs_1_, ...), custom_call_target="tpu_custom_call" | custom-call | flops 2415919104 | bytes 9437184 | tf_op jit(solution)/shard_map/experts/pallas_call | solution.py:262
  197.4 4.5 %collective-permute-done.44 = bf16[128,2048]{1,0:T(8,128)(2,1)S(1)} collective-permute-done((bf16[128,2048]{1,0:T(8,128)(2,1)S(1)}, bf16[128,2048]{1,0:T(8,128)(2,1)S(1)}, u32[]{:S(2)}, u32[]{:S(2)}) %collective-permute-start.44) | collective-permute-done | bytes 524320 | tf_op jit(solution)/shard_map/ppermute | solution.py:302
  202.1 1.5 collective-permute-start.45
  204.5 11.2 %collective-permute-done.45 = bf16[128,2048]{1,0:T(8,128)(2,1)S(1)} collective-permute-done((bf16[128,2048]{1,0:T(8,128)(2,1)S(1)}, bf16[128,2048]{1,0:T(8,128)(2,1)S(1)}, u32[]{:S(2)}, u32[]{:S(2)}) %collective-permute-start.45) | collective-permute-done | bytes 524320 | tf_op jit(solution)/shard_map/ppermute | solution.py:302
  215.7 1.5 collective-permute-done.52
  217.2 1.2 add_convert_fusion
  (140 shorter events, 20.5 us)
Async XLA Ops:
  0.6 15.2 %collective-permute-start.5 = (bf16[128,2048]{1,0:T(8,128)(2,1)}, bf16[128,2048]{1,0:T(8,128)(2,1)S(1)}, u32[]{:S(2)}, u32[]{:S(2)}) collective-permute-start(bf16[128,2048]{1,0:T(8,128)(2,1)} %refs_0_.1), channel_id=1, source_target_pairs={{0,4},{1,5},{4,8},{5,9},{8,12},{9,13},{12,14},{13,15},{14,10},{15,... | collective-permute-start | bytes 1572872 | tf_op jit(solution)/shard_map/ppermute | solution.py:302
  3.7 19.9 %collective-permute-start.7 = (bf16[128,2048]{1,0:T(8,128)(2,1)}, bf16[128,2048]{1,0:T(8,128)(2,1)S(1)}, u32[]{:S(2)}, u32[]{:S(2)}) collective-permute-start(bf16[128,2048]{1,0:T(8,128)(2,1)} %refs_0_.1), channel_id=1, source_target_pairs={{0,2},{1,3},{4,0},{5,1},{8,4},{9,5},{12,8},{13,9},{14,12},{15,13},... | collective-permute-start | bytes 1572872 | tf_op jit(solution)/shard_map/ppermute | solution.py:302
  15.8 13.1 %collective-permute-start.9 = (bf16[128,2048]{1,0:T(8,128)(2,1)S(1)}, bf16[128,2048]{1,0:T(8,128)(2,1)S(1)}, u32[]{:S(2)}, u32[]{:S(2)}) collective-permute-start(bf16[128,2048]{1,0:T(8,128)(2,1)S(1)} %collective-permute-done.5.refs_2_), channel_id=1, source_target_pairs={{0,4},{1,5},{4,8},{5,9},{8,12},{9,13},{12,14},{13,15},{14,10},{15,... | collective-permute-start | bytes 1572872 | tf_op jit(solution)/shard_map/ppermute | solution.py:302
  17.6 43.1 %collective-permute-start.4 = (bf16[128,2048]{1,0:T(8,128)(2,1)}, bf16[128,2048]{1,0:T(8,128)(2,1)S(1)}, u32[]{:S(2)}, u32[]{:S(2)}) collective-permute-start(bf16[128,2048]{1,0:T(8,128)(2,1)} %refs_0_.1), channel_id=1, source_target_pairs={{0,1},{1,0},{2,3},{3,2},{4,5},{5,4},{6,7},{7,6},{8,9},{9,8},{10,11... | collective-permute-start | bytes 1572872 | tf_op jit(solution)/shard_map/ppermute | solution.py:306
  22.3 8.7 %collective-permute-start = (bf16[1,64,128]{2,1,0:T(8,128)(2,1)S(1)}, bf16[1,64,128]{2,1,0:T(8,128)(2,1)S(1)}, u32[]{:S(2)}, u32[]{:S(2)}) collective-permute-start(bf16[1,64,128]{2,1,0:T(8,128)(2,1)S(1)} %bitcast.33), channel_id=1, source_target_pairs={{0,1},{1,0},{2,3},{3,2},{4,5},{5,4},{6,7},{7,6},{8,9},{9,8},{10,11... | collective-permute-start | bytes 49160 | tf_op jit(solution)/shard_map/ppermute | solution.py:334
  23.6 13.9 %collective-permute-start.11 = (bf16[128,2048]{1,0:T(8,128)(2,1)S(1)}, bf16[128,2048]{1,0:T(8,128)(2,1)S(1)}, u32[]{:S(2)}, u32[]{:S(2)}) collective-permute-start(bf16[128,2048]{1,0:T(8,128)(2,1)S(1)} %collective-permute-done.7.refs_4_), channel_id=1, source_target_pairs={{0,2},{1,3},{4,0},{5,1},{8,4},{9,5},{12,8},{13,9},{14,12},{15,13},... | collective-permute-start | bytes 1572872 | tf_op jit(solution)/shard_map/ppermute | solution.py:302
  28.9 23.1 %collective-permute-start.13 = (bf16[128,2048]{1,0:T(8,128)(2,1)S(1)}, bf16[128,2048]{1,0:T(8,128)(2,1)}, u32[]{:S(2)}, u32[]{:S(2)}) collective-permute-start(bf16[128,2048]{1,0:T(8,128)(2,1)S(1)} %collective-permute-done.9.refs_6_), channel_id=1, source_target_pairs={{0,4},{1,5},{4,8},{5,9},{8,12},{9,13},{12,14},{13,15},{14,10},{15,... | collective-permute-start | bytes 1572872 | tf_op jit(solution)/shard_map/ppermute | solution.py:302
  31.1 10.7 %collective-permute-start.1 = (bf16[2,64,128]{2,1,0:T(8,128)(2,1)S(1)}, bf16[2,64,128]{2,1,0:T(8,128)(2,1)S(1)}, u32[]{:S(2)}, u32[]{:S(2)}) collective-permute-start(bf16[2,64,128]{2,1,0:T(8,128)(2,1)S(1)} %pad_maximum_fusion.2), channel_id=1, source_target_pairs={{0,2},{1,3},{2,0},{3,1},{4,6},{5,7},{6,4},{7,5},{8,10},{9,11},{10,... | collective-permute-start | bytes 98312 | tf_op jit(solution)/shard_map/ppermute | solution.py:334
  37.5 15.1 %collective-permute-start.15 = (bf16[128,2048]{1,0:T(8,128)(2,1)S(1)}, bf16[128,2048]{1,0:T(8,128)(2,1)S(1)}, u32[]{:S(2)}, u32[]{:S(2)}) collective-permute-start(bf16[128,2048]{1,0:T(8,128)(2,1)S(1)} %collective-permute-done.11.refs_8_), channel_id=1, source_target_pairs={{0,2},{1,3},{4,0},{5,1},{8,4},{9,5},{12,8},{13,9},{14,12},{15,13},... | collective-permute-start | bytes 1572872 | tf_op jit(solution)/shard_map/ppermute | solution.py:302
  41.8 10.2 %collective-permute-start.2 = (bf16[4,64,128]{2,1,0:T(8,128)(2,1)S(1)}, bf16[4,64,128]{2,1,0:T(8,128)(2,1)S(1)}, u32[]{:S(2)}, u32[]{:S(2)}) collective-permute-start(bf16[4,64,128]{2,1,0:T(8,128)(2,1)S(1)} %pad_maximum_fusion.1), channel_id=1, source_target_pairs={{0,4},{1,5},{2,6},{3,7},{4,0},{5,1},{6,2},{7,3},{8,12},{9,13},{10,... | collective-permute-start | bytes 196616 | tf_op jit(solution)/shard_map/ppermute | solution.py:334
  42.0 18.8 %collective-permute-start.6 = (bf16[128,2048]{1,0:T(8,128)(2,1)S(1)}, bf16[128,2048]{1,0:T(8,128)(2,1)S(1)}, u32[]{:S(2)}, u32[]{:S(2)}) collective-permute-start(bf16[128,2048]{1,0:T(8,128)(2,1)S(1)} %collective-permute-done.5.refs_2_), channel_id=1, source_target_pairs={{0,1},{1,0},{2,3},{3,2},{4,5},{5,4},{6,7},{7,6},{8,9},{9,8},{10,11... | collective-permute-start | bytes 1572872 | tf_op jit(solution)/shard_map/ppermute | solution.py:306
  52.0 10.8 %collective-permute-start.8 = (bf16[128,2048]{1,0:T(8,128)(2,1)S(1)}, bf16[128,2048]{1,0:T(8,128)(2,1)S(1)}, u32[]{:S(2)}, u32[]{:S(2)}) collective-permute-start(bf16[128,2048]{1,0:T(8,128)(2,1)S(1)} %collective-permute-done.7.refs_4_), channel_id=1, source_target_pairs={{0,1},{1,0},{2,3},{3,2},{4,5},{5,4},{6,7},{7,6},{8,9},{9,8},{10,11... | collective-permute-start | bytes 1572872 | tf_op jit(solution)/shard_map/ppermute | solution.py:306
  52.0 10.8 %collective-permute-start.10 = (bf16[128,2048]{1,0:T(8,128)(2,1)S(1)}, bf16[128,2048]{1,0:T(8,128)(2,1)S(1)}, u32[]{:S(2)}, u32[]{:S(2)}) collective-permute-start(bf16[128,2048]{1,0:T(8,128)(2,1)S(1)} %collective-permute-done.9.refs_6_), channel_id=1, source_target_pairs={{0,1},{1,0},{2,3},{3,2},{4,5},{5,4},{6,7},{7,6},{8,9},{9,8},{10,11... | collective-permute-start | bytes 1572872 | tf_op jit(solution)/shard_map/ppermute | solution.py:306
  60.7 14.3 %collective-permute-start.12 = (bf16[128,2048]{1,0:T(8,128)(2,1)S(1)}, bf16[128,2048]{1,0:T(8,128)(2,1)S(1)}, u32[]{:S(2)}, u32[]{:S(2)}) collective-permute-start(bf16[128,2048]{1,0:T(8,128)(2,1)S(1)} %collective-permute-done.11.refs_8_), channel_id=1, source_target_pairs={{0,1},{1,0},{2,3},{3,2},{4,5},{5,4},{6,7},{7,6},{8,9},{9,8},{10,11... | collective-permute-start | bytes 1572872 | tf_op jit(solution)/shard_map/ppermute | solution.py:306
  60.7 8.7 %collective-permute-start.17 = (bf16[64,2048]{1,0:T(8,128)(2,1)S(1)}, bf16[64,2048]{1,0:T(8,128)(2,1)S(1)}, u32[]{:S(2)}, u32[]{:S(2)}) collective-permute-start(bf16[64,2048]{1,0:T(8,128)(2,1)S(1)} %slice.78), channel_id=1, source_target_pairs={{0,4},{1,5},{4,8},{5,9},{8,12},{9,13},{12,14},{13,15},{14,10},{15,... | collective-permute-start | bytes 786440 | tf_op jit(solution)/shard_map/ppermute | solution.py:302
  60.7 8.8 %collective-permute-start.18 = (bf16[64,2048]{1,0:T(8,128)(2,1)S(1)}, bf16[64,2048]{1,0:T(8,128)(2,1)S(1)}, u32[]{:S(2)}, u32[]{:S(2)}) collective-permute-start(bf16[64,2048]{1,0:T(8,128)(2,1)S(1)} %slice.79), channel_id=1, source_target_pairs={{0,2},{1,3},{4,0},{5,1},{8,4},{9,5},{12,8},{13,9},{14,12},{15,13},... | collective-permute-start | bytes 786440 | tf_op jit(solution)/shard_map/ppermute | solution.py:302
  62.8 12.2 %collective-permute-start.14 = (bf16[128,2048]{1,0:T(8,128)(2,1)}, bf16[128,2048]{1,0:T(8,128)(2,1)S(1)}, u32[]{:S(2)}, u32[]{:S(2)}) collective-permute-start(bf16[128,2048]{1,0:T(8,128)(2,1)} %collective-permute-done.13.refs_10_), channel_id=1, source_target_pairs={{0,1},{1,0},{2,3},{3,2},{4,5},{5,4},{6,7},{7,6},{8,9},{9,8},{10,11... | collective-permute-start | bytes 1572872 | tf_op jit(solution)/shard_map/ppermute | solution.py:306
  62.8 12.2 %collective-permute-start.16 = (bf16[128,2048]{1,0:T(8,128)(2,1)S(1)}, bf16[128,2048]{1,0:T(8,128)(2,1)S(1)}, u32[]{:S(2)}, u32[]{:S(2)}) collective-permute-start(bf16[128,2048]{1,0:T(8,128)(2,1)S(1)} %collective-permute-done.15.refs_12_), channel_id=1, source_target_pairs={{0,1},{1,0},{2,3},{3,2},{4,5},{5,4},{6,7},{7,6},{8,9},{9,8},{10,11... | collective-permute-start | bytes 1572872 | tf_op jit(solution)/shard_map/ppermute | solution.py:306
  69.4 12.0 %collective-permute-start.19 = (bf16[64,2048]{1,0:T(8,128)(2,1)S(1)}, bf16[64,2048]{1,0:T(8,128)(2,1)S(1)}, u32[]{:S(2)}, u32[]{:S(2)}) collective-permute-start(bf16[64,2048]{1,0:T(8,128)(2,1)S(1)} %collective-permute-done.17.a), channel_id=1, source_target_pairs={{0,1},{1,0},{2,3},{3,2},{4,5},{5,4},{6,7},{7,6},{8,9},{9,8},{10,11... | collective-permute-start | bytes 786440 | tf_op jit(solution)/shard_map/ppermute | solution.py:306
  69.5 11.9 %collective-permute-start.20 = (bf16[64,2048]{1,0:T(8,128)(2,1)S(1)}, bf16[64,2048]{1,0:T(8,128)(2,1)S(1)}, u32[]{:S(2)}, u32[]{:S(2)}) collective-permute-start(bf16[64,2048]{1,0:T(8,128)(2,1)S(1)} %collective-permute-done.18.b), channel_id=1, source_target_pairs={{0,1},{1,0},{2,3},{3,2},{4,5},{5,4},{6,7},{7,6},{8,9},{9,8},{10,11... | collective-permute-start | bytes 786440 | tf_op jit(solution)/shard_map/ppermute | solution.py:306
  84.5 13.9 %collective-permute-start.23 = (bf16[128,2048]{1,0:T(8,128)(2,1)S(1)}, bf16[128,2048]{1,0:T(8,128)(2,1)S(1)}, u32[]{:S(2)}, u32[]{:S(2)}) collective-permute-start(bf16[128,2048]{1,0:T(8,128)(2,1)S(1)} %get-tuple-element.23.refs_0_), channel_id=1, source_target_pairs={{0,4},{1,5},{4,8},{5,9},{8,12},{9,13},{12,14},{13,15},{14,10},{15,... | collective-permute-start | bytes 1572872 | tf_op jit(solution)/shard_map/ppermute | solution.py:302
  85.7 14.3 %collective-permute-start.24 = (bf16[128,2048]{1,0:T(8,128)(2,1)S(1)}, bf16[128,2048]{1,0:T(8,128)(2,1)S(1)}, u32[]{:S(2)}, u32[]{:S(2)}) collective-permute-start(bf16[128,2048]{1,0:T(8,128)(2,1)S(1)} %get-tuple-element.23.refs_0_), channel_id=1, source_target_pairs={{0,2},{1,3},{4,0},{5,1},{8,4},{9,5},{12,8},{13,9},{14,12},{15,13},... | collective-permute-start | bytes 1572872 | tf_op jit(solution)/shard_map/ppermute | solution.py:302
  98.4 13.5 %collective-permute-start.28 = (bf16[128,2048]{1,0:T(8,128)(2,1)S(1)}, bf16[128,2048]{1,0:T(8,128)(2,1)S(1)}, u32[]{:S(2)}, u32[]{:S(2)}) collective-permute-start(bf16[128,2048]{1,0:T(8,128)(2,1)S(1)} %collective-permute-done.23.refs_0_), channel_id=1, source_target_pairs={{0,4},{1,5},{4,8},{5,9},{8,12},{9,13},{12,14},{13,15},{14,10},{15,... | collective-permute-start | bytes 1572872 | tf_op jit(solution)/shard_map/ppermute | solution.py:302
  100.0 14.2 %collective-permute-start.29 = (bf16[128,2048]{1,0:T(8,128)(2,1)S(1)}, bf16[128,2048]{1,0:T(8,128)(2,1)S(1)}, u32[]{:S(2)}, u32[]{:S(2)}) collective-permute-start(bf16[128,2048]{1,0:T(8,128)(2,1)S(1)} %collective-permute-done.24.refs_1_), channel_id=1, source_target_pairs={{0,2},{1,3},{4,0},{5,1},{8,4},{9,5},{12,8},{13,9},{14,12},{15,13},... | collective-permute-start | bytes 1572872 | tf_op jit(solution)/shard_map/ppermute | solution.py:302
  111.9 12.7 %collective-permute-start.33 = (bf16[128,2048]{1,0:T(8,128)(2,1)S(1)}, bf16[128,2048]{1,0:T(8,128)(2,1)S(1)}, u32[]{:S(2)}, u32[]{:S(2)}) collective-permute-start(bf16[128,2048]{1,0:T(8,128)(2,1)S(1)} %collective-permute-done.28.refs_0_), channel_id=1, source_target_pairs={{0,4},{1,5},{4,8},{5,9},{8,12},{9,13},{12,14},{13,15},{14,10},{15,... | collective-permute-start | bytes 1572872 | tf_op jit(solution)/shard_map/ppermute | solution.py:302
  114.3 12.4 %collective-permute-start.34 = (bf16[128,2048]{1,0:T(8,128)(2,1)S(1)}, bf16[128,2048]{1,0:T(8,128)(2,1)S(1)}, u32[]{:S(2)}, u32[]{:S(2)}) collective-permute-start(bf16[128,2048]{1,0:T(8,128)(2,1)S(1)} %collective-permute-done.29.refs_1_), channel_id=1, source_target_pairs={{0,2},{1,3},{4,0},{5,1},{8,4},{9,5},{12,8},{13,9},{14,12},{15,13},... | collective-permute-start | bytes 1572872 | tf_op jit(solution)/shard_map/ppermute | solution.py:302
  133.3 9.3 %collective-permute-start.35 = (bf16[128,2048]{1,0:T(8,128)(2,1)S(1)}, bf16[128,2048]{1,0:T(8,128)(2,1)S(1)}, u32[]{:S(2)}, u32[]{:S(2)}) collective-permute-start(bf16[128,2048]{1,0:T(8,128)(2,1)S(1)} %collective-permute-done.33.refs_0_), channel_id=1, source_target_pairs={{0,1},{1,0},{2,3},{3,2},{4,5},{5,4},{6,7},{7,6},{8,9},{9,8},{10,11... | collective-permute-start | bytes 1572872 | tf_op jit(solution)/shard_map/ppermute | solution.py:306
  133.9 9.1 %collective-permute-start.36 = (bf16[128,2048]{1,0:T(8,128)(2,1)S(1)}, bf16[128,2048]{1,0:T(8,128)(2,1)S(1)}, u32[]{:S(2)}, u32[]{:S(2)}) collective-permute-start(bf16[128,2048]{1,0:T(8,128)(2,1)S(1)} %collective-permute-done.34.refs_1_), channel_id=1, source_target_pairs={{0,1},{1,0},{2,3},{3,2},{4,5},{5,4},{6,7},{7,6},{8,9},{9,8},{10,11... | collective-permute-start | bytes 1572872 | tf_op jit(solution)/shard_map/ppermute | solution.py:306
  141.8 10.8 %collective-permute-start.41 = (bf16[128,2048]{1,0:T(8,128)(2,1)S(1)}, bf16[128,2048]{1,0:T(8,128)(2,1)S(1)}, u32[]{:S(2)}, u32[]{:S(2)}) collective-permute-start(bf16[128,2048]{1,0:T(8,128)(2,1)S(1)} %get-tuple-element.33), channel_id=1, source_target_pairs={{0,1},{1,0},{2,3},{3,2},{4,5},{5,4},{6,7},{7,6},{8,9},{9,8},{10,11... | collective-permute-start | bytes 1572872 | tf_op jit(solution)/shard_map/ppermute | solution.py:306
  142.1 48.6 %collective-permute-start.21 = (bf16[128,2048]{1,0:T(8,128)(2,1)S(1)}, bf16[128,2048]{1,0:T(8,128)(2,1)S(1)}, u32[]{:S(2)}, u32[]{:S(2)}) collective-permute-start(bf16[128,2048]{1,0:T(8,128)(2,1)S(1)} %get-tuple-element.23.refs_0_), channel_id=1, source_target_pairs={{0,1},{1,0},{2,3},{3,2},{4,5},{5,4},{6,7},{7,6},{8,9},{9,8},{10,11... | collective-permute-start | bytes 1572872 | tf_op jit(solution)/shard_map/ppermute | solution.py:306
  142.5 32.9 %collective-permute-start.25 = (bf16[128,2048]{1,0:T(8,128)(2,1)S(1)}, bf16[128,2048]{1,0:T(8,128)(2,1)S(1)}, u32[]{:S(2)}, u32[]{:S(2)}) collective-permute-start(bf16[128,2048]{1,0:T(8,128)(2,1)S(1)} %collective-permute-done.23.refs_0_), channel_id=1, source_target_pairs={{0,1},{1,0},{2,3},{3,2},{4,5},{5,4},{6,7},{7,6},{8,9},{9,8},{10,11... | collective-permute-start | bytes 1572872 | tf_op jit(solution)/shard_map/ppermute | solution.py:306
  142.6 10.7 %collective-permute-start.30 = (bf16[128,2048]{1,0:T(8,128)(2,1)S(1)}, bf16[128,2048]{1,0:T(8,128)(2,1)S(1)}, u32[]{:S(2)}, u32[]{:S(2)}) collective-permute-start(bf16[128,2048]{1,0:T(8,128)(2,1)S(1)} %collective-permute-done.28.refs_0_), channel_id=1, source_target_pairs={{0,1},{1,0},{2,3},{3,2},{4,5},{5,4},{6,7},{7,6},{8,9},{9,8},{10,11... | collective-permute-start | bytes 1572872 | tf_op jit(solution)/shard_map/ppermute | solution.py:306
  143.0 10.5 %collective-permute-start.31 = (bf16[128,2048]{1,0:T(8,128)(2,1)S(1)}, bf16[128,2048]{1,0:T(8,128)(2,1)S(1)}, u32[]{:S(2)}, u32[]{:S(2)}) collective-permute-start(bf16[128,2048]{1,0:T(8,128)(2,1)S(1)} %collective-permute-done.29.refs_1_), channel_id=1, source_target_pairs={{0,1},{1,0},{2,3},{3,2},{4,5},{5,4},{6,7},{7,6},{8,9},{9,8},{10,11... | collective-permute-start | bytes 1572872 | tf_op jit(solution)/shard_map/ppermute | solution.py:306
  152.7 12.2 %collective-permute-start.37 = (bf16[128,2048]{1,0:T(8,128)(2,1)S(1)}, bf16[128,2048]{1,0:T(8,128)(2,1)S(1)}, u32[]{:S(2)}, u32[]{:S(2)}) collective-permute-start(bf16[128,2048]{1,0:T(8,128)(2,1)S(1)} %get-tuple-element.31), channel_id=1, source_target_pairs={{0,1},{1,0},{2,3},{3,2},{4,5},{5,4},{6,7},{7,6},{8,9},{9,8},{10,11... | collective-permute-start | bytes 1572872 | tf_op jit(solution)/shard_map/ppermute | solution.py:306
  153.3 12.2 %collective-permute-start.48 = (bf16[128,2048]{1,0:T(8,128)(2,1)S(1)}, bf16[128,2048]{1,0:T(8,128)(2,1)S(1)}, u32[]{:S(2)}, u32[]{:S(2)}) collective-permute-start(bf16[128,2048]{1,0:T(8,128)(2,1)S(1)} %get-tuple-element.39), channel_id=1, source_target_pairs={{0,1},{1,0},{2,3},{3,2},{4,5},{5,4},{6,7},{7,6},{8,9},{9,8},{10,11... | collective-permute-start | bytes 1572872 | tf_op jit(solution)/shard_map/ppermute | solution.py:306
  153.5 11.5 %collective-permute-start.42 = (bf16[64,2048]{1,0:T(8,128)(2,1)S(1)}, bf16[64,2048]{1,0:T(8,128)(2,1)S(1)}, u32[]{:S(2)}, u32[]{:S(2)}) collective-permute-start(bf16[64,2048]{1,0:T(8,128)(2,1)S(1)} %get-tuple-element.40), channel_id=1, source_target_pairs={{0,4},{1,5},{4,8},{5,9},{8,12},{9,13},{12,14},{13,15},{14,10},{15,... | collective-permute-start | bytes 786440 | tf_op jit(solution)/shard_map/ppermute | solution.py:302
  164.9 10.5 %collective-permute-start.26 = (bf16[128,2048]{1,0:T(8,128)(2,1)S(1)}, bf16[128,2048]{1,0:T(8,128)(2,1)S(1)}, u32[]{:S(2)}, u32[]{:S(2)}) collective-permute-start(bf16[128,2048]{1,0:T(8,128)(2,1)S(1)} %collective-permute-done.24.refs_1_), channel_id=1, source_target_pairs={{0,1},{1,0},{2,3},{3,2},{4,5},{5,4},{6,7},{7,6},{8,9},{9,8},{10,11... | collective-permute-start | bytes 1572872 | tf_op jit(solution)/shard_map/ppermute | solution.py:306
  165.0 8.7 %collective-permute-start.49 = (bf16[64,2048]{1,0:T(8,128)(2,1)S(1)}, bf16[64,2048]{1,0:T(8,128)(2,1)S(1)}, u32[]{:S(2)}, u32[]{:S(2)}) collective-permute-start(bf16[64,2048]{1,0:T(8,128)(2,1)S(1)} %get-tuple-element.41), channel_id=1, source_target_pairs={{0,2},{1,3},{4,0},{5,1},{8,4},{9,5},{12,8},{13,9},{14,12},{15,13},... | collective-permute-start | bytes 786440 | tf_op jit(solution)/shard_map/ppermute | solution.py:302
  165.6 20.1 %collective-permute-start.32 = (bf16[128,2048]{1,0:T(8,128)(2,1)S(1)}, bf16[128,2048]{1,0:T(8,128)(2,1)S(1)}, u32[]{:S(2)}, u32[]{:S(2)}) collective-permute-start(bf16[128,2048]{1,0:T(8,128)(2,1)S(1)} %get-tuple-element.29), channel_id=1, source_target_pairs={{0,1},{1,0},{2,3},{3,2},{4,5},{5,4},{6,7},{7,6},{8,9},{9,8},{10,11... | collective-permute-start | bytes 1572872 | tf_op jit(solution)/shard_map/ppermute | solution.py:306
  173.7 13.5 %collective-permute-start.43 = (bf16[128,2048]{1,0:T(8,128)(2,1)S(1)}, bf16[128,2048]{1,0:T(8,128)(2,1)S(1)}, u32[]{:S(2)}, u32[]{:S(2)}) collective-permute-start(bf16[128,2048]{1,0:T(8,128)(2,1)S(1)} %add_convert_fusion.6), channel_id=1, source_target_pairs={{0,4},{1,5},{4,8},{5,9},{8,12},{9,13},{12,14},{13,15},{14,10},{15,... | collective-permute-start | bytes 1572872 | tf_op jit(solution)/shard_map/ppermute | solution.py:302
  175.3 12.1 %collective-permute-start.47 = (bf16[128,2048]{1,0:T(8,128)(2,1)S(1)}, bf16[128,2048]{1,0:T(8,128)(2,1)S(1)}, u32[]{:S(2)}, u32[]{:S(2)}) collective-permute-start(bf16[128,2048]{1,0:T(8,128)(2,1)S(1)} %get-tuple-element.37), channel_id=1, source_target_pairs={{0,1},{1,0},{2,3},{3,2},{4,5},{5,4},{6,7},{7,6},{8,9},{9,8},{10,11... | collective-permute-start | bytes 1572872 | tf_op jit(solution)/shard_map/ppermute | solution.py:306
  175.4 14.3 %collective-permute-start.50 = (bf16[128,2048]{1,0:T(8,128)(2,1)S(1)}, bf16[128,2048]{1,0:T(8,128)(2,1)S(1)}, u32[]{:S(2)}, u32[]{:S(2)}) collective-permute-start(bf16[128,2048]{1,0:T(8,128)(2,1)S(1)} %add_convert_fusion.3), channel_id=1, source_target_pairs={{0,2},{1,3},{4,0},{5,1},{8,4},{9,5},{12,8},{13,9},{14,12},{15,13},... | collective-permute-start | bytes 1572872 | tf_op jit(solution)/shard_map/ppermute | solution.py:302
  185.6 11.7 %collective-permute-start.27 = (bf16[128,2048]{1,0:T(8,128)(2,1)S(1)}, bf16[128,2048]{1,0:T(8,128)(2,1)S(1)}, u32[]{:S(2)}, u32[]{:S(2)}) collective-permute-start(bf16[128,2048]{1,0:T(8,128)(2,1)S(1)} %get-tuple-element.27), channel_id=1, source_target_pairs={{0,1},{1,0},{2,3},{3,2},{4,5},{5,4},{6,7},{7,6},{8,9},{9,8},{10,11... | collective-permute-start | bytes 1572872 | tf_op jit(solution)/shard_map/ppermute | solution.py:306
  187.2 16.4 %collective-permute-start.46 = (bf16[128,2048]{1,0:T(8,128)(2,1)S(1)}, bf16[128,2048]{1,0:T(8,128)(2,1)S(1)}, u32[]{:S(2)}, u32[]{:S(2)}) collective-permute-start(bf16[128,2048]{1,0:T(8,128)(2,1)S(1)} %get-tuple-element.35), channel_id=1, source_target_pairs={{0,1},{1,0},{2,3},{3,2},{4,5},{5,4},{6,7},{7,6},{8,9},{9,8},{10,11... | collective-permute-start | bytes 1572872 | tf_op jit(solution)/shard_map/ppermute | solution.py:306
  187.5 14.4 %collective-permute-start.44 = (bf16[128,2048]{1,0:T(8,128)(2,1)S(1)}, bf16[128,2048]{1,0:T(8,128)(2,1)S(1)}, u32[]{:S(2)}, u32[]{:S(2)}) collective-permute-start(bf16[128,2048]{1,0:T(8,128)(2,1)S(1)} %add_convert_fusion.5), channel_id=1, source_target_pairs={{0,4},{1,5},{4,8},{5,9},{8,12},{9,13},{12,14},{13,15},{14,10},{15,... | collective-permute-start | bytes 1572872 | tf_op jit(solution)/shard_map/ppermute | solution.py:302
  190.0 13.6 %collective-permute-start.51 = (bf16[128,2048]{1,0:T(8,128)(2,1)S(1)}, bf16[128,2048]{1,0:T(8,128)(2,1)S(1)}, u32[]{:S(2)}, u32[]{:S(2)}) collective-permute-start(bf16[128,2048]{1,0:T(8,128)(2,1)S(1)} %add_convert_fusion.2), channel_id=1, source_target_pairs={{0,2},{1,3},{4,0},{5,1},{8,4},{9,5},{12,8},{13,9},{14,12},{15,13},... | collective-permute-start | bytes 1572872 | tf_op jit(solution)/shard_map/ppermute | solution.py:302
  202.1 13.6 %collective-permute-start.45 = (bf16[128,2048]{1,0:T(8,128)(2,1)S(1)}, bf16[128,2048]{1,0:T(8,128)(2,1)S(1)}, u32[]{:S(2)}, u32[]{:S(2)}) collective-permute-start(bf16[128,2048]{1,0:T(8,128)(2,1)S(1)} %add_convert_fusion.4), channel_id=1, source_target_pairs={{0,4},{1,5},{4,8},{5,9},{8,12},{9,13},{12,14},{13,15},{14,10},{15,... | collective-permute-start | bytes 1572872 | tf_op jit(solution)/shard_map/ppermute | solution.py:302
  203.8 13.3 %collective-permute-start.52 = (bf16[128,2048]{1,0:T(8,128)(2,1)S(1)}, bf16[128,2048]{1,0:T(8,128)(2,1)S(1)}, u32[]{:S(2)}, u32[]{:S(2)}) collective-permute-start(bf16[128,2048]{1,0:T(8,128)(2,1)S(1)} %add_convert_fusion.1), channel_id=1, source_target_pairs={{0,2},{1,3},{4,0},{5,1},{8,4},{9,5},{12,8},{13,9},{14,12},{15,13},... | collective-permute-start | bytes 1572872 | tf_op jit(solution)/shard_map/ppermute | solution.py:302
  (22 other events, 204.2 us)

commit v2 on v1

--- a/solution.py
+++ b/solution.py
@@ -316,25 +316,20 @@
             rows.append(row + [self.cycle[(p + self.far) % self.chips]])
         return rows
 
-    def gather(self, x):
-        half = x.shape[0] // 2
-        levels = [[x]]
-        up = down = x
-        for _ in range(1, self.far):
-            up, down = self.step(up, 1), self.step(down, -1)
-            levels.append([up, down])
-        levels.append([self.step(up[:half], 1), self.step(down[half:], -1)])
-        return levels
-
-
-def xor_gather(x, n):
-    x = x[None]
-    bit = 1
-    while bit < n:
-        other = lax.ppermute(x, "ctx", [(i, i ^ bit) for i in range(n)])
-        x = jnp.concatenate([x, other], axis=0)
-        bit *= 2
+
+def xor_step(x, bit, n):
+    other = lax.ppermute(x, "ctx", [(i, i ^ bit) for i in range(n)])
+    return jnp.concatenate([x, other], axis=0)
+
+
+def xor_rest(x, n):
+    while x.shape[0] < n:
+        x = xor_step(x, x.shape[0], n)
     return x
+
+
+def after(x, *earlier):
+    return lax.optimization_barrier((x, earlier))[0]
 
 
 def add(*xs):
@@ -364,34 +359,40 @@
     ring = Ring(n)
     near = jnp.asarray(ring.table(n), jnp.int32)[index]
 
-    rows_of_weight = ring.gather(out_weight)
-    sibling_rows = [[ring.swap(b) for b in level] for level in rows_of_weight]
-
+    half = queries.shape[0] // 2
     small = summarize(block_ids, keys, values, summary_gain, routes, route_scores, n)
-    small = xor_gather(small, n)
-    attended = attend(jnp.stack([index, index]), queries, keys, values, small[:, : 8 * KVH])
+    small = xor_step(xor_step(small[None], 1, n), 2, n)
+    up, down = ring.step(out_weight, 1), ring.step(out_weight, -1)
+    blocks = [out_weight, ring.swap(out_weight)]
+    for k in range(1, ring.far):
+        if k == 1:
+            up, down = after(up, small), after(down, small)
+            small = xor_rest(small, n)
+            attended = attend(jnp.stack([index, index]), queries, keys, values, small[:, : 8 * KVH])
+        if k == 2:
+            up, down = after(up, attended), after(down, attended)
+        blocks += [up, ring.swap(up), down, ring.swap(down)]
+        if k < ring.far - 1:
+            up, down = ring.step(up, 1), ring.step(down, -1)
+    up, down = ring.step(up[:half], 1), ring.step(down[half:], -1)
     base = 8 * KVH
     parts = lax.dynamic_index_in_dim(
         small[:, base:].reshape(n, 2, n, HD), index, axis=2, keepdims=False
     ).astype(F32)
     table = parts[:, 0] + parts[:, 1]
-
-    blocks = []
-    for mine, theirs in zip(rows_of_weight[:-1], sibling_rows[:-1]):
-        for a, b in zip(mine, theirs):
-            blocks += [a, b]
     first = jnp.concatenate([core[None], near[:-1]])
     acc = project_first(first, attended, blocks)
+    up, down = after(up, acc), after(down, acc)
     last = jnp.stack([core, near[-1]])
     hidden, projected, normed = project_last(
-        last, attended, acc, norm_gain, [*rows_of_weight[-1], *sibling_rows[-1]]
+        last, attended, acc, norm_gain, [up, down, ring.swap(up), ring.swap(down)]
     )
 
-    levels = ring.gather(normed)
-    levels[-1] = [jnp.concatenate(levels[-1], axis=0)]
+    at = 0
     partial = []
-    at = 0
-    for level in levels:
+
+    def experts(level):
+        nonlocal at
         others = [ring.swap(b) for b in level]
         chips = near[at : at + len(level)]
         at += len(level)
@@ -401,8 +402,25 @@
         )
         kept, sent = done[: len(level)], done[len(level) :]
         partial.append([(a, ring.swap(b)) for a, b in zip(kept, sent)])
-
-    half = queries.shape[0] // 2
+        return kept[0]
+
+    level = [normed]
+    up, down = ring.step(normed, 1), ring.step(normed, -1)
+    for k in range(1, ring.far):
+        done = experts(level)
+        up, down = after(up, done), after(down, done)
+        level = [up, down]
+        if k < ring.far - 1:
+            up, down = ring.step(up, 1), ring.step(down, -1)
+    up, down = ring.step(up[:half], 1), ring.step(down[half:], -1)
+    late = level
+    at += 2
+    experts([jnp.concatenate([up, down], axis=0)])
+    far = partial.pop()
+    at -= 3
+    experts([after(b, far[0][0]) for b in late])
+    partial.append(far)
+
     [(mine, theirs)] = partial[-1]
     far = add(mine, theirs).astype(BF16)
     up, down = ring.step(far[:half], 1), ring.step(far[half:], -1)

time: 219 us -> 201 us (0.918)
  waiting for transfers between devices: 113 us -> 88 us
  starting transfers between devices: 34.7 us -> 37.5 us
  local copies, waits for them, and re-layouts: 12.9 us -> 15.2 us
    ppermute x24, waiting for transfers between devices: 94.8 us -> 71.5 us  [step(): return lax.ppermute(x, 'ctx', pairs)]
    ppermute x4, waiting for transfers between devices: 17.4 us -> 13.4 us  [xor_step(): other = lax.ppermute(x, 'ctx', [(i, i ^ bit) for i in range(n)])]
    ppermute x4, starting transfers between devices: 3.92 us -> 6.27 us  [xor_step(): other = lax.ppermute(x, 'ctx', [(i, i ^ bit) for i in range(n)])]
    slice x5, local copies, waits for them, and re-layouts: 1.69 us -> 3.97 us  [the longest x4 3.37 us: ring_body(): up, down = (ring.step(up[:half], 1), ring.step(down[half:], -1))]
    unnamed x39 -> x37, local copies, waits for them, and re-layouts: 10.4 us -> 10.4 us
  transfers between devices with their start and end apart: 53 -> 53, of which waited for: 21 -> 26; matrix products, arithmetic and copies ran while one was open for 2% -> 4% of each run, Pallas kernels for 22% -> 22%
where the time goes in v2:
time: 201 us; the launch traced here: 200 us
  waiting for transfers between devices  88 us (44%)
  Pallas kernels  52.9 us (26%)
  starting transfers between devices  37.5 us (19%)
  local copies, waits for them, and re-layouts  15.2 us (8%)
  other arithmetic  3.96 us (2%)
  between operations  2.25 us (1%)
    ppermute x24, waiting for transfers between devices, step(): return lax.ppermute(x, 'ctx', pairs)  71.5 us
    pallas_call x5, Pallas kernels, expert_blocks(): pl.pallas_call(functools.partial(expert_kernel, count), grid_spec=pltpu.P...  42.2 us
    ppermute x24, starting transfers between devices, step(): return lax.ppermute(x, 'ctx', pairs)  28.2 us
    ppermute x4, waiting for transfers between devices, xor_step(): other = lax.ppermute(x, 'ctx', [(i, i ^ bit) for i in range(n)])  13.4 us
    unnamed x37, local copies, waits for them, and re-layouts  10.4 us
    ppermute x4, starting transfers between devices, xor_step(): other = lax.ppermute(x, 'ctx', [(i, i ^ bit) for i in range(n)])  6.27 us
    pallas_call x1, Pallas kernels, project_first(): pl.pallas_call(project_first_kernel, grid_spec=pltpu.PrefetchScalarGridSp...  5.66 us
  transfers between devices with their start and end apart: 53, of which 26 were waited for; matrix products, arithmetic and copies ran while one was open for 4% of the time, Pallas kernels for 22%

profile of v2, /device:TPU:0, one launch (start us, length us, event | category | flops | bytes accessed | tf_op | source)
XLA Modules:
  0.0 199.9 jit_solution(269819295157959926)
XLA Ops:
  0.6 3.1 %collective-permute-start.5 = (bf16[128,2048]{1,0:T(8,128)(2,1)}, bf16[128,2048]{1,0:T(8,128)(2,1)S(1)}, u32[]{:S(2)}, u32[]{:S(2)}) collective-permute-start(bf16[128,2048]{1,0:T(8,128)(2,1)} %refs_0_.1), channel_id=1, source_target_pairs={{0,4},{1,5},{4,8},{5,9},{8,12},{9,13},{12,14},{13,15},{14,10},{15,... | collective-permute-start | bytes 1572872 | tf_op jit(solution)/shard_map/ppermute | solution.py:302
  9.9 2.0 collective-permute-start.1
  11.9 4.6 %collective-permute-done.1 = bf16[2,64,128]{2,1,0:T(8,128)(2,1)S(1)} collective-permute-done((bf16[2,64,128]{2,1,0:T(8,128)(2,1)S(1)}, bf16[2,64,128]{2,1,0:T(8,128)(2,1)S(1)}, u32[]{:S(2)}, u32[]{:S(2)}) %collective-permute-start.1) | collective-permute-done | bytes 32800 | tf_op jit(solution)/shard_map/ppermute | solution.py:321
  16.6 4.2 %collective-permute-done.2 = bf16[4,64,128]{2,1,0:T(8,128)(2,1)S(1)} collective-permute-done((bf16[4,64,128]{2,1,0:T(8,128)(2,1)S(1)}, bf16[4,64,128]{2,1,0:T(8,128)(2,1)S(1)}, u32[]{:S(2)}, u32[]{:S(2)}) %collective-permute-start.2) | collective-permute-done | bytes 65568 | tf_op jit(solution)/shard_map/ppermute | solution.py:321
  20.9 3.7 %collective-permute-start.3 = (bf16[8,64,128]{2,1,0:T(8,128)(2,1)S(1)}, bf16[8,64,128]{2,1,0:T(8,128)(2,1)S(1)}, u32[]{:S(2)}, u32[]{:S(2)}) collective-permute-start(bf16[8,64,128]{2,1,0:T(8,128)(2,1)S(1)} %pad_maximum_fusion), channel_id=1, source_target_pairs={{0,8},{1,9},{2,10},{3,11},{4,12},{5,13},{6,14},{7,15},{8,0},{9,1},... | collective-permute-start | bytes 393224 | tf_op jit(solution)/shard_map/ppermute | solution.py:321
  24.5 2.0 %collective-permute-start.9 = (bf16[128,2048]{1,0:T(8,128)(2,1)S(1)}, bf16[128,2048]{1,0:T(8,128)(2,1)S(1)}, u32[]{:S(2)}, u32[]{:S(2)}) collective-permute-start(bf16[128,2048]{1,0:T(8,128)(2,1)S(1)} %collective-permute-done.5.refs_2_), channel_id=1, source_target_pairs={{0,4},{1,5},{4,8},{5,9},{8,12},{9,13},{12,14},{13,15},{14,10},{15,... | collective-permute-start | bytes 1572872 | tf_op jit(solution)/shard_map/ppermute | solution.py:302
  26.6 3.7 %collective-permute-done.3 = bf16[8,64,128]{2,1,0:T(8,128)(2,1)S(1)} collective-permute-done((bf16[8,64,128]{2,1,0:T(8,128)(2,1)S(1)}, bf16[8,64,128]{2,1,0:T(8,128)(2,1)S(1)}, u32[]{:S(2)}, u32[]{:S(2)}) %collective-permute-start.3) | collective-permute-done | bytes 131104 | tf_op jit(solution)/shard_map/ppermute | solution.py:321
  30.4 1.0 copy-done.6
  33.2 2.1 %attention.1.attended = bf16[128,2048]{1,0:T(8,128)(2,1)S(1)} custom-call(s32[2]{0:T(128)S(1)} %pad_add_fusion.1.me, bf16[128,2048]{1,0:T(8,128)(2,1)S(1)} %copy-done.6, bf16[128,512]{1,0:T(8,128)(2,1)S(1)} %copy-done.8, bf16[128,512]{1,0:T(8,128)(2,1)S(1)} %copy-done.10, bf16[16,32,128]{2,1,0:T(8,128)(2,1)S(1)} %get-tuple-element.71.gathered), custom_call_target="tpu_custom_call" | custom-call | flops 268435456 | bytes 2097152 | tf_op jit(solution)/shard_map/attention/pallas_call | solution.py:117
  35.4 1.1 collective-permute-done.9.refs_6_
  36.5 4.3 %collective-permute-start.13 = (bf16[128,2048]{1,0:T(8,128)(2,1)S(1)}, bf16[128,2048]{1,0:T(8,128)(2,1)}, u32[]{:S(2)}, u32[]{:S(2)}) collective-permute-start(bf16[128,2048]{1,0:T(8,128)(2,1)S(1)} %collective-permute-done.9.refs_6_), channel_id=1, source_target_pairs={{0,4},{1,5},{4,8},{5,9},{8,12},{9,13},{12,14},{13,15},{14,10},{15,... | collective-permute-start | bytes 1572872 | tf_op jit(solution)/shard_map/ppermute | solution.py:302
  42.2 7.9 %collective-permute-done.13.refs_10_ = bf16[128,2048]{1,0:T(8,128)(2,1)} collective-permute-done((bf16[128,2048]{1,0:T(8,128)(2,1)S(1)}, bf16[128,2048]{1,0:T(8,128)(2,1)}, u32[]{:S(2)}, u32[]{:S(2)}) %collective-permute-start.13) | collective-permute-done | bytes 524320 | tf_op jit(solution)/shard_map/ppermute | solution.py:302
  50.1 3.3 %collective-permute-done.15.refs_12_ = bf16[128,2048]{1,0:T(8,128)(2,1)} collective-permute-done((bf16[128,2048]{1,0:T(8,128)(2,1)}, bf16[128,2048]{1,0:T(8,128)(2,1)}, u32[]{:S(2)}, u32[]{:S(2)}) %collective-permute-start.15) | collective-permute-done | bytes 524320 | tf_op jit(solution)/shard_map/ppermute | solution.py:302
  54.1 1.7 slice.79
  55.7 1.7 slice.78
  57.4 2.0 %collective-permute-start.17 = (bf16[64,2048]{1,0:T(8,128)(2,1)}, bf16[64,2048]{1,0:T(8,128)(2,1)}, u32[]{:S(2)}, u32[]{:S(2)}) collective-permute-start(bf16[64,2048]{1,0:T(8,128)(2,1)} %slice.78), channel_id=1, source_target_pairs={{0,4},{1,5},{4,8},{5,9},{8,12},{9,13},{12,14},{13,15},{14,10},{15,... | collective-permute-start | bytes 786440 | tf_op jit(solution)/shard_map/ppermute | solution.py:302
  59.6 1.0 copy-done.5
  60.6 5.7 %project_first.1.acc = f32[128,2048]{1,0:T(8,128)} custom-call(s32[8]{0:T(128)S(1)} %pad_add_fusion.2.chips, bf16[128,2048]{1,0:T(8,128)(2,1)S(1)} %attention.1.attended, bf16[128,2048]{1,0:T(8,128)(2,1)S(1)} %copy-done.3, bf16[128,2048]{1,0:T(8,128)(2,1)S(1)} %collective-permute-done.4.refs_1_, bf16[128,2048]{1,0:T(8,128)(2,1)S(1)} %collective-permute-done.5.refs_2_, ...), custom_call_target="tpu_custom_call" | custom-call | flops 939524096 | bytes 7340032 | tf_op jit(solution)/shard_map/project_first/pallas_call | solution.py:157
  68.9 1.2 copy-done.2
  70.1 2.7 %project_last.1 = (f32[128,2048]{1,0:T(8,128)S(1)}, bf16[128,2048]{1,0:T(8,128)(2,1)}, bf16[128,2048]{1,0:T(8,128)(2,1)S(1)}) custom-call(s32[2]{0:T(128)S(1)} %pad_add_fusion.chips, bf16[128,2048]{1,0:T(8,128)(2,1)S(1)} %attention.1.attended, f32[128,2048]{1,0:T(8,128)S(1)} %copy-done.2, f32[1,2048]{1,0:T(1,128)S(1)} %bitcast.37, ...), custom_call_target="tpu_custom_call" | custom-call | flops 134217728 | bytes 3145728 | tf_op jit(solution)/shard_map/project_last/pallas_call | solution.py:199
  73.0 1.0 collective-permute-start.24
  74.0 1.1 collective-permute-start.23
  75.1 6.6 %experts.5 = (bf16[128,2048]{1,0:T(8,128)(2,1)S(1)}, bf16[128,2048]{1,0:T(8,128)(2,1)S(1)}) custom-call(s32[2]{0:T(128)S(1)} %add_xor_fusion.at, f32[16,128]{1,0:T(8,128)S(1)} %fusion.table, bf16[128,2048]{1,0:T(8,128)(2,1)S(1)} %get-tuple-element.43.refs_0_, bf16[128,2048]{1,0:T(8,128)(2,1)S(1)} %collective-permute-done.21.refs_1_, ...), custom_call_target="tpu_custom_call" | custom-call | flops 2415919104 | bytes 9437184 | tf_op jit(solution)/shard_map/experts/pallas_call | solution.py:262
  81.8 5.5 %collective-permute-done.24.refs_1_ = bf16[128,2048]{1,0:T(8,128)(2,1)S(1)} collective-permute-done((bf16[128,2048]{1,0:T(8,128)(2,1)S(1)}, bf16[128,2048]{1,0:T(8,128)(2,1)S(1)}, u32[]{:S(2)}, u32[]{:S(2)}) %collective-permute-start.24) | collective-permute-done | bytes 524320 | tf_op jit(solution)/shard_map/ppermute | solution.py:302
  87.8 1.6 collective-permute-start.29
  89.9 9.5 %experts.6 = (bf16[128,2048]{1,0:T(8,128)(2,1)S(1)}, bf16[128,2048]{1,0:T(8,128)(2,1)S(1)}, bf16[128,2048]{1,0:T(8,128)(2,1)S(1)}, bf16[128,2048]{1,0:T(8,128)(2,1)S(1)}) custom-call(s32[4]{0:T(128)S(1)} %add_xor_fusion.1.at, f32[16,128]{1,0:T(8,128)S(1)} %fusion.table, bf16[128,2048]{1,0:T(8,128)(2,1)S(1)} %collective-permute-done.23.refs_0_, ...), custom_call_target="tpu_custom_call" | custom-call | flops 4831838208 | bytes 9437184 | tf_op jit(solution)/shard_map/experts/pallas_call | solution.py:262
  99.5 2.5 %collective-permute-done.29.refs_1_ = bf16[128,2048]{1,0:T(8,128)(2,1)S(1)} collective-permute-done((bf16[128,2048]{1,0:T(8,128)(2,1)S(1)}, bf16[128,2048]{1,0:T(8,128)(2,1)S(1)}, u32[]{:S(2)}, u32[]{:S(2)}) %collective-permute-start.29) | collective-permute-done | bytes 524320 | tf_op jit(solution)/shard_map/ppermute | solution.py:302
  102.0 1.5 collective-permute-done.28.refs_0_
  104.0 1.7 collective-permute-start.35
  105.7 9.8 %experts.7 = (bf16[128,2048]{1,0:T(8,128)(2,1)S(1)}, bf16[128,2048]{1,0:T(8,128)(2,1)S(1)}, bf16[128,2048]{1,0:T(8,128)(2,1)S(1)}, bf16[128,2048]{1,0:T(8,128)(2,1)S(1)}) custom-call(s32[4]{0:T(128)S(1)} %add_xor_fusion.2.at, f32[16,128]{1,0:T(8,128)S(1)} %fusion.table, bf16[128,2048]{1,0:T(8,128)(2,1)S(1)} %collective-permute-done.28.refs_0_, ...), custom_call_target="tpu_custom_call" | custom-call | flops 4831838208 | bytes 9437184 | tf_op jit(solution)/shard_map/experts/pallas_call | solution.py:262
  115.6 2.2 %collective-permute-done.33.refs_0_ = bf16[128,2048]{1,0:T(8,128)(2,1)S(1)} collective-permute-done((bf16[128,2048]{1,0:T(8,128)(2,1)S(1)}, bf16[128,2048]{1,0:T(8,128)(2,1)S(1)}, u32[]{:S(2)}, u32[]{:S(2)}) %collective-permute-start.33) | collective-permute-done | bytes 524320 | tf_op jit(solution)/shard_map/ppermute | solution.py:302
  118.2 1.8 collective-permute-start.36
  120.0 5.8 %collective-permute-done.34 = bf16[64,2048]{1,0:T(8,128)(2,1)S(1)} collective-permute-done((bf16[64,2048]{1,0:T(8,128)(2,1)S(1)}, bf16[64,2048]{1,0:T(8,128)(2,1)S(1)}, u32[]{:S(2)}, u32[]{:S(2)}) %collective-permute-start.34) | collective-permute-done | bytes 262176 | tf_op jit(solution)/shard_map/ppermute | solution.py:302
  126.7 1.2 collective-permute-done.37.refs_1_
  127.9 6.6 %experts.8 = (bf16[128,2048]{1,0:T(8,128)(2,1)S(1)}, bf16[128,2048]{1,0:T(8,128)(2,1)S(1)}) custom-call(s32[2]{0:T(128)S(1)} %add_xor_fusion.4.at, f32[16,128]{1,0:T(8,128)S(1)} %fusion.table, bf16[128,2048]{1,0:T(8,128)(2,1)S(1)} %constant_dynamic-update-slice_fusion.5.refs_0_, bf16[128,2048]{1,0:T(8,128)(2,1)S(1)} %collective-permute-done.37.refs_1_, ...), custom_call_target="tpu_custom_call" | custom-call | flops 2415919104 | bytes 9437184 | tf_op jit(solution)/shard_map/experts/pallas_call | solution.py:262
  135.3 1.2 collective-permute-done.39.refs_3_
  137.3 9.5 %experts.9 = (bf16[128,2048]{1,0:T(8,128)(2,1)S(1)}, bf16[128,2048]{1,0:T(8,128)(2,1)S(1)}, bf16[128,2048]{1,0:T(8,128)(2,1)S(1)}, bf16[128,2048]{1,0:T(8,128)(2,1)S(1)}) custom-call(s32[4]{0:T(128)S(1)} %add_xor_fusion.3.at, f32[16,128]{1,0:T(8,128)S(1)} %fusion.table, bf16[128,2048]{1,0:T(8,128)(2,1)S(1)} %collective-permute-done.33.refs_0_, ...), custom_call_target="tpu_custom_call" | custom-call | flops 4831838208 | bytes 9437184 | tf_op jit(solution)/shard_map/experts/pallas_call | solution.py:262
  147.2 1.3 collective-permute-start.42
  149.8 6.0 %collective-permute-done.42 = bf16[64,2048]{1,0:T(8,128)(2,1)S(1)} collective-permute-done((bf16[64,2048]{1,0:T(8,128)(2,1)S(1)}, bf16[64,2048]{1,0:T(8,128)(2,1)S(1)}, u32[]{:S(2)}, u32[]{:S(2)}) %collective-permute-start.42) | collective-permute-done | bytes 262176 | tf_op jit(solution)/shard_map/ppermute | solution.py:302
  156.0 1.3 collective-permute-start.43
  158.6 10.9 %collective-permute-done.43 = bf16[128,2048]{1,0:T(8,128)(2,1)S(1)} collective-permute-done((bf16[128,2048]{1,0:T(8,128)(2,1)S(1)}, bf16[128,2048]{1,0:T(8,128)(2,1)S(1)}, u32[]{:S(2)}, u32[]{:S(2)}) %collective-permute-start.43) | collective-permute-done | bytes 524320 | tf_op jit(solution)/shard_map/ppermute | solution.py:302
  169.7 1.2 collective-permute-start.44
  173.0 9.2 %collective-permute-done.44 = bf16[128,2048]{1,0:T(8,128)(2,1)S(1)} collective-permute-done((bf16[128,2048]{1,0:T(8,128)(2,1)S(1)}, bf16[128,2048]{1,0:T(8,128)(2,1)S(1)}, u32[]{:S(2)}, u32[]{:S(2)}) %collective-permute-start.44) | collective-permute-done | bytes 524320 | tf_op jit(solution)/shard_map/ppermute | solution.py:302
  182.5 1.2 collective-permute-start.45
  183.7 2.0 %collective-permute-done.51 = bf16[128,2048]{1,0:T(8,128)(2,1)S(1)} collective-permute-done((bf16[128,2048]{1,0:T(8,128)(2,1)S(1)}, bf16[128,2048]{1,0:T(8,128)(2,1)S(1)}, u32[]{:S(2)}, u32[]{:S(2)}) %collective-permute-start.51) | collective-permute-done | bytes 524320 | tf_op jit(solution)/shard_map/ppermute | solution.py:302
  186.8 7.3 %collective-permute-done.45 = bf16[128,2048]{1,0:T(8,128)(2,1)S(1)} collective-permute-done((bf16[128,2048]{1,0:T(8,128)(2,1)S(1)}, bf16[128,2048]{1,0:T(8,128)(2,1)S(1)}, u32[]{:S(2)}, u32[]{:S(2)}) %collective-permute-start.45) | collective-permute-done | bytes 524320 | tf_op jit(solution)/shard_map/ppermute | solution.py:302
  194.1 4.6 %collective-permute-done.52 = bf16[128,2048]{1,0:T(8,128)(2,1)S(1)} collective-permute-done((bf16[128,2048]{1,0:T(8,128)(2,1)S(1)}, bf16[128,2048]{1,0:T(8,128)(2,1)S(1)}, u32[]{:S(2)}, u32[]{:S(2)}) %collective-permute-start.52) | collective-permute-done | bytes 524320 | tf_op jit(solution)/shard_map/ppermute | solution.py:302
  198.7 1.2 add_convert_fusion
  (138 shorter events, 23.2 us)
Async XLA Ops:
  0.6 23.9 %collective-permute-start.5 = (bf16[128,2048]{1,0:T(8,128)(2,1)}, bf16[128,2048]{1,0:T(8,128)(2,1)S(1)}, u32[]{:S(2)}, u32[]{:S(2)}) collective-permute-start(bf16[128,2048]{1,0:T(8,128)(2,1)} %refs_0_.1), channel_id=1, source_target_pairs={{0,4},{1,5},{4,8},{5,9},{8,12},{9,13},{12,14},{13,15},{14,10},{15,... | collective-permute-start | bytes 1572872 | tf_op jit(solution)/shard_map/ppermute | solution.py:302
  3.7 22.8 %collective-permute-start.7 = (bf16[128,2048]{1,0:T(8,128)(2,1)}, bf16[128,2048]{1,0:T(8,128)(2,1)S(1)}, u32[]{:S(2)}, u32[]{:S(2)}) collective-permute-start(bf16[128,2048]{1,0:T(8,128)(2,1)} %refs_0_.1), channel_id=1, source_target_pairs={{0,2},{1,3},{4,0},{5,1},{8,4},{9,5},{12,8},{13,9},{14,12},{15,13},... | collective-permute-start | bytes 1572872 | tf_op jit(solution)/shard_map/ppermute | solution.py:302
  3.7 37.1 %collective-permute-start.4 = (bf16[128,2048]{1,0:T(8,128)(2,1)}, bf16[128,2048]{1,0:T(8,128)(2,1)S(1)}, u32[]{:S(2)}, u32[]{:S(2)}) collective-permute-start(bf16[128,2048]{1,0:T(8,128)(2,1)} %refs_0_.1), channel_id=1, source_target_pairs={{0,1},{1,0},{2,3},{3,2},{4,5},{5,4},{6,7},{7,6},{8,9},{9,8},{10,11... | collective-permute-start | bytes 1572872 | tf_op jit(solution)/shard_map/ppermute | solution.py:306
  9.9 6.6 %collective-permute-start.1 = (bf16[2,64,128]{2,1,0:T(8,128)(2,1)S(1)}, bf16[2,64,128]{2,1,0:T(8,128)(2,1)S(1)}, u32[]{:S(2)}, u32[]{:S(2)}) collective-permute-start(bf16[2,64,128]{2,1,0:T(8,128)(2,1)S(1)} %pad_maximum_fusion.2), channel_id=1, source_target_pairs={{0,2},{1,3},{2,0},{3,1},{4,6},{5,7},{6,4},{7,5},{8,10},{9,11},{10,... | collective-permute-start | bytes 98312 | tf_op jit(solution)/shard_map/ppermute | solution.py:321
  16.5 4.3 %collective-permute-start.2 = (bf16[4,64,128]{2,1,0:T(8,128)(2,1)S(1)}, bf16[4,64,128]{2,1,0:T(8,128)(2,1)S(1)}, u32[]{:S(2)}, u32[]{:S(2)}) collective-permute-start(bf16[4,64,128]{2,1,0:T(8,128)(2,1)S(1)} %pad_maximum_fusion.1), channel_id=1, source_target_pairs={{0,4},{1,5},{2,6},{3,7},{4,0},{5,1},{6,2},{7,3},{8,12},{9,13},{10,... | collective-permute-start | bytes 196616 | tf_op jit(solution)/shard_map/ppermute | solution.py:321
  20.9 9.4 %collective-permute-start.3 = (bf16[8,64,128]{2,1,0:T(8,128)(2,1)S(1)}, bf16[8,64,128]{2,1,0:T(8,128)(2,1)S(1)}, u32[]{:S(2)}, u32[]{:S(2)}) collective-permute-start(bf16[8,64,128]{2,1,0:T(8,128)(2,1)S(1)} %pad_maximum_fusion), channel_id=1, source_target_pairs={{0,8},{1,9},{2,10},{3,11},{4,12},{5,13},{6,14},{7,15},{8,0},{9,1},... | collective-permute-start | bytes 393224 | tf_op jit(solution)/shard_map/ppermute | solution.py:321
  24.5 12.0 %collective-permute-start.9 = (bf16[128,2048]{1,0:T(8,128)(2,1)S(1)}, bf16[128,2048]{1,0:T(8,128)(2,1)S(1)}, u32[]{:S(2)}, u32[]{:S(2)}) collective-permute-start(bf16[128,2048]{1,0:T(8,128)(2,1)S(1)} %collective-permute-done.5.refs_2_), channel_id=1, source_target_pairs={{0,4},{1,5},{4,8},{5,9},{8,12},{9,13},{12,14},{13,15},{14,10},{15,... | collective-permute-start | bytes 1572872 | tf_op jit(solution)/shard_map/ppermute | solution.py:302
  26.6 14.2 %collective-permute-start.11 = (bf16[128,2048]{1,0:T(8,128)(2,1)S(1)}, bf16[128,2048]{1,0:T(8,128)(2,1)}, u32[]{:S(2)}, u32[]{:S(2)}) collective-permute-start(bf16[128,2048]{1,0:T(8,128)(2,1)S(1)} %collective-permute-done.7.refs_4_), channel_id=1, source_target_pairs={{0,2},{1,3},{4,0},{5,1},{8,4},{9,5},{12,8},{13,9},{14,12},{15,13},... | collective-permute-start | bytes 1572872 | tf_op jit(solution)/shard_map/ppermute | solution.py:302
  35.3 6.0 %collective-permute-start.6 = (bf16[128,2048]{1,0:T(8,128)(2,1)S(1)}, bf16[128,2048]{1,0:T(8,128)(2,1)S(1)}, u32[]{:S(2)}, u32[]{:S(2)}) collective-permute-start(bf16[128,2048]{1,0:T(8,128)(2,1)S(1)} %collective-permute-done.5.refs_2_), channel_id=1, source_target_pairs={{0,1},{1,0},{2,3},{3,2},{4,5},{5,4},{6,7},{7,6},{8,9},{9,8},{10,11... | collective-permute-start | bytes 1572872 | tf_op jit(solution)/shard_map/ppermute | solution.py:306
  36.5 13.6 %collective-permute-start.13 = (bf16[128,2048]{1,0:T(8,128)(2,1)S(1)}, bf16[128,2048]{1,0:T(8,128)(2,1)}, u32[]{:S(2)}, u32[]{:S(2)}) collective-permute-start(bf16[128,2048]{1,0:T(8,128)(2,1)S(1)} %collective-permute-done.9.refs_6_), channel_id=1, source_target_pairs={{0,4},{1,5},{4,8},{5,9},{8,12},{9,13},{12,14},{13,15},{14,10},{15,... | collective-permute-start | bytes 1572872 | tf_op jit(solution)/shard_map/ppermute | solution.py:302
  40.8 12.6 %collective-permute-start.15 = (bf16[128,2048]{1,0:T(8,128)(2,1)}, bf16[128,2048]{1,0:T(8,128)(2,1)}, u32[]{:S(2)}, u32[]{:S(2)}) collective-permute-start(bf16[128,2048]{1,0:T(8,128)(2,1)} %collective-permute-done.11.refs_8_), channel_id=1, source_target_pairs={{0,2},{1,3},{4,0},{5,1},{8,4},{9,5},{12,8},{13,9},{14,12},{15,13},... | collective-permute-start | bytes 1572872 | tf_op jit(solution)/shard_map/ppermute | solution.py:302
  40.8 16.6 %collective-permute-start.8 = (bf16[128,2048]{1,0:T(8,128)(2,1)S(1)}, bf16[128,2048]{1,0:T(8,128)(2,1)}, u32[]{:S(2)}, u32[]{:S(2)}) collective-permute-start(bf16[128,2048]{1,0:T(8,128)(2,1)S(1)} %collective-permute-done.7.refs_4_), channel_id=1, source_target_pairs={{0,1},{1,0},{2,3},{3,2},{4,5},{5,4},{6,7},{7,6},{8,9},{9,8},{10,11... | collective-permute-start | bytes 1572872 | tf_op jit(solution)/shard_map/ppermute | solution.py:306
  40.8 16.6 %collective-permute-start.10 = (bf16[128,2048]{1,0:T(8,128)(2,1)S(1)}, bf16[128,2048]{1,0:T(8,128)(2,1)}, u32[]{:S(2)}, u32[]{:S(2)}) collective-permute-start(bf16[128,2048]{1,0:T(8,128)(2,1)S(1)} %collective-permute-done.9.refs_6_), channel_id=1, source_target_pairs={{0,1},{1,0},{2,3},{3,2},{4,5},{5,4},{6,7},{7,6},{8,9},{9,8},{10,11... | collective-permute-start | bytes 1572872 | tf_op jit(solution)/shard_map/ppermute | solution.py:306
  42.1 17.4 %collective-permute-start.12 = (bf16[128,2048]{1,0:T(8,128)(2,1)}, bf16[128,2048]{1,0:T(8,128)(2,1)}, u32[]{:S(2)}, u32[]{:S(2)}) collective-permute-start(bf16[128,2048]{1,0:T(8,128)(2,1)} %collective-permute-done.11.refs_8_), channel_id=1, source_target_pairs={{0,1},{1,0},{2,3},{3,2},{4,5},{5,4},{6,7},{7,6},{8,9},{9,8},{10,11... | collective-permute-start | bytes 1572872 | tf_op jit(solution)/shard_map/ppermute | solution.py:306
  50.1 9.4 %collective-permute-start.14 = (bf16[128,2048]{1,0:T(8,128)(2,1)}, bf16[128,2048]{1,0:T(8,128)(2,1)}, u32[]{:S(2)}, u32[]{:S(2)}) collective-permute-start(bf16[128,2048]{1,0:T(8,128)(2,1)} %collective-permute-done.13.refs_10_), channel_id=1, source_target_pairs={{0,1},{1,0},{2,3},{3,2},{4,5},{5,4},{6,7},{7,6},{8,9},{9,8},{10,11... | collective-permute-start | bytes 1572872 | tf_op jit(solution)/shard_map/ppermute | solution.py:306
  53.4 6.2 %collective-permute-start.16 = (bf16[128,2048]{1,0:T(8,128)(2,1)}, bf16[128,2048]{1,0:T(8,128)(2,1)}, u32[]{:S(2)}, u32[]{:S(2)}) collective-permute-start(bf16[128,2048]{1,0:T(8,128)(2,1)} %collective-permute-done.15.refs_12_), channel_id=1, source_target_pairs={{0,1},{1,0},{2,3},{3,2},{4,5},{5,4},{6,7},{7,6},{8,9},{9,8},{10,11... | collective-permute-start | bytes 1572872 | tf_op jit(solution)/shard_map/ppermute | solution.py:306
  57.4 8.9 %collective-permute-start.18 = (bf16[64,2048]{1,0:T(8,128)(2,1)}, bf16[64,2048]{1,0:T(8,128)(2,1)S(1)}, u32[]{:S(2)}, u32[]{:S(2)}) collective-permute-start(bf16[64,2048]{1,0:T(8,128)(2,1)} %slice.79), channel_id=1, source_target_pairs={{0,2},{1,3},{4,0},{5,1},{8,4},{9,5},{12,8},{13,9},{14,12},{15,13},... | collective-permute-start | bytes 786440 | tf_op jit(solution)/shard_map/ppermute | solution.py:302
  57.4 9.1 %collective-permute-start.17 = (bf16[64,2048]{1,0:T(8,128)(2,1)}, bf16[64,2048]{1,0:T(8,128)(2,1)}, u32[]{:S(2)}, u32[]{:S(2)}) collective-permute-start(bf16[64,2048]{1,0:T(8,128)(2,1)} %slice.78), channel_id=1, source_target_pairs={{0,4},{1,5},{4,8},{5,9},{8,12},{9,13},{12,14},{13,15},{14,10},{15,... | collective-permute-start | bytes 786440 | tf_op jit(solution)/shard_map/ppermute | solution.py:302
  66.4 2.5 %collective-permute-start.20 = (bf16[64,2048]{1,0:T(8,128)(2,1)S(1)}, bf16[64,2048]{1,0:T(8,128)(2,1)S(1)}, u32[]{:S(2)}, u32[]{:S(2)}) collective-permute-start(bf16[64,2048]{1,0:T(8,128)(2,1)S(1)} %collective-permute-done.18.b), channel_id=1, source_target_pairs={{0,1},{1,0},{2,3},{3,2},{4,5},{5,4},{6,7},{7,6},{8,9},{9,8},{10,11... | collective-permute-start | bytes 786440 | tf_op jit(solution)/shard_map/ppermute | solution.py:306
  66.5 2.4 %collective-permute-start.19 = (bf16[64,2048]{1,0:T(8,128)(2,1)}, bf16[64,2048]{1,0:T(8,128)(2,1)S(1)}, u32[]{:S(2)}, u32[]{:S(2)}) collective-permute-start(bf16[64,2048]{1,0:T(8,128)(2,1)} %collective-permute-done.17.a), channel_id=1, source_target_pairs={{0,1},{1,0},{2,3},{3,2},{4,5},{5,4},{6,7},{7,6},{8,9},{9,8},{10,11... | collective-permute-start | bytes 786440 | tf_op jit(solution)/shard_map/ppermute | solution.py:306
  73.0 14.2 %collective-permute-start.24 = (bf16[128,2048]{1,0:T(8,128)(2,1)S(1)}, bf16[128,2048]{1,0:T(8,128)(2,1)S(1)}, u32[]{:S(2)}, u32[]{:S(2)}) collective-permute-start(bf16[128,2048]{1,0:T(8,128)(2,1)S(1)} %get-tuple-element.43.refs_0_), channel_id=1, source_target_pairs={{0,2},{1,3},{4,0},{5,1},{8,4},{9,5},{12,8},{13,9},{14,12},{15,13},... | collective-permute-start | bytes 1572872 | tf_op jit(solution)/shard_map/ppermute | solution.py:302
  74.0 13.6 %collective-permute-start.23 = (bf16[128,2048]{1,0:T(8,128)(2,1)S(1)}, bf16[128,2048]{1,0:T(8,128)(2,1)S(1)}, u32[]{:S(2)}, u32[]{:S(2)}) collective-permute-start(bf16[128,2048]{1,0:T(8,128)(2,1)S(1)} %get-tuple-element.43.refs_0_), channel_id=1, source_target_pairs={{0,4},{1,5},{4,8},{5,9},{8,12},{9,13},{12,14},{13,15},{14,10},{15,... | collective-permute-start | bytes 1572872 | tf_op jit(solution)/shard_map/ppermute | solution.py:302
  87.2 2.7 %collective-permute-start.26 = (bf16[128,2048]{1,0:T(8,128)(2,1)S(1)}, bf16[128,2048]{1,0:T(8,128)(2,1)S(1)}, u32[]{:S(2)}, u32[]{:S(2)}) collective-permute-start(bf16[128,2048]{1,0:T(8,128)(2,1)S(1)} %collective-permute-done.24.refs_1_), channel_id=1, source_target_pairs={{0,1},{1,0},{2,3},{3,2},{4,5},{5,4},{6,7},{7,6},{8,9},{9,8},{10,11... | collective-permute-start | bytes 1572872 | tf_op jit(solution)/shard_map/ppermute | solution.py:306
  87.6 2.4 %collective-permute-start.25 = (bf16[128,2048]{1,0:T(8,128)(2,1)S(1)}, bf16[128,2048]{1,0:T(8,128)(2,1)S(1)}, u32[]{:S(2)}, u32[]{:S(2)}) collective-permute-start(bf16[128,2048]{1,0:T(8,128)(2,1)S(1)} %collective-permute-done.23.refs_0_), channel_id=1, source_target_pairs={{0,1},{1,0},{2,3},{3,2},{4,5},{5,4},{6,7},{7,6},{8,9},{9,8},{10,11... | collective-permute-start | bytes 1572872 | tf_op jit(solution)/shard_map/ppermute | solution.py:306
  87.8 14.2 %collective-permute-start.29 = (bf16[128,2048]{1,0:T(8,128)(2,1)S(1)}, bf16[128,2048]{1,0:T(8,128)(2,1)S(1)}, u32[]{:S(2)}, u32[]{:S(2)}) collective-permute-start(bf16[128,2048]{1,0:T(8,128)(2,1)S(1)} %collective-permute-done.24.refs_1_), channel_id=1, source_target_pairs={{0,2},{1,3},{4,0},{5,1},{8,4},{9,5},{12,8},{13,9},{14,12},{15,13},... | collective-permute-start | bytes 1572872 | tf_op jit(solution)/shard_map/ppermute | solution.py:302
  89.4 14.1 %collective-permute-start.28 = (bf16[128,2048]{1,0:T(8,128)(2,1)S(1)}, bf16[128,2048]{1,0:T(8,128)(2,1)S(1)}, u32[]{:S(2)}, u32[]{:S(2)}) collective-permute-start(bf16[128,2048]{1,0:T(8,128)(2,1)S(1)} %collective-permute-done.23.refs_0_), channel_id=1, source_target_pairs={{0,4},{1,5},{4,8},{5,9},{8,12},{9,13},{12,14},{13,15},{14,10},{15,... | collective-permute-start | bytes 1572872 | tf_op jit(solution)/shard_map/ppermute | solution.py:302
  102.0 3.7 %collective-permute-start.31 = (bf16[128,2048]{1,0:T(8,128)(2,1)S(1)}, bf16[128,2048]{1,0:T(8,128)(2,1)S(1)}, u32[]{:S(2)}, u32[]{:S(2)}) collective-permute-start(bf16[128,2048]{1,0:T(8,128)(2,1)S(1)} %collective-permute-done.29.refs_1_), channel_id=1, source_target_pairs={{0,1},{1,0},{2,3},{3,2},{4,5},{5,4},{6,7},{7,6},{8,9},{9,8},{10,11... | collective-permute-start | bytes 1572872 | tf_op jit(solution)/shard_map/ppermute | solution.py:306
  103.5 14.3 %collective-permute-start.33 = (bf16[128,2048]{1,0:T(8,128)(2,1)S(1)}, bf16[128,2048]{1,0:T(8,128)(2,1)S(1)}, u32[]{:S(2)}, u32[]{:S(2)}) collective-permute-start(bf16[128,2048]{1,0:T(8,128)(2,1)S(1)} %collective-permute-done.28.refs_0_), channel_id=1, source_target_pairs={{0,4},{1,5},{4,8},{5,9},{8,12},{9,13},{12,14},{13,15},{14,10},{15,... | collective-permute-start | bytes 1572872 | tf_op jit(solution)/shard_map/ppermute | solution.py:302
  104.0 14.1 %collective-permute-start.35 = (bf16[128,2048]{1,0:T(8,128)(2,1)S(1)}, bf16[128,2048]{1,0:T(8,128)(2,1)S(1)}, u32[]{:S(2)}, u32[]{:S(2)}) collective-permute-start(bf16[128,2048]{1,0:T(8,128)(2,1)S(1)} %collective-permute-done.29.refs_1_), channel_id=1, source_target_pairs={{0,2},{1,3},{4,0},{5,1},{8,4},{9,5},{12,8},{13,9},{14,12},{15,13},... | collective-permute-start | bytes 1572872 | tf_op jit(solution)/shard_map/ppermute | solution.py:302
  117.8 8.0 %collective-permute-start.34 = (bf16[64,2048]{1,0:T(8,128)(2,1)S(1)}, bf16[64,2048]{1,0:T(8,128)(2,1)S(1)}, u32[]{:S(2)}, u32[]{:S(2)}) collective-permute-start(bf16[64,2048]{1,0:T(8,128)(2,1)S(1)} %slice.73), channel_id=1, source_target_pairs={{0,4},{1,5},{4,8},{5,9},{8,12},{9,13},{12,14},{13,15},{14,10},{15,... | collective-permute-start | bytes 786440 | tf_op jit(solution)/shard_map/ppermute | solution.py:302
  118.2 7.7 %collective-permute-start.36 = (bf16[64,2048]{1,0:T(8,128)(2,1)S(1)}, bf16[64,2048]{1,0:T(8,128)(2,1)S(1)}, u32[]{:S(2)}, u32[]{:S(2)}) collective-permute-start(bf16[64,2048]{1,0:T(8,128)(2,1)S(1)} %slice.74), channel_id=1, source_target_pairs={{0,2},{1,3},{4,0},{5,1},{8,4},{9,5},{12,8},{13,9},{14,12},{15,13},... | collective-permute-start | bytes 786440 | tf_op jit(solution)/shard_map/ppermute | solution.py:302
  134.7 2.5 %collective-permute-start.38 = (bf16[128,2048]{1,0:T(8,128)(2,1)S(1)}, bf16[128,2048]{1,0:T(8,128)(2,1)S(1)}, u32[]{:S(2)}, u32[]{:S(2)}) collective-permute-start(bf16[128,2048]{1,0:T(8,128)(2,1)S(1)} %collective-permute-done.33.refs_0_), channel_id=1, source_target_pairs={{0,1},{1,0},{2,3},{3,2},{4,5},{5,4},{6,7},{7,6},{8,9},{9,8},{10,11... | collective-permute-start | bytes 1572872 | tf_op jit(solution)/shard_map/ppermute | solution.py:306
  135.1 11.9 %collective-permute-start.41 = (bf16[128,2048]{1,0:T(8,128)(2,1)S(1)}, bf16[128,2048]{1,0:T(8,128)(2,1)S(1)}, u32[]{:S(2)}, u32[]{:S(2)}) collective-permute-start(bf16[128,2048]{1,0:T(8,128)(2,1)S(1)} %get-tuple-element.63), channel_id=1, source_target_pairs={{0,1},{1,0},{2,3},{3,2},{4,5},{5,4},{6,7},{7,6},{8,9},{9,8},{10,11... | collective-permute-start | bytes 1572872 | tf_op jit(solution)/shard_map/ppermute | solution.py:306
  146.8 9.0 %collective-permute-start.40 = (bf16[128,2048]{1,0:T(8,128)(2,1)S(1)}, bf16[128,2048]{1,0:T(8,128)(2,1)S(1)}, u32[]{:S(2)}, u32[]{:S(2)}) collective-permute-start(bf16[128,2048]{1,0:T(8,128)(2,1)S(1)} %get-tuple-element.62), channel_id=1, source_target_pairs={{0,1},{1,0},{2,3},{3,2},{4,5},{5,4},{6,7},{7,6},{8,9},{9,8},{10,11... | collective-permute-start | bytes 1572872 | tf_op jit(solution)/shard_map/ppermute | solution.py:306
  147.2 8.6 %collective-permute-start.42 = (bf16[64,2048]{1,0:T(8,128)(2,1)S(1)}, bf16[64,2048]{1,0:T(8,128)(2,1)S(1)}, u32[]{:S(2)}, u32[]{:S(2)}) collective-permute-start(bf16[64,2048]{1,0:T(8,128)(2,1)S(1)} %get-tuple-element.68), channel_id=1, source_target_pairs={{0,4},{1,5},{4,8},{5,9},{8,12},{9,13},{12,14},{13,15},{14,10},{15,... | collective-permute-start | bytes 786440 | tf_op jit(solution)/shard_map/ppermute | solution.py:302
  148.5 8.8 %collective-permute-start.48 = (bf16[128,2048]{1,0:T(8,128)(2,1)S(1)}, bf16[128,2048]{1,0:T(8,128)(2,1)S(1)}, u32[]{:S(2)}, u32[]{:S(2)}) collective-permute-start(bf16[128,2048]{1,0:T(8,128)(2,1)S(1)} %get-tuple-element.67), channel_id=1, source_target_pairs={{0,1},{1,0},{2,3},{3,2},{4,5},{5,4},{6,7},{7,6},{8,9},{9,8},{10,11... | collective-permute-start | bytes 1572872 | tf_op jit(solution)/shard_map/ppermute | solution.py:306
  148.6 10.0 %collective-permute-start.32 = (bf16[128,2048]{1,0:T(8,128)(2,1)S(1)}, bf16[128,2048]{1,0:T(8,128)(2,1)S(1)}, u32[]{:S(2)}, u32[]{:S(2)}) collective-permute-start(bf16[128,2048]{1,0:T(8,128)(2,1)S(1)} %get-tuple-element.54), channel_id=1, source_target_pairs={{0,1},{1,0},{2,3},{3,2},{4,5},{5,4},{6,7},{7,6},{8,9},{9,8},{10,11... | collective-permute-start | bytes 1572872 | tf_op jit(solution)/shard_map/ppermute | solution.py:306
  149.0 8.3 %collective-permute-start.49 = (bf16[64,2048]{1,0:T(8,128)(2,1)S(1)}, bf16[64,2048]{1,0:T(8,128)(2,1)S(1)}, u32[]{:S(2)}, u32[]{:S(2)}) collective-permute-start(bf16[64,2048]{1,0:T(8,128)(2,1)S(1)} %get-tuple-element.69), channel_id=1, source_target_pairs={{0,2},{1,3},{4,0},{5,1},{8,4},{9,5},{12,8},{13,9},{14,12},{15,13},... | collective-permute-start | bytes 786440 | tf_op jit(solution)/shard_map/ppermute | solution.py:302
  156.0 13.4 %collective-permute-start.43 = (bf16[128,2048]{1,0:T(8,128)(2,1)S(1)}, bf16[128,2048]{1,0:T(8,128)(2,1)S(1)}, u32[]{:S(2)}, u32[]{:S(2)}) collective-permute-start(bf16[128,2048]{1,0:T(8,128)(2,1)S(1)} %add_convert_fusion.6), channel_id=1, source_target_pairs={{0,4},{1,5},{4,8},{5,9},{8,12},{9,13},{12,14},{13,15},{14,10},{15,... | collective-permute-start | bytes 1572872 | tf_op jit(solution)/shard_map/ppermute | solution.py:302
  157.3 13.7 %collective-permute-start.47 = (bf16[128,2048]{1,0:T(8,128)(2,1)S(1)}, bf16[128,2048]{1,0:T(8,128)(2,1)S(1)}, u32[]{:S(2)}, u32[]{:S(2)}) collective-permute-start(bf16[128,2048]{1,0:T(8,128)(2,1)S(1)} %get-tuple-element.65), channel_id=1, source_target_pairs={{0,1},{1,0},{2,3},{3,2},{4,5},{5,4},{6,7},{7,6},{8,9},{9,8},{10,11... | collective-permute-start | bytes 1572872 | tf_op jit(solution)/shard_map/ppermute | solution.py:306
  157.5 14.4 %collective-permute-start.50 = (bf16[128,2048]{1,0:T(8,128)(2,1)S(1)}, bf16[128,2048]{1,0:T(8,128)(2,1)S(1)}, u32[]{:S(2)}, u32[]{:S(2)}) collective-permute-start(bf16[128,2048]{1,0:T(8,128)(2,1)S(1)} %add_convert_fusion.3), channel_id=1, source_target_pairs={{0,2},{1,3},{4,0},{5,1},{8,4},{9,5},{12,8},{13,9},{14,12},{15,13},... | collective-permute-start | bytes 1572872 | tf_op jit(solution)/shard_map/ppermute | solution.py:302
  158.4 14.6 %collective-permute-start.27 = (bf16[128,2048]{1,0:T(8,128)(2,1)S(1)}, bf16[128,2048]{1,0:T(8,128)(2,1)S(1)}, u32[]{:S(2)}, u32[]{:S(2)}) collective-permute-start(bf16[128,2048]{1,0:T(8,128)(2,1)S(1)} %get-tuple-element.49), channel_id=1, source_target_pairs={{0,1},{1,0},{2,3},{3,2},{4,5},{5,4},{6,7},{7,6},{8,9},{9,8},{10,11... | collective-permute-start | bytes 1572872 | tf_op jit(solution)/shard_map/ppermute | solution.py:306
  169.7 12.5 %collective-permute-start.44 = (bf16[128,2048]{1,0:T(8,128)(2,1)S(1)}, bf16[128,2048]{1,0:T(8,128)(2,1)S(1)}, u32[]{:S(2)}, u32[]{:S(2)}) collective-permute-start(bf16[128,2048]{1,0:T(8,128)(2,1)S(1)} %add_convert_fusion.5), channel_id=1, source_target_pairs={{0,4},{1,5},{4,8},{5,9},{8,12},{9,13},{12,14},{13,15},{14,10},{15,... | collective-permute-start | bytes 1572872 | tf_op jit(solution)/shard_map/ppermute | solution.py:302
  171.0 12.8 %collective-permute-start.46 = (bf16[128,2048]{1,0:T(8,128)(2,1)S(1)}, bf16[128,2048]{1,0:T(8,128)(2,1)S(1)}, u32[]{:S(2)}, u32[]{:S(2)}) collective-permute-start(bf16[128,2048]{1,0:T(8,128)(2,1)S(1)} %get-tuple-element.64), channel_id=1, source_target_pairs={{0,1},{1,0},{2,3},{3,2},{4,5},{5,4},{6,7},{7,6},{8,9},{9,8},{10,11... | collective-permute-start | bytes 1572872 | tf_op jit(solution)/shard_map/ppermute | solution.py:306
  172.1 13.6 %collective-permute-start.51 = (bf16[128,2048]{1,0:T(8,128)(2,1)S(1)}, bf16[128,2048]{1,0:T(8,128)(2,1)S(1)}, u32[]{:S(2)}, u32[]{:S(2)}) collective-permute-start(bf16[128,2048]{1,0:T(8,128)(2,1)S(1)} %add_convert_fusion.2), channel_id=1, source_target_pairs={{0,2},{1,3},{4,0},{5,1},{8,4},{9,5},{12,8},{13,9},{14,12},{15,13},... | collective-permute-start | bytes 1572872 | tf_op jit(solution)/shard_map/ppermute | solution.py:302
  173.0 13.8 %collective-permute-start.22 = (bf16[128,2048]{1,0:T(8,128)(2,1)S(1)}, bf16[128,2048]{1,0:T(8,128)(2,1)S(1)}, u32[]{:S(2)}, u32[]{:S(2)}) collective-permute-start(bf16[128,2048]{1,0:T(8,128)(2,1)S(1)} %get-tuple-element.45), channel_id=1, source_target_pairs={{0,1},{1,0},{2,3},{3,2},{4,5},{5,4},{6,7},{7,6},{8,9},{9,8},{10,11... | collective-permute-start | bytes 1572872 | tf_op jit(solution)/shard_map/ppermute | solution.py:306
  182.5 11.6 %collective-permute-start.45 = (bf16[128,2048]{1,0:T(8,128)(2,1)S(1)}, bf16[128,2048]{1,0:T(8,128)(2,1)S(1)}, u32[]{:S(2)}, u32[]{:S(2)}) collective-permute-start(bf16[128,2048]{1,0:T(8,128)(2,1)S(1)} %add_convert_fusion.4), channel_id=1, source_target_pairs={{0,4},{1,5},{4,8},{5,9},{8,12},{9,13},{12,14},{13,15},{14,10},{15,... | collective-permute-start | bytes 1572872 | tf_op jit(solution)/shard_map/ppermute | solution.py:302
  186.0 12.7 %collective-permute-start.52 = (bf16[128,2048]{1,0:T(8,128)(2,1)S(1)}, bf16[128,2048]{1,0:T(8,128)(2,1)S(1)}, u32[]{:S(2)}, u32[]{:S(2)}) collective-permute-start(bf16[128,2048]{1,0:T(8,128)(2,1)S(1)} %add_convert_fusion.1), channel_id=1, source_target_pairs={{0,2},{1,3},{4,0},{5,1},{8,4},{9,5},{12,8},{13,9},{14,12},{15,13},... | collective-permute-start | bytes 1572872 | tf_op jit(solution)/shard_map/ppermute | solution.py:302
  (21 other events, 124.2 us)

commit v3 on v1

v3 whole, which is shorter than its diff:
```python
import functools
import math

import jax
import jax.numpy as jnp
from jax import lax
from jax.experimental import pallas as pl
from jax.experimental.pallas import tpu as pltpu
from jax.sharding import PartitionSpec as P

D = 2048
HQ = 16
KVH = 4
HD = 128
TOP = 8
NB = 4
CORES = 2
VMEM_BYTES = 16 * 1024 * 1024
F32 = jnp.float32
BF16 = jnp.bfloat16


def normalize(x):
    return x * lax.rsqrt(jnp.mean(x * x, axis=-1, keepdims=True) + 1e-06)


def params():
    return pltpu.CompilerParams(vmem_limit_bytes=VMEM_BYTES)


def whole(*shape):
    return pl.BlockSpec(shape, lambda *_: (0,) * len(shape))


def summary_kernel(experts, ids, keys, values, gain, routes, scores, out, rows):
    tokens = ids.shape[1]
    block = lax.broadcasted_iota(jnp.int32, (8, tokens), 0)
    member = (ids[...] == block) & (block < NB)
    ones = jnp.where(member, 1.0, 0.0).astype(F32)
    count = jnp.maximum(jnp.sum(ones, axis=-1, keepdims=True), 1.0)
    indicator = ones.astype(BF16)
    kmean = jnp.dot(indicator, keys[...], preferred_element_type=F32) / count
    vmean = jnp.dot(indicator, values[...], preferred_element_type=F32) / count
    for g in range(KVH):
        cols = slice(g * HD, (g + 1) * HD)
        rows[8 * g : 8 * g + NB, :] = (normalize(kmean[:, cols]) * gain[...])[:NB]
        rows[8 * g + NB : 8 * g + 2 * NB, :] = normalize(vmean[:, cols])[:NB]
    base = 8 * KVH
    if experts:
        combine = scores[...] / jnp.sum(scores[...], axis=0, keepdims=True)
        expert = lax.broadcasted_iota(jnp.int32, (experts, tokens), 0)
        table = jnp.zeros((experts, tokens), F32)
        for k in range(TOP):
            table += jnp.where(routes[k : k + 1, :] == expert, combine[k : k + 1, :], 0.0)
        high = table.astype(BF16).astype(F32)
        rows[base : base + experts, :] = high
        rows[base + experts : base + 2 * experts, :] = table - high
    out[...] = rows[...].astype(BF16)


def summarize(ids, keys, values, gain, routes, scores, experts):
    tokens = ids.shape[0]
    height = 8 * KVH + 2 * experts
    return pl.pallas_call(
        functools.partial(summary_kernel, experts),
        out_shape=jax.ShapeDtypeStruct((height, HD), BF16),
        scratch_shapes=[pltpu.VMEM((height, HD), F32)],
        compiler_params=params(),
        name="summaries",
    )(ids.reshape(1, tokens), keys, values, gain.reshape(1, HD), routes.T, scores.T)


def attention_kernel(me, queries, keys, values, gathered, attended):
    tokens = queries.shape[0]
    group = HQ // KVH
    scale = 1.0 / math.sqrt(HD)
    shards = gathered.shape[0]
    wide = shards * 2 * NB
    row = lax.broadcasted_iota(jnp.int32, (tokens, tokens), 0)
    col = lax.broadcasted_iota(jnp.int32, (tokens, tokens), 1)
    causal = row >= col
    place = lax.broadcasted_iota(jnp.int32, (tokens, wide), 1)
    owner = (place // (2 * NB)) ^ me[1]
    earlier = (owner < me[0]) & (place % (2 * NB) < NB)
    seen = jnp.concatenate([causal, earlier], axis=1)
    for g in range(KVH):
        cols = slice(g * HD, (g + 1) * HD)
        pairs = gathered[:, 16 * (g // 2) : 16 * (g // 2) + 16, :].astype(F32)
        half = 8 * (g % 2)
        remote = pairs[:, half : half + 8, :].reshape(wide, HD)
        key_all = jnp.concatenate([keys[:, cols], remote.astype(BF16)], axis=0)
        shifted = pltpu.roll(remote, wide - NB, 0)
        value_all = jnp.concatenate([values[:, cols], shifted.astype(BF16)], axis=0)
        for i in range(group):
            h = g * group + i
            head = slice(h * HD, (h + 1) * HD)
            scores = (
                lax.dot_general(
                    queries[:, head],
                    key_all,
                    (((1,), (1,)), ((), ())),
                    preferred_element_type=F32,
                )
                * scale
            )
            scores = jnp.where(seen, scores, -jnp.inf)
            top = jnp.max(scores, axis=-1, keepdims=True)
            expo = jnp.exp(scores - top)
            weights = (expo / jnp.sum(expo, axis=-1, keepdims=True)).astype(BF16)
            attended[:, head] = jnp.dot(
                weights, value_all, preferred_element_type=F32
            ).astype(BF16)


def attend(me, queries, keys, values, gathered):
    tokens = queries.shape[0]
    return pl.pallas_call(
        attention_kernel,
        grid_spec=pltpu.PrefetchScalarGridSpec(
            num_scalar_prefetch=1,
            grid=(1,),
            in_specs=[whole(*a.shape) for a in (queries, keys, values, gathered)],
            out_specs=whole(tokens, HQ * HD),
        ),
        out_shape=jax.ShapeDtypeStruct((tokens, HQ * HD), BF16),
        compiler_params=params(),
        cost_estimate=pl.CostEstimate(
            flops=4 * HQ * HD * tokens * 2 * tokens,
            bytes_accessed=2 * 4 * tokens * HQ * HD,
            transcendentals=HQ * tokens * 2 * tokens,
        ),
        name="attention",
    )(me, queries, keys, values, gathered)


def smem():
    return pl.BlockSpec(memory_space=pltpu.SMEM)


def vmem():
    return pl.BlockSpec(memory_space=pltpu.VMEM)


def pair_up(here, pair, own, other):
    rows = pair.shape[0] // CORES
    at = pl.multiple_of(here[0] * rows, rows)
    for i, block in enumerate(own):
        step = i * block.shape[0]
        pair[pl.ds(at + step, block.shape[0]), :] = block[...]
    at = pl.multiple_of((1 - here[0]) * rows, rows)
    for i, block in enumerate(other):
        step = i * block.shape[0]
        pair[pl.ds(at + step, block.shape[0]), :] = block[...]


def project_first_kernel(levels, here, tokens, *refs):
    blocks, acc, pair = refs[:-2], refs[-2], refs[-1]
    rows = pair.shape[1]
    for i in range(levels):
        pair_up(here, pair.at[i], [blocks[2 * i]], [blocks[2 * i + 1]])
    for i in range(levels):
        at = pl.multiple_of(here[1 + i] * rows, rows)
        part = jnp.dot(tokens[:, pl.ds(at, rows)], pair[i], preferred_element_type=F32)
        if i == 0:
            acc[...] = part
        else:
            acc[...] += part


def project_first(here, tokens, blocks):
    rows, width = blocks[0].shape
    levels = len(blocks) // 2
    return pl.pallas_call(
        functools.partial(project_first_kernel, levels),
        in_specs=[smem()] + [vmem()] * (1 + len(blocks)),
        out_specs=vmem(),
        out_shape=jax.ShapeDtypeStruct((tokens.shape[0], width), F32),
        scratch_shapes=[pltpu.VMEM((levels, 2 * rows, width), BF16)],
        compiler_params=params(),
        cost_estimate=pl.CostEstimate(
            flops=2 * tokens.shape[0] * rows * width * len(blocks),
            bytes_accessed=2 * rows * width * len(blocks),
            transcendentals=0,
        ),
        name="project_first",
    )(here, tokens, *blocks)


def project_last_kernel(at, here, tokens, acc, gain, a, b, c, d, hidden, projected, normed, pair):
    rows = pair.shape[0]
    pair_up(here, pair, [a, b], [c, d])
    columns = pl.ds(pl.multiple_of(here[at] * rows, rows), rows)
    total = acc[...] + jnp.dot(tokens[:, columns], pair[...], preferred_element_type=F32)
    hidden[...] = total
    projected[...] = total.astype(BF16)
    normed[...] = (normalize(total) * gain[...]).astype(BF16)


def project_last(at, here, tokens, acc, gain, halves):
    count, width = acc.shape
    half = halves[0].shape[0]
    return pl.pallas_call(
        functools.partial(project_last_kernel, at),
        in_specs=[smem()] + [vmem()] * 7,
        out_specs=[vmem()] * 3,
        out_shape=[
            jax.ShapeDtypeStruct((count, width), F32),
            jax.ShapeDtypeStruct((count, width), BF16),
            jax.ShapeDtypeStruct((count, width), BF16),
        ],
        scratch_shapes=[pltpu.VMEM((4 * half, width), BF16)],
        compiler_params=params(),
        cost_estimate=pl.CostEstimate(
            flops=8 * count * half * width, bytes_accessed=12 * count * width, transcendentals=0
        ),
        name="project_last",
    )(here, tokens, acc, gain.reshape(1, width), *halves)


def expert_kernel(places, here, table, *refs):
    count = len(places)
    own = count // 2
    blocks, (gate, up, down) = refs[:count], refs[count : count + 3]
    outs = refs[count + 3 : count + 3 + own]
    sent = refs[count + 3 + own]
    tokens, act, scale = refs[count + 4 + own :]
    rows, depth = blocks[0].shape
    lanes = table.shape[1]
    ff = gate.shape[2]
    tile = 256
    for i in range(count):
        tokens[i * rows : (i + 1) * rows, :] = blocks[i][...]
        weight = table[pl.ds(here[places[i]], 1), :]
        weight = jnp.transpose(jnp.broadcast_to(weight, (lanes, lanes)))
        scale[i * rows : (i + 1) * rows, :] = weight
    for f in range(0, ff, tile):
        cols = slice(f, f + tile)
        g = jnp.dot(tokens[...], gate[0, :, cols], preferred_element_type=F32)
        u = jnp.dot(tokens[...], up[0, :, cols], preferred_element_type=F32)
        act[:, cols] = (g / (1.0 + jnp.exp(-g)) * u).astype(BF16)
    for d in range(0, depth, tile):
        cols = slice(d, d + tile)
        part = jnp.dot(act[...], down[0, :, cols], preferred_element_type=F32)
        weight = jnp.concatenate([scale[...]] * (tile // lanes), axis=1)
        part = (part * weight).astype(BF16)
        for i in range(own):
            outs[i][:, cols] = part[i * rows : (i + 1) * rows]
        sent[:, cols] = part[own * rows :]


def expert_blocks(places, here, table, blocks, gate, up, down):
    count = len(blocks)
    own = count // 2
    rows, width = blocks[0].shape
    ff = gate.shape[2]
    return pl.pallas_call(
        functools.partial(expert_kernel, places),
        in_specs=[smem()] + [vmem()] * (1 + count + 3),
        out_specs=[vmem()] * (own + 1),
        out_shape=[jax.ShapeDtypeStruct((rows, width), BF16)] * own
        + [jax.ShapeDtypeStruct((own * rows, width), BF16)],
        scratch_shapes=[
            pltpu.VMEM((count * rows, width), BF16),
            pltpu.VMEM((count * rows, ff), BF16),
            pltpu.VMEM((count * rows, table.shape[1]), F32),
        ],
        compiler_params=params(),
        cost_estimate=pl.CostEstimate(flops=0, bytes_accessed=0, transcendentals=0),
        name="experts",
    )(here, table, *blocks, gate, up, down)


class Ring:
    def __init__(self, n):
        self.chips = n // CORES
        self.cycle = [*range(0, self.chips, 2), *range(self.chips - 1, 0, -2)]
        self.far = self.chips // 2

    def step(self, x, by, label):
        pairs = []
        for p, chip in enumerate(self.cycle):
            to = self.cycle[(p + by) % self.chips]
            pairs += [(chip * CORES + c, to * CORES + c) for c in range(CORES)]
        with jax.named_scope(label + ("_up" if by > 0 else "_down")):
            return lax.ppermute(x, "ctx", pairs)

    def swap(self, x):
        n = self.chips * CORES
        with jax.named_scope("swap_cores"):
            return lax.ppermute(x, "ctx", [(i, i ^ 1) for i in range(n)])

    def table(self, n):
        place = {chip: p for p, chip in enumerate(self.cycle)}
        rows = []
        for i in range(n):
            p, core = place[i // CORES], i % CORES
            chips = [self.cycle[p]]
            for k in range(1, self.far):
                chips += [self.cycle[(p - k) % self.chips], self.cycle[(p + k) % self.chips]]
            chips.append(self.cycle[(p + self.far) % self.chips])
            own = [(chip * CORES + core) ^ i for chip in chips]
            other = [(chip * CORES + 1 - core) ^ i for chip in chips]
            rows.append([core, *chips, *own, *other])
        return rows


def xor_round(x, count, n):
    m = x.shape[0]
    with jax.named_scope("summary_round"):
        others = [
            lax.ppermute(x, "ctx", [(i, i ^ (m * c)) for i in range(n)]) for c in range(1, count)
        ]
    return jnp.concatenate([x, *others], axis=0)


def after(x, *earlier):
    return lax.optimization_barrier((x, earlier))[0]


def add(*xs):
    total = xs[0].astype(F32)
    for x in xs[1:]:
        total = total + x.astype(F32)
    return total.astype(BF16)


def ring_body(
    n,
    queries,
    keys,
    values,
    block_ids,
    out_weight,
    summary_gain,
    norm_gain,
    routes,
    route_scores,
    expert_gate,
    expert_up,
    expert_down,
):
    index = lax.axis_index("ctx")
    core = index % CORES
    ring = Ring(n)
    here = jnp.asarray(ring.table(n), jnp.int32)[index]
    half = queries.shape[0] // 2

    def both(pair, *earlier):
        return [after(x, *earlier) for x in pair]

    def forward(pair, label):
        return [ring.step(pair[0], 1, label), ring.step(pair[1], -1, label)]

    def forward_far(pair, label):
        return forward([pair[0][:half], pair[1][half:]], label)

    pair = forward([out_weight, out_weight], "weight_1")
    blocks = [out_weight, ring.swap(out_weight)]
    small = summarize(block_ids, keys, values, summary_gain, routes, route_scores, n)[None]
    small = xor_round(xor_round(small, 2, n), 4, n)
    for k in range(1, ring.far):
        if k == 1:
            small = after(small, *pair)
            while small.shape[0] < n:
                small = xor_round(small, 2, n)
        if k == 2:
            pair = both(pair, small)
            attended = attend(jnp.stack([index, index]), queries, keys, values, small[:, : 8 * KVH])
        if k == 3:
            pair = both(pair, attended)
        for x in pair:
            blocks += [x, ring.swap(x)]
        if k < ring.far - 1:
            pair = forward(pair, "weight_" + str(k + 1))
    pair = forward_far(pair, "weight_far")
    base = 8 * KVH
    parts = lax.dynamic_index_in_dim(
        small[:, base:].reshape(n, 2, n, HD), index, axis=2, keepdims=False
    ).astype(F32)
    table = parts[:, 0] + parts[:, 1]
    acc = project_first(here, attended, blocks)
    pair = both(pair, acc, table)
    hidden, projected, normed = project_last(
        ring.chips, here, attended, acc, norm_gain, [*pair, *(ring.swap(x) for x in pair)]
    )

    def experts(level, chips):
        others = [ring.swap(x) for x in level]
        places = [1 + ring.chips + c for c in chips] + [1 + 2 * ring.chips + c for c in chips]
        *kept, sent = expert_blocks(
            tuple(places), here, table, [*level, *others], expert_gate, expert_up, expert_down
        )
        return [*kept, ring.swap(sent)]

    pair = forward([normed, normed], "token_1")
    results = [experts([normed], [0])]
    for k in range(1, ring.far):
        pair = both(pair, results[-1][0])
        level = pair
        if k < ring.far - 1:
            pair = forward(pair, "token_" + str(k + 1))
        else:
            pair = forward_far(pair, "token_far")
        results.append(experts(level, [2 * k - 1, 2 * k]))
    pair = both(pair, *(r[-1] for r in results[:-1]), results[-1][0])
    far = experts([jnp.concatenate(pair, axis=0)], [ring.chips - 1])

    total = add(*far)
    pair = forward_far([total, total], "sum_far")
    rows = queries.shape[0]
    for k in range(ring.far - 1, 0, -1):
        behind, ahead, back = results[k]
        up, down = pair
        if k == ring.far - 1:
            zero = jnp.zeros_like(up)
            up = jnp.concatenate([up, zero], axis=0)
            down = jnp.concatenate([zero, down], axis=0)
        up = add(after(ahead, total), back[rows:], up)
        total = add(after(behind, up), back[:rows], down)
        pair = forward([up, total], "sum_" + str(k))
    mine, back = results[0]
    mixed = add(hidden, mine, back, *pair)
    return projected, mixed


def exchange_body(
    n,
    queries,
    keys,
    values,
    block_ids,
    out_weight,
    summary_gain,
    norm_gain,
    routes,
    route_scores,
    expert_gate,
    expert_up,
    expert_down,
):
    tokens_here = queries.shape[0]
    index = lax.axis_index("ctx")
    small = summarize(block_ids, keys, values, summary_gain, routes, route_scores, 0)
    small = lax.all_gather(small, "ctx", axis=0, tiled=False)
    attended = attend(jnp.stack([index, 0 * index]), queries, keys, values, small)
    hidden = jnp.dot(
        attended,
        lax.all_gather(out_weight, "ctx", axis=0, tiled=True),
        preferred_element_type=F32,
    )
    normed = (normalize(hidden) * norm_gain).astype(BF16)
    combine = route_scores / jnp.sum(route_scores, axis=-1, keepdims=True)
    held = expert_gate.shape[0]
    experts_all = held * n
    capacity = capacity_of(tokens_here, experts_all)
    flat_routes = routes.reshape(-1)
    count = tokens_here * TOP
    hits = flat_routes[:, None] == jnp.arange(experts_all, dtype=jnp.int32)[None, :]
    before = jnp.arange(count)[:, None] > jnp.arange(count)[None, :]
    ahead = jnp.dot(before.astype(BF16), hits.astype(BF16), preferred_element_type=F32)
    slot = jnp.sum(jnp.where(hits, ahead, 0.0), axis=-1).astype(jnp.int32)
    target = flat_routes * capacity + slot
    source = jnp.arange(count, dtype=jnp.int32) // TOP
    outgoing = jnp.zeros((experts_all * capacity, D), BF16).at[target].set(normed[source])
    outgoing = outgoing.reshape(experts_all, capacity, D)
    arrived = lax.all_to_all(outgoing, "ctx", split_axis=0, concat_axis=0, tiled=True)
    inputs = (
        arrived.reshape(n, held, capacity, D).transpose(1, 0, 2, 3).reshape(held, n * capacity, D)
    )
    gate = jnp.einsum("erd,edf->erf", inputs, expert_gate, preferred_element_type=F32)
    upper = jnp.einsum("erd,edf->erf", inputs, expert_up, preferred_element_type=F32)
    act = (jax.nn.silu(gate) * upper).astype(BF16)
    result = jnp.einsum("erf,efd->erd", act, expert_down, preferred_element_type=F32)
    result = (
        result.astype(BF16)
        .reshape(held, n, capacity, D)
        .transpose(1, 0, 2, 3)
        .reshape(n * held, capacity, D)
    )
    returned = lax.all_to_all(result, "ctx", split_axis=0, concat_axis=0, tiled=True)
    returned = returned.reshape(experts_all * capacity, D)
    picked = jnp.take(returned, target, axis=0).reshape(tokens_here, TOP, D)
    blended = jnp.sum(combine[:, :, None] * picked.astype(F32), axis=1)
    return (hidden.astype(BF16), (hidden + blended).astype(BF16))


def capacity_of(tokens, experts):
    return max(2, 5 * tokens * TOP // (4 * experts))


def solution(mesh):
    n = mesh.shape["ctx"]

    def body(*args):
        tokens, held = args[0].shape[0], args[9].shape[0]
        dense = tokens <= 2 * capacity_of(tokens, held * n) and held == 1
        fits = n >= 16 and n & (n - 1) == 0
        return (ring_body if dense and fits else exchange_body)(n, *args)

    in_specs = (
        P(("groups", "ctx"), None),
        P(("groups", "ctx"), None),
        P(("groups", "ctx"), None),
        P(("groups", "ctx")),
        P("ctx", None),
        P(),
        P(),
        P(("groups", "ctx"), None),
        P(("groups", "ctx"), None),
        P("ctx", None, None),
        P("ctx", None, None),
        P("ctx", None, None),
    )
    out_specs = (P(("groups", "ctx"), None), P(("groups", "ctx"), None))
    return jax.shard_map(body, mesh=mesh, in_specs=in_specs, out_specs=out_specs, check_vma=False)
```

time: 219 us -> 179 us (0.82)
  Pallas kernels: 50.8 us -> 30.5 us
  waiting for transfers between devices: 113 us -> 100 us
  local copies, waits for them, and re-layouts: 12.9 us -> 8.3 us
    pallas_call x7, Pallas kernels: 48.4 us -> 28.1 us  [the longest x5 23.3 us: expert_blocks(): pl.pallas_call(functools.partial(expert_kernel, places), in_specs=[smem()...]
    ppermute x24, waiting for transfers between devices: 94.8 us -> 77.9 us  [step(): return lax.ppermute(x, 'ctx', pairs)]
    ppermute x25 -> x22, waiting for transfers between devices: 1.28 us -> 5.18 us  [swap(): return lax.ppermute(x, 'ctx', [(i, i ^ 1) for i in range(n)])]
    unnamed x39 -> x34, local copies, waits for them, and re-layouts: 10.4 us -> 7.41 us
    ppermute x4 -> x5, starting transfers between devices: 3.92 us -> 5.99 us  [xor_round(): lax.ppermute(x, 'ctx', [(i, i ^ m * c) for i in range(n)])]
    ppermute x25 -> x22, starting transfers between devices: 4.72 us -> 3.48 us  [swap(): return lax.ppermute(x, 'ctx', [(i, i ^ 1) for i in range(n)])]
    ppermute x4 -> x5, waiting for transfers between devices: 17.4 us -> 17.2 us  [xor_round(): lax.ppermute(x, 'ctx', [(i, i ^ m * c) for i in range(n)])]
  transfers between devices with their start and end apart: 53 -> 51, of which waited for: 21 -> 26; matrix products, arithmetic and copies ran while one was open for 2% -> 1% of each run, Pallas kernels for 22% -> 14%
where the time goes in v3:
time: 179 us
  waiting for transfers between devices  100 us (56%)
  starting transfers between devices  35.8 us (20%)
  Pallas kernels  30.5 us (17%)
  local copies, waits for them, and re-layouts  8.3 us (5%)
  other arithmetic  2.73 us (2%)
    ppermute x24, waiting for transfers between devices, step(): return lax.ppermute(x, 'ctx', pairs)  77.9 us
    ppermute x24, starting transfers between devices, step(): return lax.ppermute(x, 'ctx', pairs)  26.4 us
    pallas_call x5, Pallas kernels, expert_blocks(): pl.pallas_call(functools.partial(expert_kernel, places), in_specs=[smem()...  23.3 us
    ppermute x5, waiting for transfers between devices, xor_round(): lax.ppermute(x, 'ctx', [(i, i ^ m * c) for i in range(n)])  17.2 us
    unnamed x34, local copies, waits for them, and re-layouts  7.41 us
    ppermute x5, starting transfers between devices, xor_round(): lax.ppermute(x, 'ctx', [(i, i ^ m * c) for i in range(n)])  5.99 us
    ppermute x22, waiting for transfers between devices, swap(): return lax.ppermute(x, 'ctx', [(i, i ^ 1) for i in range(n)])  5.18 us
  transfers between devices with their start and end apart: 51, of which 26 were waited for; matrix products, arithmetic and copies ran while one was open for 1% of the time, Pallas kernels for 14%

profile of v3, /device:TPU:0, one launch (start us, length us, event | category | flops | bytes accessed | tf_op | source)
XLA Modules:
  0.0 178.7 jit_solution(1451734903876942484)
XLA Ops:
  0.6 3.1 %collective-permute-start.4 = (bf16[128,2048]{1,0:T(8,128)(2,1)}, bf16[128,2048]{1,0:T(8,128)(2,1)S(1)}, u32[]{:S(2)}, u32[]{:S(2)}) collective-permute-start(bf16[128,2048]{1,0:T(8,128)(2,1)} %refs_0_.1), channel_id=1, source_target_pairs={{0,4},{1,5},{4,8},{5,9},{8,12},{9,13},{12,14},{13,15},{14,10},{15,... | collective-permute-start | bytes 1572872 | tf_op jit(solution)/shard_map/weight_1_up/ppermute | solution.py:285
  3.7 0.9 copy-done.5
  4.6 0.9 copy-done.7
  8.6 1.2 collective-permute-done
  9.7 2.0 %collective-permute-start.1 = (bf16[2,64,128]{2,1,0:T(8,128)(2,1)S(1)}, bf16[2,64,128]{2,1,0:T(8,128)(2,1)S(1)}, u32[]{:S(2)}, u32[]{:S(2)}) collective-permute-start(bf16[2,64,128]{2,1,0:T(8,128)(2,1)S(1)} %pad_maximum_fusion), channel_id=1, source_target_pairs={{0,2},{1,3},{2,0},{3,1},{4,6},{5,7},{6,4},{7,5},{8,10},{9,11},{10,... | collective-permute-start | bytes 98312 | tf_op jit(solution)/shard_map/summary_round/ppermute | solution.py:311
  11.7 1.6 collective-permute-start.2
  13.3 2.9 %collective-permute-done.4.refs_2_ = bf16[128,2048]{1,0:T(8,128)(2,1)S(1)} collective-permute-done((bf16[128,2048]{1,0:T(8,128)(2,1)}, bf16[128,2048]{1,0:T(8,128)(2,1)S(1)}, u32[]{:S(2)}, u32[]{:S(2)}) %collective-permute-start.4) | collective-permute-done | bytes 524320 | tf_op jit(solution)/shard_map/weight_1_up/ppermute | solution.py:285
  16.2 2.1 %collective-permute-start.10 = (bf16[128,2048]{1,0:T(8,128)(2,1)S(1)}, bf16[128,2048]{1,0:T(8,128)(2,1)S(1)}, u32[]{:S(2)}, u32[]{:S(2)}) collective-permute-start(bf16[128,2048]{1,0:T(8,128)(2,1)S(1)} %collective-permute-done.4.refs_2_), channel_id=1, source_target_pairs={{0,4},{1,5},{4,8},{5,9},{8,12},{9,13},{12,14},{13,15},{14,10},{15,... | collective-permute-start | bytes 1572872 | tf_op jit(solution)/shard_map/weight_2_up/ppermute | solution.py:285
  18.7 2.4 %collective-permute-start.6 = (bf16[8,64,128]{2,1,0:T(8,128)(2,1)S(1)}, bf16[8,64,128]{2,1,0:T(8,128)(2,1)S(1)}, u32[]{:S(2)}, u32[]{:S(2)}) collective-permute-start(bf16[8,64,128]{2,1,0:T(8,128)(2,1)S(1)} %constant_dynamic-update-slice_fusion), channel_id=1, source_target_pairs={{0,8},{1,9},{2,10},{3,11},{4,12},{5,13},{6,14},{7,15},{8,0},{9,1},... | collective-permute-start | bytes 393224 | tf_op jit(solution)/shard_map/summary_round/ppermute | solution.py:311
  21.1 16.0 %collective-permute-done.6 = bf16[8,64,128]{2,1,0:T(8,128)(2,1)S(1)} collective-permute-done((bf16[8,64,128]{2,1,0:T(8,128)(2,1)S(1)}, bf16[8,64,128]{2,1,0:T(8,128)(2,1)S(1)}, u32[]{:S(2)}, u32[]{:S(2)}) %collective-permute-start.6) | collective-permute-done | bytes 131104 | tf_op jit(solution)/shard_map/summary_round/ppermute | solution.py:311
  37.2 2.0 %collective-permute-start.16 = (bf16[128,2048]{1,0:T(8,128)(2,1)}, bf16[128,2048]{1,0:T(8,128)(2,1)S(1)}, u32[]{:S(2)}, u32[]{:S(2)}) collective-permute-start(bf16[128,2048]{1,0:T(8,128)(2,1)} %collective-permute-done.12.refs_8_), channel_id=1, source_target_pairs={{0,2},{1,3},{4,0},{5,1},{8,4},{9,5},{12,8},{13,9},{14,12},{15,13},... | collective-permute-start | bytes 1572872 | tf_op jit(solution)/shard_map/weight_3_down/ppermute | solution.py:285
  40.5 6.4 %collective-permute-done.14.refs_10_ = bf16[128,2048]{1,0:T(8,128)(2,1)S(1)} collective-permute-done((bf16[128,2048]{1,0:T(8,128)(2,1)S(1)}, bf16[128,2048]{1,0:T(8,128)(2,1)S(1)}, u32[]{:S(2)}, u32[]{:S(2)}) %collective-permute-start.14) | collective-permute-done | bytes 524320 | tf_op jit(solution)/shard_map/weight_3_up/ppermute | solution.py:285
  46.9 1.0 copy-done.4
  49.8 2.1 %attention.1.tokens = bf16[128,2048]{1,0:T(8,128)(2,1)S(1)} custom-call(s32[2]{0:T(128)S(1)} %pad_add_fusion.me, bf16[128,2048]{1,0:T(8,128)(2,1)S(1)} %copy-done.4, bf16[128,512]{1,0:T(8,128)(2,1)S(1)} %copy-done.6, bf16[128,512]{1,0:T(8,128)(2,1)S(1)} %copy-done.8, bf16[16,32,128]{2,1,0:T(8,128)(2,1)S(1)} %get-tuple-element.79.gathered), custom_call_target="tpu_custom_call" | custom-call | flops 268435456 | bytes 2097152 | tf_op jit(solution)/shard_map/attention/pallas_call | solution.py:117
  53.1 1.4 collective-permute-start.19
  55.5 3.1 %project_first.1.acc = f32[128,2048]{1,0:T(8,128)S(1)} custom-call(s32[25]{0:T(128)S(1)} %dynamic-slice_bitcast_fusion.here, bf16[128,2048]{1,0:T(8,128)(2,1)S(1)} %attention.1.tokens, bf16[128,2048]{1,0:T(8,128)(2,1)S(1)} %copy-done.3, bf16[128,2048]{1,0:T(8,128)(2,1)} %collective-permute-done.7.refs_1_, ...), custom_call_target="tpu_custom_call" | custom-call | flops 939524096 | bytes 7340032 | tf_op jit(solution)/shard_map/project_first/pallas_call | solution.py:173
  58.7 2.8 %collective-permute-done.19.b = bf16[64,2048]{1,0:T(8,128)(2,1)S(1)} collective-permute-done((bf16[64,2048]{1,0:T(8,128)(2,1)S(1)}, bf16[64,2048]{1,0:T(8,128)(2,1)S(1)}, u32[]{:S(2)}, u32[]{:S(2)}) %collective-permute-start.19) | collective-permute-done | bytes 262176 | tf_op jit(solution)/shard_map/weight_far_down/ppermute | solution.py:285
  61.5 1.0 collective-permute-done.18.a
  63.0 1.0 collective-permute-done.20.c
  64.0 1.7 project_last.1
  65.9 1.0 collective-permute-start.25
  66.9 1.1 collective-permute-start.24
  68.0 3.2 %experts.5 = (bf16[128,2048]{1,0:T(8,128)(2,1)S(1)}, bf16[128,2048]{1,0:T(8,128)(2,1)S(1)}) custom-call(s32[25]{0:T(128)S(1)} %dynamic-slice_bitcast_fusion.here, f32[16,128]{1,0:T(8,128)S(1)} %fusion.table, bf16[128,2048]{1,0:T(8,128)(2,1)S(1)} %get-tuple-element.48.refs_0_, bf16[128,2048]{1,0:T(8,128)(2,1)S(1)} %collective-permute-done.22.refs_1_, ...), custom_call_target="tpu_custom_call" | custom-call | tf_op jit(solution)/shard_map/experts/pallas_call | solution.py:256
  71.2 8.9 %collective-permute-done.25.refs_1_ = bf16[128,2048]{1,0:T(8,128)(2,1)S(1)} collective-permute-done((bf16[128,2048]{1,0:T(8,128)(2,1)S(1)}, bf16[128,2048]{1,0:T(8,128)(2,1)S(1)}, u32[]{:S(2)}, u32[]{:S(2)}) %collective-permute-start.25) | collective-permute-done | bytes 524320 | tf_op jit(solution)/shard_map/token_1_down/ppermute | solution.py:285
  80.8 1.7 collective-permute-start.29
  82.8 5.6 %experts.6 = (bf16[128,2048]{1,0:T(8,128)(2,1)S(1)}, bf16[128,2048]{1,0:T(8,128)(2,1)S(1)}, bf16[256,2048]{1,0:T(8,128)(2,1)S(1)}) custom-call(s32[25]{0:T(128)S(1)} %dynamic-slice_bitcast_fusion.here, f32[16,128]{1,0:T(8,128)S(1)} %fusion.table, bf16[128,2048]{1,0:T(8,128)(2,1)S(1)} %collective-permute-done.24.refs_0_, ...), custom_call_target="tpu_custom_call" | custom-call | tf_op jit(solution)/shard_map/experts/pallas_call | solution.py:256
  88.5 6.7 %collective-permute-done.29.refs_1_ = bf16[128,2048]{1,0:T(8,128)(2,1)S(1)} collective-permute-done((bf16[128,2048]{1,0:T(8,128)(2,1)S(1)}, bf16[128,2048]{1,0:T(8,128)(2,1)S(1)}, u32[]{:S(2)}, u32[]{:S(2)}) %collective-permute-start.29) | collective-permute-done | bytes 524320 | tf_op jit(solution)/shard_map/token_2_down/ppermute | solution.py:285
  95.1 1.5 collective-permute-done.28.refs_0_
  96.6 1.7 collective-permute-start.33
  98.6 5.6 %experts.7 = (bf16[128,2048]{1,0:T(8,128)(2,1)S(1)}, bf16[128,2048]{1,0:T(8,128)(2,1)S(1)}, bf16[256,2048]{1,0:T(8,128)(2,1)S(1)}) custom-call(s32[25]{0:T(128)S(1)} %dynamic-slice_bitcast_fusion.here, f32[16,128]{1,0:T(8,128)S(1)} %fusion.table, bf16[128,2048]{1,0:T(8,128)(2,1)S(1)} %collective-permute-done.28.refs_0_, ...), custom_call_target="tpu_custom_call" | custom-call | tf_op jit(solution)/shard_map/experts/pallas_call | solution.py:256
  104.8 6.1 %collective-permute-done.33.refs_1_ = bf16[128,2048]{1,0:T(8,128)(2,1)S(1)} collective-permute-done((bf16[128,2048]{1,0:T(8,128)(2,1)S(1)}, bf16[128,2048]{1,0:T(8,128)(2,1)S(1)}, u32[]{:S(2)}, u32[]{:S(2)}) %collective-permute-start.33) | collective-permute-done | bytes 524320 | tf_op jit(solution)/shard_map/token_3_down/ppermute | solution.py:285
  110.9 1.5 collective-permute-done.32.refs_0_
  112.9 1.6 collective-permute-start.39
  115.1 5.6 %experts.8 = (bf16[128,2048]{1,0:T(8,128)(2,1)S(1)}, bf16[128,2048]{1,0:T(8,128)(2,1)S(1)}, bf16[256,2048]{1,0:T(8,128)(2,1)S(1)}) custom-call(s32[25]{0:T(128)S(1)} %dynamic-slice_bitcast_fusion.here, f32[16,128]{1,0:T(8,128)S(1)} %fusion.table, bf16[128,2048]{1,0:T(8,128)(2,1)S(1)} %collective-permute-done.32.refs_0_, ...), custom_call_target="tpu_custom_call" | custom-call | tf_op jit(solution)/shard_map/experts/pallas_call | solution.py:256
  121.2 1.5 collective-permute-done.36
  122.9 1.9 %collective-permute-done.40.refs_1_ = bf16[128,2048]{1,0:T(8,128)(2,1)S(1)} collective-permute-done((bf16[128,2048]{1,0:T(8,128)(2,1)S(1)}, bf16[128,2048]{1,0:T(8,128)(2,1)S(1)}, u32[]{:S(2)}, u32[]{:S(2)}) %collective-permute-start.40) | collective-permute-done | bytes 524320 | tf_op jit(solution)/shard_map/swap_cores/ppermute | solution.py:290
  124.8 3.2 %experts.9 = (bf16[128,2048]{1,0:T(8,128)(2,1)S(1)}, bf16[128,2048]{1,0:T(8,128)(2,1)S(1)}) custom-call(s32[25]{0:T(128)S(1)} %dynamic-slice_bitcast_fusion.here, f32[16,128]{1,0:T(8,128)S(1)} %fusion.table, bf16[128,2048]{1,0:T(8,128)(2,1)S(1)} %constant_dynamic-update-slice_fusion.7.refs_0_, bf16[128,2048]{1,0:T(8,128)(2,1)S(1)} %collective-permute-done.40.refs_1_, ...), custom_call_target="tpu_custom_call" | custom-call | tf_op jit(solution)/shard_map/experts/pallas_call | solution.py:256
  128.5 1.4 collective-permute-done.41
  130.5 1.7 collective-permute-start.44
  132.2 6.3 %collective-permute-done.43 = bf16[64,2048]{1,0:T(8,128)(2,1)S(1)} collective-permute-done((bf16[64,2048]{1,0:T(8,128)(2,1)S(1)}, bf16[64,2048]{1,0:T(8,128)(2,1)S(1)}, u32[]{:S(2)}, u32[]{:S(2)}) %collective-permute-start.43) | collective-permute-done | bytes 262176 | tf_op jit(solution)/shard_map/sum_far_up/ppermute | solution.py:285
  139.2 1.8 collective-permute-start.46
  141.0 10.9 %collective-permute-done.45 = bf16[128,2048]{1,0:T(8,128)(2,1)S(1)} collective-permute-done((bf16[128,2048]{1,0:T(8,128)(2,1)S(1)}, bf16[128,2048]{1,0:T(8,128)(2,1)S(1)}, u32[]{:S(2)}, u32[]{:S(2)}) %collective-permute-start.45) | collective-permute-done | bytes 524320 | tf_op jit(solution)/shard_map/sum_3_up/ppermute | solution.py:285
  152.7 1.8 collective-permute-start.49
  154.5 9.9 %collective-permute-done.47 = bf16[128,2048]{1,0:T(8,128)(2,1)S(1)} collective-permute-done((bf16[128,2048]{1,0:T(8,128)(2,1)S(1)}, bf16[128,2048]{1,0:T(8,128)(2,1)S(1)}, u32[]{:S(2)}, u32[]{:S(2)}) %collective-permute-start.47) | collective-permute-done | bytes 524320 | tf_op jit(solution)/shard_map/sum_2_up/ppermute | solution.py:285
  165.0 1.8 collective-permute-start.50
  167.0 9.2 %collective-permute-done.50 = bf16[128,2048]{1,0:T(8,128)(2,1)S(1)} collective-permute-done((bf16[128,2048]{1,0:T(8,128)(2,1)S(1)}, bf16[128,2048]{1,0:T(8,128)(2,1)S(1)}, u32[]{:S(2)}, u32[]{:S(2)}) %collective-permute-start.50) | collective-permute-done | bytes 524320 | tf_op jit(solution)/shard_map/sum_1_down/ppermute | solution.py:285
  176.2 1.2 collective-permute-done.48
  177.5 1.2 add_convert_fusion
  (120 shorter events, 16.5 us)
Async XLA Ops:
  0.6 15.5 %collective-permute-start.4 = (bf16[128,2048]{1,0:T(8,128)(2,1)}, bf16[128,2048]{1,0:T(8,128)(2,1)S(1)}, u32[]{:S(2)}, u32[]{:S(2)}) collective-permute-start(bf16[128,2048]{1,0:T(8,128)(2,1)} %refs_0_.1), channel_id=1, source_target_pairs={{0,4},{1,5},{4,8},{5,9},{8,12},{9,13},{12,14},{13,15},{14,10},{15,... | collective-permute-start | bytes 1572872 | tf_op jit(solution)/shard_map/weight_1_up/ppermute | solution.py:285
  3.7 14.7 %collective-permute-start.5 = (bf16[128,2048]{1,0:T(8,128)(2,1)}, bf16[128,2048]{1,0:T(8,128)(2,1)S(1)}, u32[]{:S(2)}, u32[]{:S(2)}) collective-permute-start(bf16[128,2048]{1,0:T(8,128)(2,1)} %refs_0_.1), channel_id=1, source_target_pairs={{0,2},{1,3},{4,0},{5,1},{8,4},{9,5},{12,8},{13,9},{14,12},{15,13},... | collective-permute-start | bytes 1572872 | tf_op jit(solution)/shard_map/weight_1_down/ppermute | solution.py:285
  9.7 8.6 %collective-permute-start.1 = (bf16[2,64,128]{2,1,0:T(8,128)(2,1)S(1)}, bf16[2,64,128]{2,1,0:T(8,128)(2,1)S(1)}, u32[]{:S(2)}, u32[]{:S(2)}) collective-permute-start(bf16[2,64,128]{2,1,0:T(8,128)(2,1)S(1)} %pad_maximum_fusion), channel_id=1, source_target_pairs={{0,2},{1,3},{2,0},{3,1},{4,6},{5,7},{6,4},{7,5},{8,10},{9,11},{10,... | collective-permute-start | bytes 98312 | tf_op jit(solution)/shard_map/summary_round/ppermute | solution.py:311
  11.7 6.7 %collective-permute-start.2 = (bf16[2,64,128]{2,1,0:T(8,128)(2,1)S(1)}, bf16[2,64,128]{2,1,0:T(8,128)(2,1)S(1)}, u32[]{:S(2)}, u32[]{:S(2)}) collective-permute-start(bf16[2,64,128]{2,1,0:T(8,128)(2,1)S(1)} %pad_maximum_fusion), channel_id=1, source_target_pairs={{0,4},{1,5},{2,6},{3,7},{4,0},{5,1},{6,2},{7,3},{8,12},{9,13},{10,... | collective-permute-start | bytes 98312 | tf_op jit(solution)/shard_map/summary_round/ppermute | solution.py:311
  13.3 5.5 %collective-permute-start.3 = (bf16[2,64,128]{2,1,0:T(8,128)(2,1)S(1)}, bf16[2,64,128]{2,1,0:T(8,128)(2,1)S(1)}, u32[]{:S(2)}, u32[]{:S(2)}) collective-permute-start(bf16[2,64,128]{2,1,0:T(8,128)(2,1)S(1)} %pad_maximum_fusion), channel_id=1, source_target_pairs={{0,6},{1,7},{2,4},{3,5},{4,2},{5,3},{6,0},{7,1},{8,14},{9,15},{10,... | collective-permute-start | bytes 98312 | tf_op jit(solution)/shard_map/summary_round/ppermute | solution.py:311
  16.2 21.0 %collective-permute-start.10 = (bf16[128,2048]{1,0:T(8,128)(2,1)S(1)}, bf16[128,2048]{1,0:T(8,128)(2,1)S(1)}, u32[]{:S(2)}, u32[]{:S(2)}) collective-permute-start(bf16[128,2048]{1,0:T(8,128)(2,1)S(1)} %collective-permute-done.4.refs_2_), channel_id=1, source_target_pairs={{0,4},{1,5},{4,8},{5,9},{8,12},{9,13},{12,14},{13,15},{14,10},{15,... | collective-permute-start | bytes 1572872 | tf_op jit(solution)/shard_map/weight_2_up/ppermute | solution.py:285
  18.4 18.8 %collective-permute-start.12 = (bf16[128,2048]{1,0:T(8,128)(2,1)S(1)}, bf16[128,2048]{1,0:T(8,128)(2,1)}, u32[]{:S(2)}, u32[]{:S(2)}) collective-permute-start(bf16[128,2048]{1,0:T(8,128)(2,1)S(1)} %collective-permute-done.5.refs_4_), channel_id=1, source_target_pairs={{0,2},{1,3},{4,0},{5,1},{8,4},{9,5},{12,8},{13,9},{14,12},{15,13},... | collective-permute-start | bytes 1572872 | tf_op jit(solution)/shard_map/weight_2_down/ppermute | solution.py:285
  18.7 18.4 %collective-permute-start.6 = (bf16[8,64,128]{2,1,0:T(8,128)(2,1)S(1)}, bf16[8,64,128]{2,1,0:T(8,128)(2,1)S(1)}, u32[]{:S(2)}, u32[]{:S(2)}) collective-permute-start(bf16[8,64,128]{2,1,0:T(8,128)(2,1)S(1)} %constant_dynamic-update-slice_fusion), channel_id=1, source_target_pairs={{0,8},{1,9},{2,10},{3,11},{4,12},{5,13},{6,14},{7,15},{8,0},{9,1},... | collective-permute-start | bytes 393224 | tf_op jit(solution)/shard_map/summary_round/ppermute | solution.py:311
  37.2 9.7 %collective-permute-start.14 = (bf16[128,2048]{1,0:T(8,128)(2,1)S(1)}, bf16[128,2048]{1,0:T(8,128)(2,1)S(1)}, u32[]{:S(2)}, u32[]{:S(2)}) collective-permute-start(bf16[128,2048]{1,0:T(8,128)(2,1)S(1)} %collective-permute-done.10.refs_6_), channel_id=1, source_target_pairs={{0,4},{1,5},{4,8},{5,9},{8,12},{9,13},{12,14},{13,15},{14,10},{15,... | collective-permute-start | bytes 1572872 | tf_op jit(solution)/shard_map/weight_3_up/ppermute | solution.py:285
  37.2 14.7 %collective-permute-start.16 = (bf16[128,2048]{1,0:T(8,128)(2,1)}, bf16[128,2048]{1,0:T(8,128)(2,1)S(1)}, u32[]{:S(2)}, u32[]{:S(2)}) collective-permute-start(bf16[128,2048]{1,0:T(8,128)(2,1)} %collective-permute-done.12.refs_8_), channel_id=1, source_target_pairs={{0,2},{1,3},{4,0},{5,1},{8,4},{9,5},{12,8},{13,9},{14,12},{15,13},... | collective-permute-start | bytes 1572872 | tf_op jit(solution)/shard_map/weight_3_down/ppermute | solution.py:285
  39.2 13.2 %collective-permute-start.7 = (bf16[128,2048]{1,0:T(8,128)(2,1)}, bf16[128,2048]{1,0:T(8,128)(2,1)}, u32[]{:S(2)}, u32[]{:S(2)}) collective-permute-start(bf16[128,2048]{1,0:T(8,128)(2,1)} %refs_0_.1), channel_id=1, source_target_pairs={{0,1},{1,0},{2,3},{3,2},{4,5},{5,4},{6,7},{7,6},{8,9},{9,8},{10,11... | collective-permute-start | bytes 1572872 | tf_op jit(solution)/shard_map/swap_cores/ppermute | solution.py:290
  39.2 13.3 %collective-permute-start.8 = (bf16[128,2048]{1,0:T(8,128)(2,1)S(1)}, bf16[128,2048]{1,0:T(8,128)(2,1)}, u32[]{:S(2)}, u32[]{:S(2)}) collective-permute-start(bf16[128,2048]{1,0:T(8,128)(2,1)S(1)} %collective-permute-done.4.refs_2_), channel_id=1, source_target_pairs={{0,1},{1,0},{2,3},{3,2},{4,5},{5,4},{6,7},{7,6},{8,9},{9,8},{10,11... | collective-permute-start | bytes 1572872 | tf_op jit(solution)/shard_map/swap_cores/ppermute | solution.py:290
  40.5 12.6 %collective-permute-start.9 = (bf16[128,2048]{1,0:T(8,128)(2,1)S(1)}, bf16[128,2048]{1,0:T(8,128)(2,1)S(1)}, u32[]{:S(2)}, u32[]{:S(2)}) collective-permute-start(bf16[128,2048]{1,0:T(8,128)(2,1)S(1)} %collective-permute-done.5.refs_4_), channel_id=1, source_target_pairs={{0,1},{1,0},{2,3},{3,2},{4,5},{5,4},{6,7},{7,6},{8,9},{9,8},{10,11... | collective-permute-start | bytes 1572872 | tf_op jit(solution)/shard_map/swap_cores/ppermute | solution.py:290
  46.9 7.6 %collective-permute-start.11 = (bf16[128,2048]{1,0:T(8,128)(2,1)S(1)}, bf16[128,2048]{1,0:T(8,128)(2,1)S(1)}, u32[]{:S(2)}, u32[]{:S(2)}) collective-permute-start(bf16[128,2048]{1,0:T(8,128)(2,1)S(1)} %collective-permute-done.10.refs_6_), channel_id=1, source_target_pairs={{0,1},{1,0},{2,3},{3,2},{4,5},{5,4},{6,7},{7,6},{8,9},{9,8},{10,11... | collective-permute-start | bytes 1572872 | tf_op jit(solution)/shard_map/swap_cores/ppermute | solution.py:290
  51.9 3.3 %collective-permute-start.13 = (bf16[128,2048]{1,0:T(8,128)(2,1)}, bf16[128,2048]{1,0:T(8,128)(2,1)S(1)}, u32[]{:S(2)}, u32[]{:S(2)}) collective-permute-start(bf16[128,2048]{1,0:T(8,128)(2,1)} %collective-permute-done.12.refs_8_), channel_id=1, source_target_pairs={{0,1},{1,0},{2,3},{3,2},{4,5},{5,4},{6,7},{7,6},{8,9},{9,8},{10,11... | collective-permute-start | bytes 1572872 | tf_op jit(solution)/shard_map/swap_cores/ppermute | solution.py:290
  52.5 2.7 %collective-permute-start.15 = (bf16[128,2048]{1,0:T(8,128)(2,1)S(1)}, bf16[128,2048]{1,0:T(8,128)(2,1)S(1)}, u32[]{:S(2)}, u32[]{:S(2)}) collective-permute-start(bf16[128,2048]{1,0:T(8,128)(2,1)S(1)} %collective-permute-done.14.refs_10_), channel_id=1, source_target_pairs={{0,1},{1,0},{2,3},{3,2},{4,5},{5,4},{6,7},{7,6},{8,9},{9,8},{10,11... | collective-permute-start | bytes 1572872 | tf_op jit(solution)/shard_map/swap_cores/ppermute | solution.py:290
  52.6 2.9 %collective-permute-start.17 = (bf16[128,2048]{1,0:T(8,128)(2,1)S(1)}, bf16[128,2048]{1,0:T(8,128)(2,1)S(1)}, u32[]{:S(2)}, u32[]{:S(2)}) collective-permute-start(bf16[128,2048]{1,0:T(8,128)(2,1)S(1)} %collective-permute-done.16.refs_12_), channel_id=1, source_target_pairs={{0,1},{1,0},{2,3},{3,2},{4,5},{5,4},{6,7},{7,6},{8,9},{9,8},{10,11... | collective-permute-start | bytes 1572872 | tf_op jit(solution)/shard_map/swap_cores/ppermute | solution.py:290
  53.1 8.3 %collective-permute-start.19 = (bf16[64,2048]{1,0:T(8,128)(2,1)S(1)}, bf16[64,2048]{1,0:T(8,128)(2,1)S(1)}, u32[]{:S(2)}, u32[]{:S(2)}) collective-permute-start(bf16[64,2048]{1,0:T(8,128)(2,1)S(1)} %slice.53), channel_id=1, source_target_pairs={{0,2},{1,3},{4,0},{5,1},{8,4},{9,5},{12,8},{13,9},{14,12},{15,13},... | collective-permute-start | bytes 786440 | tf_op jit(solution)/shard_map/weight_far_down/ppermute | solution.py:285
  54.5 8.0 %collective-permute-start.18 = (bf16[64,2048]{1,0:T(8,128)(2,1)S(1)}, bf16[64,2048]{1,0:T(8,128)(2,1)S(1)}, u32[]{:S(2)}, u32[]{:S(2)}) collective-permute-start(bf16[64,2048]{1,0:T(8,128)(2,1)S(1)} %slice.49), channel_id=1, source_target_pairs={{0,4},{1,5},{4,8},{5,9},{8,12},{9,13},{12,14},{13,15},{14,10},{15,... | collective-permute-start | bytes 786440 | tf_op jit(solution)/shard_map/weight_far_up/ppermute | solution.py:285
  65.8 2.2 %collective-permute-start.22 = (bf16[128,2048]{1,0:T(8,128)(2,1)S(1)}, bf16[128,2048]{1,0:T(8,128)(2,1)S(1)}, u32[]{:S(2)}, u32[]{:S(2)}) collective-permute-start(bf16[128,2048]{1,0:T(8,128)(2,1)S(1)} %get-tuple-element.48.refs_0_), channel_id=1, source_target_pairs={{0,1},{1,0},{2,3},{3,2},{4,5},{5,4},{6,7},{7,6},{8,9},{9,8},{10,11... | collective-permute-start | bytes 1572872 | tf_op jit(solution)/shard_map/swap_cores/ppermute | solution.py:290
  65.9 14.2 %collective-permute-start.25 = (bf16[128,2048]{1,0:T(8,128)(2,1)S(1)}, bf16[128,2048]{1,0:T(8,128)(2,1)S(1)}, u32[]{:S(2)}, u32[]{:S(2)}) collective-permute-start(bf16[128,2048]{1,0:T(8,128)(2,1)S(1)} %get-tuple-element.48.refs_0_), channel_id=1, source_target_pairs={{0,2},{1,3},{4,0},{5,1},{8,4},{9,5},{12,8},{13,9},{14,12},{15,13},... | collective-permute-start | bytes 1572872 | tf_op jit(solution)/shard_map/token_1_down/ppermute | solution.py:285
  66.9 13.9 %collective-permute-start.24 = (bf16[128,2048]{1,0:T(8,128)(2,1)S(1)}, bf16[128,2048]{1,0:T(8,128)(2,1)S(1)}, u32[]{:S(2)}, u32[]{:S(2)}) collective-permute-start(bf16[128,2048]{1,0:T(8,128)(2,1)S(1)} %get-tuple-element.48.refs_0_), channel_id=1, source_target_pairs={{0,4},{1,5},{4,8},{5,9},{8,12},{9,13},{12,14},{13,15},{14,10},{15,... | collective-permute-start | bytes 1572872 | tf_op jit(solution)/shard_map/token_1_up/ppermute | solution.py:285
  80.1 2.7 %collective-permute-start.27 = (bf16[128,2048]{1,0:T(8,128)(2,1)S(1)}, bf16[128,2048]{1,0:T(8,128)(2,1)S(1)}, u32[]{:S(2)}, u32[]{:S(2)}) collective-permute-start(bf16[128,2048]{1,0:T(8,128)(2,1)S(1)} %collective-permute-done.25.refs_1_), channel_id=1, source_target_pairs={{0,1},{1,0},{2,3},{3,2},{4,5},{5,4},{6,7},{7,6},{8,9},{9,8},{10,11... | collective-permute-start | bytes 1572872 | tf_op jit(solution)/shard_map/swap_cores/ppermute | solution.py:290
  80.8 2.0 %collective-permute-start.26 = (bf16[128,2048]{1,0:T(8,128)(2,1)S(1)}, bf16[128,2048]{1,0:T(8,128)(2,1)S(1)}, u32[]{:S(2)}, u32[]{:S(2)}) collective-permute-start(bf16[128,2048]{1,0:T(8,128)(2,1)S(1)} %collective-permute-done.24.refs_0_), channel_id=1, source_target_pairs={{0,1},{1,0},{2,3},{3,2},{4,5},{5,4},{6,7},{7,6},{8,9},{9,8},{10,11... | collective-permute-start | bytes 1572872 | tf_op jit(solution)/shard_map/swap_cores/ppermute | solution.py:290
  80.8 14.3 %collective-permute-start.29 = (bf16[128,2048]{1,0:T(8,128)(2,1)S(1)}, bf16[128,2048]{1,0:T(8,128)(2,1)S(1)}, u32[]{:S(2)}, u32[]{:S(2)}) collective-permute-start(bf16[128,2048]{1,0:T(8,128)(2,1)S(1)} %collective-permute-done.25.refs_1_), channel_id=1, source_target_pairs={{0,2},{1,3},{4,0},{5,1},{8,4},{9,5},{12,8},{13,9},{14,12},{15,13},... | collective-permute-start | bytes 1572872 | tf_op jit(solution)/shard_map/token_2_down/ppermute | solution.py:285
  82.5 14.1 %collective-permute-start.28 = (bf16[128,2048]{1,0:T(8,128)(2,1)S(1)}, bf16[128,2048]{1,0:T(8,128)(2,1)S(1)}, u32[]{:S(2)}, u32[]{:S(2)}) collective-permute-start(bf16[128,2048]{1,0:T(8,128)(2,1)S(1)} %collective-permute-done.24.refs_0_), channel_id=1, source_target_pairs={{0,4},{1,5},{4,8},{5,9},{8,12},{9,13},{12,14},{13,15},{14,10},{15,... | collective-permute-start | bytes 1572872 | tf_op jit(solution)/shard_map/token_2_up/ppermute | solution.py:285
  95.1 3.5 %collective-permute-start.31 = (bf16[128,2048]{1,0:T(8,128)(2,1)S(1)}, bf16[128,2048]{1,0:T(8,128)(2,1)S(1)}, u32[]{:S(2)}, u32[]{:S(2)}) collective-permute-start(bf16[128,2048]{1,0:T(8,128)(2,1)S(1)} %collective-permute-done.29.refs_1_), channel_id=1, source_target_pairs={{0,1},{1,0},{2,3},{3,2},{4,5},{5,4},{6,7},{7,6},{8,9},{9,8},{10,11... | collective-permute-start | bytes 1572872 | tf_op jit(solution)/shard_map/swap_cores/ppermute | solution.py:290
  96.6 2.0 %collective-permute-start.30 = (bf16[128,2048]{1,0:T(8,128)(2,1)S(1)}, bf16[128,2048]{1,0:T(8,128)(2,1)S(1)}, u32[]{:S(2)}, u32[]{:S(2)}) collective-permute-start(bf16[128,2048]{1,0:T(8,128)(2,1)S(1)} %collective-permute-done.28.refs_0_), channel_id=1, source_target_pairs={{0,1},{1,0},{2,3},{3,2},{4,5},{5,4},{6,7},{7,6},{8,9},{9,8},{10,11... | collective-permute-start | bytes 1572872 | tf_op jit(solution)/shard_map/swap_cores/ppermute | solution.py:290
  96.6 14.3 %collective-permute-start.33 = (bf16[128,2048]{1,0:T(8,128)(2,1)S(1)}, bf16[128,2048]{1,0:T(8,128)(2,1)S(1)}, u32[]{:S(2)}, u32[]{:S(2)}) collective-permute-start(bf16[128,2048]{1,0:T(8,128)(2,1)S(1)} %collective-permute-done.29.refs_1_), channel_id=1, source_target_pairs={{0,2},{1,3},{4,0},{5,1},{8,4},{9,5},{12,8},{13,9},{14,12},{15,13},... | collective-permute-start | bytes 1572872 | tf_op jit(solution)/shard_map/token_3_down/ppermute | solution.py:285
  98.3 14.1 %collective-permute-start.32 = (bf16[128,2048]{1,0:T(8,128)(2,1)S(1)}, bf16[128,2048]{1,0:T(8,128)(2,1)S(1)}, u32[]{:S(2)}, u32[]{:S(2)}) collective-permute-start(bf16[128,2048]{1,0:T(8,128)(2,1)S(1)} %collective-permute-done.28.refs_0_), channel_id=1, source_target_pairs={{0,4},{1,5},{4,8},{5,9},{8,12},{9,13},{12,14},{13,15},{14,10},{15,... | collective-permute-start | bytes 1572872 | tf_op jit(solution)/shard_map/token_3_up/ppermute | solution.py:285
  98.6 22.6 %collective-permute-start.37 = (bf16[256,2048]{1,0:T(8,128)(2,1)S(1)}, bf16[256,2048]{1,0:T(8,128)(2,1)S(1)}, u32[]{:S(2)}, u32[]{:S(2)}) collective-permute-start(bf16[256,2048]{1,0:T(8,128)(2,1)S(1)} %get-tuple-element.63), channel_id=1, source_target_pairs={{0,1},{1,0},{2,3},{3,2},{4,5},{5,4},{6,7},{7,6},{8,9},{9,8},{10,11... | collective-permute-start | bytes 3145736 | tf_op jit(solution)/shard_map/swap_cores/ppermute | solution.py:290
  104.3 16.9 %collective-permute-start.38 = (bf16[256,2048]{1,0:T(8,128)(2,1)S(1)}, bf16[256,2048]{1,0:T(8,128)(2,1)S(1)}, u32[]{:S(2)}, u32[]{:S(2)}) collective-permute-start(bf16[256,2048]{1,0:T(8,128)(2,1)S(1)} %get-tuple-element.64), channel_id=1, source_target_pairs={{0,1},{1,0},{2,3},{3,2},{4,5},{5,4},{6,7},{7,6},{8,9},{9,8},{10,11... | collective-permute-start | bytes 3145736 | tf_op jit(solution)/shard_map/swap_cores/ppermute | solution.py:290
  110.9 2.0 %collective-permute-start.35 = (bf16[128,2048]{1,0:T(8,128)(2,1)S(1)}, bf16[128,2048]{1,0:T(8,128)(2,1)S(1)}, u32[]{:S(2)}, u32[]{:S(2)}) collective-permute-start(bf16[128,2048]{1,0:T(8,128)(2,1)S(1)} %collective-permute-done.33.refs_1_), channel_id=1, source_target_pairs={{0,1},{1,0},{2,3},{3,2},{4,5},{5,4},{6,7},{7,6},{8,9},{9,8},{10,11... | collective-permute-start | bytes 1572872 | tf_op jit(solution)/shard_map/swap_cores/ppermute | solution.py:290
  112.4 2.2 %collective-permute-start.34 = (bf16[128,2048]{1,0:T(8,128)(2,1)S(1)}, bf16[128,2048]{1,0:T(8,128)(2,1)S(1)}, u32[]{:S(2)}, u32[]{:S(2)}) collective-permute-start(bf16[128,2048]{1,0:T(8,128)(2,1)S(1)} %collective-permute-done.32.refs_0_), channel_id=1, source_target_pairs={{0,1},{1,0},{2,3},{3,2},{4,5},{5,4},{6,7},{7,6},{8,9},{9,8},{10,11... | collective-permute-start | bytes 1572872 | tf_op jit(solution)/shard_map/swap_cores/ppermute | solution.py:290
  112.4 8.3 %collective-permute-start.23 = (bf16[128,2048]{1,0:T(8,128)(2,1)S(1)}, bf16[128,2048]{1,0:T(8,128)(2,1)S(1)}, u32[]{:S(2)}, u32[]{:S(2)}) collective-permute-start(bf16[128,2048]{1,0:T(8,128)(2,1)S(1)} %get-tuple-element.50), channel_id=1, source_target_pairs={{0,1},{1,0},{2,3},{3,2},{4,5},{5,4},{6,7},{7,6},{8,9},{9,8},{10,11... | collective-permute-start | bytes 1572872 | tf_op jit(solution)/shard_map/swap_cores/ppermute | solution.py:290
  112.9 8.3 %collective-permute-start.39 = (bf16[64,2048]{1,0:T(8,128)(2,1)S(1)}, bf16[64,2048]{1,0:T(8,128)(2,1)S(1)}, u32[]{:S(2)}, u32[]{:S(2)}) collective-permute-start(bf16[64,2048]{1,0:T(8,128)(2,1)S(1)} %slice.55), channel_id=1, source_target_pairs={{0,2},{1,3},{4,0},{5,1},{8,4},{9,5},{12,8},{13,9},{14,12},{15,13},... | collective-permute-start | bytes 786440 | tf_op jit(solution)/shard_map/token_far_down/ppermute | solution.py:285
  114.6 8.1 %collective-permute-start.36 = (bf16[64,2048]{1,0:T(8,128)(2,1)S(1)}, bf16[64,2048]{1,0:T(8,128)(2,1)S(1)}, u32[]{:S(2)}, u32[]{:S(2)}) collective-permute-start(bf16[64,2048]{1,0:T(8,128)(2,1)S(1)} %slice.54), channel_id=1, source_target_pairs={{0,4},{1,5},{4,8},{5,9},{8,12},{9,13},{12,14},{13,15},{14,10},{15,... | collective-permute-start | bytes 786440 | tf_op jit(solution)/shard_map/token_far_up/ppermute | solution.py:285
  122.8 2.0 %collective-permute-start.40 = (bf16[128,2048]{1,0:T(8,128)(2,1)S(1)}, bf16[128,2048]{1,0:T(8,128)(2,1)S(1)}, u32[]{:S(2)}, u32[]{:S(2)}) collective-permute-start(bf16[128,2048]{1,0:T(8,128)(2,1)S(1)} %constant_dynamic-update-slice_fusion.7.refs_0_), channel_id=1, source_target_pairs={{0,1},{1,0},{2,3},{3,2},{4,5},{5,4},{6,7},{7,6},{8,9},{9,8},{10,11... | collective-permute-start | bytes 1572872 | tf_op jit(solution)/shard_map/swap_cores/ppermute | solution.py:290
  128.0 2.0 %collective-permute-start.41 = (bf16[128,2048]{1,0:T(8,128)(2,1)S(1)}, bf16[128,2048]{1,0:T(8,128)(2,1)S(1)}, u32[]{:S(2)}, u32[]{:S(2)}) collective-permute-start(bf16[128,2048]{1,0:T(8,128)(2,1)S(1)} %get-tuple-element.68), channel_id=1, source_target_pairs={{0,1},{1,0},{2,3},{3,2},{4,5},{5,4},{6,7},{7,6},{8,9},{9,8},{10,11... | collective-permute-start | bytes 1572872 | tf_op jit(solution)/shard_map/swap_cores/ppermute | solution.py:290
  128.2 4.0 %collective-permute-start.42 = (bf16[256,2048]{1,0:T(8,128)(2,1)S(1)}, bf16[256,2048]{1,0:T(8,128)(2,1)S(1)}, u32[]{:S(2)}, u32[]{:S(2)}) collective-permute-start(bf16[256,2048]{1,0:T(8,128)(2,1)S(1)} %get-tuple-element.70), channel_id=1, source_target_pairs={{0,1},{1,0},{2,3},{3,2},{4,5},{5,4},{6,7},{7,6},{8,9},{9,8},{10,11... | collective-permute-start | bytes 3145736 | tf_op jit(solution)/shard_map/swap_cores/ppermute | solution.py:290
  130.1 8.4 %collective-permute-start.43 = (bf16[64,2048]{1,0:T(8,128)(2,1)S(1)}, bf16[64,2048]{1,0:T(8,128)(2,1)S(1)}, u32[]{:S(2)}, u32[]{:S(2)}) collective-permute-start(bf16[64,2048]{1,0:T(8,128)(2,1)S(1)} %get-tuple-element.77), channel_id=1, source_target_pairs={{0,4},{1,5},{4,8},{5,9},{8,12},{9,13},{12,14},{13,15},{14,10},{15,... | collective-permute-start | bytes 786440 | tf_op jit(solution)/shard_map/sum_far_up/ppermute | solution.py:285
  130.5 8.6 %collective-permute-start.44 = (bf16[64,2048]{1,0:T(8,128)(2,1)S(1)}, bf16[64,2048]{1,0:T(8,128)(2,1)S(1)}, u32[]{:S(2)}, u32[]{:S(2)}) collective-permute-start(bf16[64,2048]{1,0:T(8,128)(2,1)S(1)} %get-tuple-element.76), channel_id=1, source_target_pairs={{0,2},{1,3},{4,0},{5,1},{8,4},{9,5},{12,8},{13,9},{14,12},{15,13},... | collective-permute-start | bytes 786440 | tf_op jit(solution)/shard_map/sum_far_down/ppermute | solution.py:285
  138.7 13.2 %collective-permute-start.45 = (bf16[128,2048]{1,0:T(8,128)(2,1)S(1)}, bf16[128,2048]{1,0:T(8,128)(2,1)S(1)}, u32[]{:S(2)}, u32[]{:S(2)}) collective-permute-start(bf16[128,2048]{1,0:T(8,128)(2,1)S(1)} %add_convert_fusion.6), channel_id=1, source_target_pairs={{0,4},{1,5},{4,8},{5,9},{8,12},{9,13},{12,14},{13,15},{14,10},{15,... | collective-permute-start | bytes 1572872 | tf_op jit(solution)/shard_map/sum_3_up/ppermute | solution.py:285
  139.2 13.2 %collective-permute-start.46 = (bf16[128,2048]{1,0:T(8,128)(2,1)S(1)}, bf16[128,2048]{1,0:T(8,128)(2,1)S(1)}, u32[]{:S(2)}, u32[]{:S(2)}) collective-permute-start(bf16[128,2048]{1,0:T(8,128)(2,1)S(1)} %add_convert_fusion.5), channel_id=1, source_target_pairs={{0,2},{1,3},{4,0},{5,1},{8,4},{9,5},{12,8},{13,9},{14,12},{15,13},... | collective-permute-start | bytes 1572872 | tf_op jit(solution)/shard_map/sum_3_down/ppermute | solution.py:285
  152.1 12.3 %collective-permute-start.47 = (bf16[128,2048]{1,0:T(8,128)(2,1)S(1)}, bf16[128,2048]{1,0:T(8,128)(2,1)S(1)}, u32[]{:S(2)}, u32[]{:S(2)}) collective-permute-start(bf16[128,2048]{1,0:T(8,128)(2,1)S(1)} %add_convert_fusion.4), channel_id=1, source_target_pairs={{0,4},{1,5},{4,8},{5,9},{8,12},{9,13},{12,14},{13,15},{14,10},{15,... | collective-permute-start | bytes 1572872 | tf_op jit(solution)/shard_map/sum_2_up/ppermute | solution.py:285
  152.7 12.0 %collective-permute-start.49 = (bf16[128,2048]{1,0:T(8,128)(2,1)S(1)}, bf16[128,2048]{1,0:T(8,128)(2,1)S(1)}, u32[]{:S(2)}, u32[]{:S(2)}) collective-permute-start(bf16[128,2048]{1,0:T(8,128)(2,1)S(1)} %add_convert_fusion.3), channel_id=1, source_target_pairs={{0,2},{1,3},{4,0},{5,1},{8,4},{9,5},{12,8},{13,9},{14,12},{15,13},... | collective-permute-start | bytes 1572872 | tf_op jit(solution)/shard_map/sum_2_down/ppermute | solution.py:285
  165.0 11.3 %collective-permute-start.50 = (bf16[128,2048]{1,0:T(8,128)(2,1)S(1)}, bf16[128,2048]{1,0:T(8,128)(2,1)S(1)}, u32[]{:S(2)}, u32[]{:S(2)}) collective-permute-start(bf16[128,2048]{1,0:T(8,128)(2,1)S(1)} %add_convert_fusion.1), channel_id=1, source_target_pairs={{0,2},{1,3},{4,0},{5,1},{8,4},{9,5},{12,8},{13,9},{14,12},{15,13},... | collective-permute-start | bytes 1572872 | tf_op jit(solution)/shard_map/sum_1_down/ppermute | solution.py:285
  166.7 10.7 %collective-permute-start.48 = (bf16[128,2048]{1,0:T(8,128)(2,1)S(1)}, bf16[128,2048]{1,0:T(8,128)(2,1)S(1)}, u32[]{:S(2)}, u32[]{:S(2)}) collective-permute-start(bf16[128,2048]{1,0:T(8,128)(2,1)S(1)} %add_convert_fusion.2), channel_id=1, source_target_pairs={{0,4},{1,5},{4,8},{5,9},{8,12},{9,13},{12,14},{13,15},{14,10},{15,... | collective-permute-start | bytes 1572872 | tf_op jit(solution)/shard_map/sum_1_up/ppermute | solution.py:285
  (17 other events, 112.6 us)

commit v4 on v3

--- a/solution.py
+++ b/solution.py
@@ -24,15 +24,43 @@
     return x * lax.rsqrt(jnp.mean(x * x, axis=-1, keepdims=True) + 1e-06)
 
 
-def params():
-    return pltpu.CompilerParams(vmem_limit_bytes=VMEM_BYTES)
-
-
-def whole(*shape):
-    return pl.BlockSpec(shape, lambda *_: (0,) * len(shape))
-
-
-def summary_kernel(experts, ids, keys, values, gain, routes, scores, out, rows):
+def params(size=VMEM_BYTES):
+    return pltpu.CompilerParams(vmem_limit_bytes=size)
+
+
+def smem():
+    return pl.BlockSpec(memory_space=pltpu.SMEM)
+
+
+def vmem():
+    return pl.BlockSpec(memory_space=pltpu.VMEM)
+
+
+def hbm():
+    return pl.BlockSpec(memory_space=pltpu.HBM)
+
+
+def load(sources, targets, arrived):
+    copies = [
+        pltpu.make_async_copy(source, target, arrived.at[i])
+        for i, (source, target) in enumerate(zip(sources, targets))
+    ]
+    for copy in copies:
+        copy.start()
+    for copy in copies:
+        copy.wait()
+
+
+def landing(arrays):
+    return [pltpu.VMEM(a.shape, a.dtype) for a in arrays] + [
+        pltpu.SemaphoreType.DMA((len(arrays),))
+    ]
+
+
+def summary_kernel(experts, *refs):
+    sources, out, rows = refs[:6], refs[6], refs[7]
+    ids, keys, values, gain, routes, scores, arrived = refs[8:]
+    load(sources, (ids, keys, values, gain, routes, scores), arrived)
     tokens = ids.shape[1]
     block = lax.broadcasted_iota(jnp.int32, (8, tokens), 0)
     member = (ids[...] == block) & (block < NB)
@@ -61,16 +89,22 @@
 def summarize(ids, keys, values, gain, routes, scores, experts):
     tokens = ids.shape[0]
     height = 8 * KVH + 2 * experts
+    arrays = (ids.reshape(1, tokens), keys, values, gain.reshape(1, HD), routes.T, scores.T)
     return pl.pallas_call(
         functools.partial(summary_kernel, experts),
+        in_specs=[hbm()] * 6,
+        out_specs=vmem(),
         out_shape=jax.ShapeDtypeStruct((height, HD), BF16),
-        scratch_shapes=[pltpu.VMEM((height, HD), F32)],
-        compiler_params=params(),
+        scratch_shapes=[pltpu.VMEM((height, HD), F32), *landing(arrays)],
+        compiler_params=params(60 * 1024 * 1024),
         name="summaries",
-    )(ids.reshape(1, tokens), keys, values, gain.reshape(1, HD), routes.T, scores.T)
-
-
-def attention_kernel(me, queries, keys, values, gathered, attended):
+    )(*arrays)
+
+
+def attention_kernel(me, owners, gathered, *refs):
+    sources, attended = refs[:3], refs[3]
+    queries, keys, values, arrived = refs[4:]
+    load(sources, (queries, keys, values), arrived)
     tokens = queries.shape[0]
     group = HQ // KVH
     scale = 1.0 / math.sqrt(HD)
@@ -80,8 +114,7 @@
     col = lax.broadcasted_iota(jnp.int32, (tokens, tokens), 1)
     causal = row >= col
     place = lax.broadcasted_iota(jnp.int32, (tokens, wide), 1)
-    owner = (place // (2 * NB)) ^ me[1]
-    earlier = (owner < me[0]) & (place % (2 * NB) < NB)
+    earlier = (owners[...] < me[0]) & (place % (2 * NB) < NB)
     seen = jnp.concatenate([causal, earlier], axis=1)
     for g in range(KVH):
         cols = slice(g * HD, (g + 1) * HD)
@@ -112,33 +145,23 @@
             ).astype(BF16)
 
 
-def attend(me, queries, keys, values, gathered):
+def attend(index, shards, queries, keys, values, gathered):
     tokens = queries.shape[0]
+    owners = jnp.repeat(shards, 2 * NB).reshape(1, -1)
     return pl.pallas_call(
         attention_kernel,
-        grid_spec=pltpu.PrefetchScalarGridSpec(
-            num_scalar_prefetch=1,
-            grid=(1,),
-            in_specs=[whole(*a.shape) for a in (queries, keys, values, gathered)],
-            out_specs=whole(tokens, HQ * HD),
-        ),
+        in_specs=[smem(), vmem(), vmem()] + [hbm()] * 3,
+        out_specs=vmem(),
         out_shape=jax.ShapeDtypeStruct((tokens, HQ * HD), BF16),
-        compiler_params=params(),
+        scratch_shapes=landing((queries, keys, values)),
+        compiler_params=params(56 * 1024 * 1024),
         cost_estimate=pl.CostEstimate(
             flops=4 * HQ * HD * tokens * 2 * tokens,
             bytes_accessed=2 * 4 * tokens * HQ * HD,
             transcendentals=HQ * tokens * 2 * tokens,
         ),
         name="attention",
-    )(me, queries, keys, values, gathered)
-
-
-def smem():
-    return pl.BlockSpec(memory_space=pltpu.SMEM)
-
-
-def vmem():
-    return pl.BlockSpec(memory_space=pltpu.VMEM)
+    )(index.reshape(1), owners, gathered, queries, keys, values)
 
 
 def pair_up(here, pair, own, other):
@@ -289,7 +312,7 @@
         with jax.named_scope("swap_cores"):
             return lax.ppermute(x, "ctx", [(i, i ^ 1) for i in range(n)])
 
-    def table(self, n):
+    def table(self, n, order):
         place = {chip: p for p, chip in enumerate(self.cycle)}
         rows = []
         for i in range(n):
@@ -298,19 +321,16 @@
             for k in range(1, self.far):
                 chips += [self.cycle[(p - k) % self.chips], self.cycle[(p + k) % self.chips]]
             chips.append(self.cycle[(p + self.far) % self.chips])
-            own = [(chip * CORES + core) ^ i for chip in chips]
-            other = [(chip * CORES + 1 - core) ^ i for chip in chips]
+            own = [order.index((chip * CORES + core) ^ i) for chip in chips]
+            other = [order.index((chip * CORES + 1 - core) ^ i) for chip in chips]
             rows.append([core, *chips, *own, *other])
         return rows
 
 
-def xor_round(x, count, n):
-    m = x.shape[0]
+def xor_round(x, order, masks, n):
     with jax.named_scope("summary_round"):
-        others = [
-            lax.ppermute(x, "ctx", [(i, i ^ (m * c)) for i in range(n)]) for c in range(1, count)
-        ]
-    return jnp.concatenate([x, *others], axis=0)
+        others = [lax.ppermute(x, "ctx", [(i, i ^ mask) for i in range(n)]) for mask in masks]
+    return jnp.concatenate([x, *others], axis=0), [o ^ m for m in (0, *masks) for o in order]
 
 
 def after(x, *earlier):
@@ -342,7 +362,6 @@
     index = lax.axis_index("ctx")
     core = index % CORES
     ring = Ring(n)
-    here = jnp.asarray(ring.table(n), jnp.int32)[index]
     half = queries.shape[0] // 2
 
     def both(pair, *earlier):
@@ -357,16 +376,17 @@
     pair = forward([out_weight, out_weight], "weight_1")
     blocks = [out_weight, ring.swap(out_weight)]
     small = summarize(block_ids, keys, values, summary_gain, routes, route_scores, n)[None]
-    small = xor_round(xor_round(small, 2, n), 4, n)
+    small, order = xor_round(small, [0], [1], n)
+    for bit in range(n.bit_length() - 2, 2, -1):
+        small, order = xor_round(small, order, [1 << bit], n)
     for k in range(1, ring.far):
         if k == 1:
             small = after(small, *pair)
-            while small.shape[0] < n:
-                small = xor_round(small, 2, n)
+            small, order = xor_round(small, order, [2, 4, 6], n)
+            shards = jnp.asarray(order, jnp.int32) ^ index
+            here = jnp.asarray(ring.table(n, order), jnp.int32)[index]
+            attended = attend(index, shards, queries, keys, values, small[:, : 8 * KVH])
         if k == 2:
-            pair = both(pair, small)
-            attended = attend(jnp.stack([index, index]), queries, keys, values, small[:, : 8 * KVH])
-        if k == 3:
             pair = both(pair, attended)
         for x in pair:
             blocks += [x, ring.swap(x)]
@@ -442,7 +462,8 @@
     index = lax.axis_index("ctx")
     small = summarize(block_ids, keys, values, summary_gain, routes, route_scores, 0)
     small = lax.all_gather(small, "ctx", axis=0, tiled=False)
-    attended = attend(jnp.stack([index, 0 * index]), queries, keys, values, small)
+    shards = jnp.arange(n, dtype=jnp.int32)
+    attended = attend(index, shards, queries, keys, values, small)
     hidden = jnp.dot(
         attended,
         lax.all_gather(out_weight, "ctx", axis=0, tiled=True),

time: 179 us -> 173 us (0.966)
  waiting for transfers between devices: 100 us -> 93 us
  local copies, waits for them, and re-layouts: 8.3 us -> 3.39 us
  Pallas kernels: 30.5 us -> 34.7 us
  other arithmetic: 2.73 us -> 4.78 us
    ppermute x5, waiting for transfers between devices: 17.2 us -> 10.7 us  [xor_round(): lax.ppermute(x, 'ctx', [(i, i ^ mask) for i in range(n)])]
    unnamed x34 -> x16, local copies, waits for them, and re-layouts: 7.41 us -> 1.11 us
    pallas_call x2, Pallas kernels: 2.36 us -> 6.28 us  [the longest x1 4.4 us: attend(): pl.pallas_call(attention_kernel, in_specs=[smem(), vmem(), vmem()] + [hbm...]
  transfers between devices with their start and end apart: 51 -> 51, of which waited for: 26 -> 29; matrix products, arithmetic and copies ran while one was open for 1% -> 3% of each run, Pallas kernels for 14% -> 17%
where the time goes in v4:
time: 173 us
  waiting for transfers between devices  93 us (54%)
  starting transfers between devices  36 us (21%)
  Pallas kernels  34.7 us (20%)
  other arithmetic  4.78 us (3%)
  local copies, waits for them, and re-layouts  3.39 us (2%)
    ppermute x24, waiting for transfers between devices, step(): return lax.ppermute(x, 'ctx', pairs)  76.9 us
    ppermute x24, starting transfers between devices, step(): return lax.ppermute(x, 'ctx', pairs)  25.8 us
    pallas_call x5, Pallas kernels, expert_blocks(): pl.pallas_call(functools.partial(expert_kernel, places), in_specs=[smem()...  23.3 us
    ppermute x5, waiting for transfers between devices, xor_round(): lax.ppermute(x, 'ctx', [(i, i ^ mask) for i in range(n)])  10.7 us
    ppermute x5, starting transfers between devices, xor_round(): lax.ppermute(x, 'ctx', [(i, i ^ mask) for i in range(n)])  6.65 us
    ppermute x22, waiting for transfers between devices, swap(): return lax.ppermute(x, 'ctx', [(i, i ^ 1) for i in range(n)])  5.39 us
    pallas_call x1, Pallas kernels, attend(): pl.pallas_call(attention_kernel, in_specs=[smem(), vmem(), vmem()] + [hbm...  4.4 us
    ppermute x22, starting transfers between devices, swap(): return lax.ppermute(x, 'ctx', [(i, i ^ 1) for i in range(n)])  3.52 us
  transfers between devices with their start and end apart: 51, of which 29 were waited for; matrix products, arithmetic and copies ran while one was open for 3% of the time, Pallas kernels for 17%

profile of v4, /device:TPU:0, one launch (start us, length us, event | category | flops | bytes accessed | tf_op | source)
XLA Modules:
  0.0 172.8 jit_solution(4169865044878511645)
XLA Ops:
  0.6 3.1 %collective-permute-start.2 = (bf16[128,2048]{1,0:T(8,128)(2,1)}, bf16[128,2048]{1,0:T(8,128)(2,1)S(1)}, u32[]{:S(2)}, u32[]{:S(2)}) collective-permute-start(bf16[128,2048]{1,0:T(8,128)(2,1)} %refs_0_.3), channel_id=1, source_target_pairs={{0,4},{1,5},{4,8},{5,9},{8,12},{9,13},{12,14},{13,15},{14,10},{15,... | collective-permute-start | bytes 1572872 | tf_op jit(solution)/shard_map/weight_1_up/ppermute | solution.py:308
  3.7 1.9 %summaries.1 = bf16[64,128]{1,0:T(8,128)(2,1)} custom-call(s32[1,128]{1,0:T(1,128)} %bitcast.24, bf16[128,512]{1,0:T(8,128)(2,1)} %refs_1_.3, bf16[128,512]{1,0:T(8,128)(2,1)} %refs_2_.5, f32[1,128]{1,0:T(1,128)} %bitcast.25, s32[8,128]{1,0:T(8,128)} %bitcast.22, f32[8,128]{1,0:T(8,128)} %bitcast.23), custom_call_target="tpu_custom_call" | custom-call | tf_op jit(solution)/shard_map/summaries/pallas_call | solution.py:93
  6.2 0.9 collective-permute-done
  7.8 3.0 %collective-permute-start.1 = (bf16[2,64,128]{2,1,0:T(8,128)(2,1)S(1)}, bf16[2,64,128]{2,1,0:T(8,128)(2,1)S(1)}, u32[]{:S(2)}, u32[]{:S(2)}) collective-permute-start(bf16[2,64,128]{2,1,0:T(8,128)(2,1)S(1)} %pad_maximum_fusion.1), channel_id=1, source_target_pairs={{0,8},{1,9},{2,10},{3,11},{4,12},{5,13},{6,14},{7,15},{8,0},{9,1},... | collective-permute-start | bytes 98312 | tf_op jit(solution)/shard_map/summary_round/ppermute | solution.py:332
  12.2 7.1 %collective-permute-done.1 = bf16[2,64,128]{2,1,0:T(8,128)(2,1)S(1)} collective-permute-done((bf16[2,64,128]{2,1,0:T(8,128)(2,1)S(1)}, bf16[2,64,128]{2,1,0:T(8,128)(2,1)S(1)}, u32[]{:S(2)}, u32[]{:S(2)}) %collective-permute-start.1) | collective-permute-done | bytes 32800 | tf_op jit(solution)/shard_map/summary_round/ppermute | solution.py:332
  20.4 1.2 collective-permute-start.5
  21.6 2.0 %collective-permute-start.6 = (bf16[4,64,128]{2,1,0:T(8,128)(2,1)S(1)}, bf16[4,64,128]{2,1,0:T(8,128)(2,1)S(1)}, u32[]{:S(2)}, u32[]{:S(2)}) collective-permute-start(bf16[4,64,128]{2,1,0:T(8,128)(2,1)S(1)} %pad_maximum_fusion), channel_id=1, source_target_pairs={{0,6},{1,7},{2,4},{3,5},{4,2},{5,3},{6,0},{7,1},{8,14},{9,15},{10,... | collective-permute-start | bytes 196616 | tf_op jit(solution)/shard_map/summary_round/ppermute | solution.py:332
  23.7 1.2 collective-permute-start.10
  25.9 2.2 %collective-permute-done.6 = bf16[4,64,128]{2,1,0:T(8,128)(2,1)S(1)} collective-permute-done((bf16[4,64,128]{2,1,0:T(8,128)(2,1)S(1)}, bf16[4,64,128]{2,1,0:T(8,128)(2,1)S(1)}, u32[]{:S(2)}, u32[]{:S(2)}) %collective-permute-start.6) | collective-permute-done | bytes 65568 | tf_op jit(solution)/shard_map/summary_round/ppermute | solution.py:332
  28.8 4.4 %attention.1.tokens = bf16[128,2048]{1,0:T(8,128)(2,1)} custom-call(s32[1]{0:T(128)} %bitcast.1.me, s32[1,128]{1,0:T(1,128)} %reshape_reshape.3.owners, bf16[16,32,128]{2,1,0:T(8,128)(2,1)} %get-tuple-element.75.gathered, bf16[128,2048]{1,0:T(8,128)(2,1)} %refs_0_.2, bf16[128,512]{1,0:T(8,128)(2,1)} %refs_1_.3, bf16[128,512]{1,0:T(8,128)(2,1)} %refs_2_.5), custom_call_target="tpu_custom_call" | custom-call | flops 268435456 | bytes 2097152 | tf_op jit(solution)/shard_map/attention/pallas_call | solution.py:151
  33.2 3.5 %collective-permute-done.10.refs_6_ = bf16[128,2048]{1,0:T(8,128)(2,1)} collective-permute-done((bf16[128,2048]{1,0:T(8,128)(2,1)S(1)}, bf16[128,2048]{1,0:T(8,128)(2,1)}, u32[]{:S(2)}, u32[]{:S(2)}) %collective-permute-start.10) | collective-permute-done | bytes 524320 | tf_op jit(solution)/shard_map/weight_2_up/ppermute | solution.py:308
  36.7 1.1 collective-permute-start.14
  37.8 1.0 collective-permute-start.16
  39.9 8.5 %collective-permute-done.14.refs_10_ = bf16[128,2048]{1,0:T(8,128)(2,1)S(1)} collective-permute-done((bf16[128,2048]{1,0:T(8,128)(2,1)}, bf16[128,2048]{1,0:T(8,128)(2,1)S(1)}, u32[]{:S(2)}, u32[]{:S(2)}) %collective-permute-start.14) | collective-permute-done | bytes 524320 | tf_op jit(solution)/shard_map/weight_3_up/ppermute | solution.py:308
  49.4 0.9 collective-permute-start.19
  50.4 1.2 collective-permute-start.18
  51.6 1.0 copy-done.3
  52.6 3.4 %project_first.1.acc = f32[128,2048]{1,0:T(8,128)S(1)} custom-call(s32[25]{0:T(128)S(1)} %dynamic-slice_bitcast_fusion.here, bf16[128,2048]{1,0:T(8,128)(2,1)S(1)} %copy-done.3, bf16[128,2048]{1,0:T(8,128)(2,1)S(1)} %copy-done.4, bf16[128,2048]{1,0:T(8,128)(2,1)S(1)} %collective-permute-done.7.refs_1_, bf16[128,2048]{1,0:T(8,128)(2,1)S(1)} %collective-permute-done.2.refs_2_, ...), custom_call_target="tpu_custom_call" | custom-call | flops 939524096 | bytes 7340032 | tf_op jit(solution)/shard_map/project_first/pallas_call | solution.py:196
  56.1 2.1 %collective-permute-done.19.b = bf16[64,2048]{1,0:T(8,128)(2,1)S(1)} collective-permute-done((bf16[64,2048]{1,0:T(8,128)(2,1)S(1)}, bf16[64,2048]{1,0:T(8,128)(2,1)S(1)}, u32[]{:S(2)}, u32[]{:S(2)}) %collective-permute-start.19) | collective-permute-done | bytes 262176 | tf_op jit(solution)/shard_map/weight_far_down/ppermute | solution.py:308
  58.8 0.9 collective-permute-done.21.d
  60.3 1.7 %project_last.1 = (f32[128,2048]{1,0:T(8,128)S(1)}, bf16[128,2048]{1,0:T(8,128)(2,1)}, bf16[128,2048]{1,0:T(8,128)(2,1)S(1)}) custom-call(s32[25]{0:T(128)S(1)} %dynamic-slice_bitcast_fusion.here, bf16[128,2048]{1,0:T(8,128)(2,1)S(1)} %copy-done.3, f32[128,2048]{1,0:T(8,128)S(1)} %project_first.1.acc, f32[1,2048]{1,0:T(1,128)S(1)} %bitcast.17, ...), custom_call_target="tpu_custom_call" | custom-call | flops 134217728 | bytes 3145728 | tf_op jit(solution)/shard_map/project_last/pallas_call | solution.py:225
  62.9 1.4 collective-permute-start.24
  64.3 3.2 %experts.5 = (bf16[128,2048]{1,0:T(8,128)(2,1)S(1)}, bf16[128,2048]{1,0:T(8,128)(2,1)S(1)}) custom-call(s32[25]{0:T(128)S(1)} %dynamic-slice_bitcast_fusion.here, f32[16,128]{1,0:T(8,128)S(1)} %fusion.table, bf16[128,2048]{1,0:T(8,128)(2,1)S(1)} %get-tuple-element.44.refs_0_, bf16[128,2048]{1,0:T(8,128)(2,1)S(1)} %collective-permute-done.22.refs_1_, ...), custom_call_target="tpu_custom_call" | custom-call | tf_op jit(solution)/shard_map/experts/pallas_call | solution.py:279
  67.5 8.9 %collective-permute-done.25.refs_1_ = bf16[128,2048]{1,0:T(8,128)(2,1)S(1)} collective-permute-done((bf16[128,2048]{1,0:T(8,128)(2,1)S(1)}, bf16[128,2048]{1,0:T(8,128)(2,1)S(1)}, u32[]{:S(2)}, u32[]{:S(2)}) %collective-permute-start.25) | collective-permute-done | bytes 524320 | tf_op jit(solution)/shard_map/token_1_down/ppermute | solution.py:308
  77.6 1.4 collective-permute-start.28
  79.1 5.6 %experts.6 = (bf16[128,2048]{1,0:T(8,128)(2,1)S(1)}, bf16[128,2048]{1,0:T(8,128)(2,1)S(1)}, bf16[256,2048]{1,0:T(8,128)(2,1)S(1)}) custom-call(s32[25]{0:T(128)S(1)} %dynamic-slice_bitcast_fusion.here, f32[16,128]{1,0:T(8,128)S(1)} %fusion.table, bf16[128,2048]{1,0:T(8,128)(2,1)S(1)} %collective-permute-done.24.refs_0_, ...), custom_call_target="tpu_custom_call" | custom-call | tf_op jit(solution)/shard_map/experts/pallas_call | solution.py:279
  84.7 6.4 %collective-permute-done.29.refs_1_ = bf16[128,2048]{1,0:T(8,128)(2,1)S(1)} collective-permute-done((bf16[128,2048]{1,0:T(8,128)(2,1)S(1)}, bf16[128,2048]{1,0:T(8,128)(2,1)S(1)}, u32[]{:S(2)}, u32[]{:S(2)}) %collective-permute-start.29) | collective-permute-done | bytes 524320 | tf_op jit(solution)/shard_map/token_2_down/ppermute | solution.py:308
  92.5 1.2 collective-permute-start.32
  93.8 5.6 %experts.7 = (bf16[128,2048]{1,0:T(8,128)(2,1)S(1)}, bf16[128,2048]{1,0:T(8,128)(2,1)S(1)}, bf16[256,2048]{1,0:T(8,128)(2,1)S(1)}) custom-call(s32[25]{0:T(128)S(1)} %dynamic-slice_bitcast_fusion.here, f32[16,128]{1,0:T(8,128)S(1)} %fusion.table, bf16[128,2048]{1,0:T(8,128)(2,1)S(1)} %collective-permute-done.28.refs_0_, ...), custom_call_target="tpu_custom_call" | custom-call | tf_op jit(solution)/shard_map/experts/pallas_call | solution.py:279
  99.9 5.6 %collective-permute-done.33.refs_1_ = bf16[128,2048]{1,0:T(8,128)(2,1)S(1)} collective-permute-done((bf16[128,2048]{1,0:T(8,128)(2,1)S(1)}, bf16[128,2048]{1,0:T(8,128)(2,1)S(1)}, u32[]{:S(2)}, u32[]{:S(2)}) %collective-permute-start.33) | collective-permute-done | bytes 524320 | tf_op jit(solution)/shard_map/token_3_down/ppermute | solution.py:308
  105.5 1.1 collective-permute-done.32.refs_0_
  107.4 1.4 collective-permute-start.39
  108.8 1.1 collective-permute-start.36
  109.9 5.6 %experts.8 = (bf16[128,2048]{1,0:T(8,128)(2,1)S(1)}, bf16[128,2048]{1,0:T(8,128)(2,1)S(1)}, bf16[256,2048]{1,0:T(8,128)(2,1)S(1)}) custom-call(s32[25]{0:T(128)S(1)} %dynamic-slice_bitcast_fusion.here, f32[16,128]{1,0:T(8,128)S(1)} %fusion.table, bf16[128,2048]{1,0:T(8,128)(2,1)S(1)} %collective-permute-done.32.refs_0_, ...), custom_call_target="tpu_custom_call" | custom-call | tf_op jit(solution)/shard_map/experts/pallas_call | solution.py:279
  115.8 1.2 collective-permute-done.36
  117.0 1.9 %collective-permute-done.40.refs_1_ = bf16[128,2048]{1,0:T(8,128)(2,1)S(1)} collective-permute-done((bf16[128,2048]{1,0:T(8,128)(2,1)S(1)}, bf16[128,2048]{1,0:T(8,128)(2,1)S(1)}, u32[]{:S(2)}, u32[]{:S(2)}) %collective-permute-start.40) | collective-permute-done | bytes 524320 | tf_op jit(solution)/shard_map/swap_cores/ppermute | solution.py:313
  118.9 3.2 %experts.9 = (bf16[128,2048]{1,0:T(8,128)(2,1)S(1)}, bf16[128,2048]{1,0:T(8,128)(2,1)S(1)}) custom-call(s32[25]{0:T(128)S(1)} %dynamic-slice_bitcast_fusion.here, f32[16,128]{1,0:T(8,128)S(1)} %fusion.table, bf16[128,2048]{1,0:T(8,128)(2,1)S(1)} %constant_dynamic-update-slice_fusion.4.refs_0_, bf16[128,2048]{1,0:T(8,128)(2,1)S(1)} %collective-permute-done.40.refs_1_, ...), custom_call_target="tpu_custom_call" | custom-call | tf_op jit(solution)/shard_map/experts/pallas_call | solution.py:279
  122.7 1.4 collective-permute-done.41
  124.3 1.4 collective-permute-start.43
  126.4 6.3 %collective-permute-done.43 = bf16[64,2048]{1,0:T(8,128)(2,1)S(1)} collective-permute-done((bf16[64,2048]{1,0:T(8,128)(2,1)S(1)}, bf16[64,2048]{1,0:T(8,128)(2,1)S(1)}, u32[]{:S(2)}, u32[]{:S(2)}) %collective-permute-start.43) | collective-permute-done | bytes 262176 | tf_op jit(solution)/shard_map/sum_far_up/ppermute | solution.py:308
  132.9 1.4 collective-permute-start.45
  135.2 10.9 %collective-permute-done.45 = bf16[128,2048]{1,0:T(8,128)(2,1)S(1)} collective-permute-done((bf16[128,2048]{1,0:T(8,128)(2,1)S(1)}, bf16[128,2048]{1,0:T(8,128)(2,1)S(1)}, u32[]{:S(2)}, u32[]{:S(2)}) %collective-permute-start.45) | collective-permute-done | bytes 524320 | tf_op jit(solution)/shard_map/sum_3_up/ppermute | solution.py:308
  146.3 1.4 collective-permute-start.47
  148.7 9.9 %collective-permute-done.47 = bf16[128,2048]{1,0:T(8,128)(2,1)S(1)} collective-permute-done((bf16[128,2048]{1,0:T(8,128)(2,1)S(1)}, bf16[128,2048]{1,0:T(8,128)(2,1)S(1)}, u32[]{:S(2)}, u32[]{:S(2)}) %collective-permute-start.47) | collective-permute-done | bytes 524320 | tf_op jit(solution)/shard_map/sum_2_up/ppermute | solution.py:308
  158.8 1.1 collective-permute-done.49
  160.9 1.3 collective-permute-start.48
  162.2 9.0 %collective-permute-done.50 = bf16[128,2048]{1,0:T(8,128)(2,1)S(1)} collective-permute-done((bf16[128,2048]{1,0:T(8,128)(2,1)S(1)}, bf16[128,2048]{1,0:T(8,128)(2,1)S(1)}, u32[]{:S(2)}, u32[]{:S(2)}) %collective-permute-start.50) | collective-permute-done | bytes 524320 | tf_op jit(solution)/shard_map/sum_1_down/ppermute | solution.py:308
  171.6 1.2 add_convert_fusion
  (104 shorter events, 19.4 us)
Async XLA Ops:
  0.6 19.5 %collective-permute-start.2 = (bf16[128,2048]{1,0:T(8,128)(2,1)}, bf16[128,2048]{1,0:T(8,128)(2,1)S(1)}, u32[]{:S(2)}, u32[]{:S(2)}) collective-permute-start(bf16[128,2048]{1,0:T(8,128)(2,1)} %refs_0_.3), channel_id=1, source_target_pairs={{0,4},{1,5},{4,8},{5,9},{8,12},{9,13},{12,14},{13,15},{14,10},{15,... | collective-permute-start | bytes 1572872 | tf_op jit(solution)/shard_map/weight_1_up/ppermute | solution.py:308
  3.7 16.4 %collective-permute-start.3 = (bf16[128,2048]{1,0:T(8,128)(2,1)}, bf16[128,2048]{1,0:T(8,128)(2,1)S(1)}, u32[]{:S(2)}, u32[]{:S(2)}) collective-permute-start(bf16[128,2048]{1,0:T(8,128)(2,1)} %refs_0_.3), channel_id=1, source_target_pairs={{0,2},{1,3},{4,0},{5,1},{8,4},{9,5},{12,8},{13,9},{14,12},{15,13},... | collective-permute-start | bytes 1572872 | tf_op jit(solution)/shard_map/weight_1_down/ppermute | solution.py:308
  5.7 33.0 %collective-permute-start.7 = (bf16[128,2048]{1,0:T(8,128)(2,1)}, bf16[128,2048]{1,0:T(8,128)(2,1)S(1)}, u32[]{:S(2)}, u32[]{:S(2)}) collective-permute-start(bf16[128,2048]{1,0:T(8,128)(2,1)} %refs_0_.3), channel_id=1, source_target_pairs={{0,1},{1,0},{2,3},{3,2},{4,5},{5,4},{6,7},{7,6},{8,9},{9,8},{10,11... | collective-permute-start | bytes 1572872 | tf_op jit(solution)/shard_map/swap_cores/ppermute | solution.py:313
  7.8 11.6 %collective-permute-start.1 = (bf16[2,64,128]{2,1,0:T(8,128)(2,1)S(1)}, bf16[2,64,128]{2,1,0:T(8,128)(2,1)S(1)}, u32[]{:S(2)}, u32[]{:S(2)}) collective-permute-start(bf16[2,64,128]{2,1,0:T(8,128)(2,1)S(1)} %pad_maximum_fusion.1), channel_id=1, source_target_pairs={{0,8},{1,9},{2,10},{3,11},{4,12},{5,13},{6,14},{7,15},{8,0},{9,1},... | collective-permute-start | bytes 98312 | tf_op jit(solution)/shard_map/summary_round/ppermute | solution.py:332
  20.1 5.2 %collective-permute-start.4 = (bf16[4,64,128]{2,1,0:T(8,128)(2,1)S(1)}, bf16[4,64,128]{2,1,0:T(8,128)(2,1)S(1)}, u32[]{:S(2)}, u32[]{:S(2)}) collective-permute-start(bf16[4,64,128]{2,1,0:T(8,128)(2,1)S(1)} %pad_maximum_fusion), channel_id=1, source_target_pairs={{0,2},{1,3},{2,0},{3,1},{4,6},{5,7},{6,4},{7,5},{8,10},{9,11},{10,... | collective-permute-start | bytes 196616 | tf_op jit(solution)/shard_map/summary_round/ppermute | solution.py:332
  20.4 5.4 %collective-permute-start.5 = (bf16[4,64,128]{2,1,0:T(8,128)(2,1)S(1)}, bf16[4,64,128]{2,1,0:T(8,128)(2,1)S(1)}, u32[]{:S(2)}, u32[]{:S(2)}) collective-permute-start(bf16[4,64,128]{2,1,0:T(8,128)(2,1)S(1)} %pad_maximum_fusion), channel_id=1, source_target_pairs={{0,4},{1,5},{2,6},{3,7},{4,0},{5,1},{6,2},{7,3},{8,12},{9,13},{10,... | collective-permute-start | bytes 196616 | tf_op jit(solution)/shard_map/summary_round/ppermute | solution.py:332
  21.6 6.4 %collective-permute-start.6 = (bf16[4,64,128]{2,1,0:T(8,128)(2,1)S(1)}, bf16[4,64,128]{2,1,0:T(8,128)(2,1)S(1)}, u32[]{:S(2)}, u32[]{:S(2)}) collective-permute-start(bf16[4,64,128]{2,1,0:T(8,128)(2,1)S(1)} %pad_maximum_fusion), channel_id=1, source_target_pairs={{0,6},{1,7},{2,4},{3,5},{4,2},{5,3},{6,0},{7,1},{8,14},{9,15},{10,... | collective-permute-start | bytes 196616 | tf_op jit(solution)/shard_map/summary_round/ppermute | solution.py:332
  23.7 13.0 %collective-permute-start.10 = (bf16[128,2048]{1,0:T(8,128)(2,1)S(1)}, bf16[128,2048]{1,0:T(8,128)(2,1)}, u32[]{:S(2)}, u32[]{:S(2)}) collective-permute-start(bf16[128,2048]{1,0:T(8,128)(2,1)S(1)} %collective-permute-done.2.refs_2_), channel_id=1, source_target_pairs={{0,4},{1,5},{4,8},{5,9},{8,12},{9,13},{12,14},{13,15},{14,10},{15,... | collective-permute-start | bytes 1572872 | tf_op jit(solution)/shard_map/weight_2_up/ppermute | solution.py:308
  25.4 12.4 %collective-permute-start.12 = (bf16[128,2048]{1,0:T(8,128)(2,1)S(1)}, bf16[128,2048]{1,0:T(8,128)(2,1)}, u32[]{:S(2)}, u32[]{:S(2)}) collective-permute-start(bf16[128,2048]{1,0:T(8,128)(2,1)S(1)} %collective-permute-done.3.refs_4_), channel_id=1, source_target_pairs={{0,2},{1,3},{4,0},{5,1},{8,4},{9,5},{12,8},{13,9},{14,12},{15,13},... | collective-permute-start | bytes 1572872 | tf_op jit(solution)/shard_map/weight_2_down/ppermute | solution.py:308
  25.8 14.1 %collective-permute-start.8 = (bf16[128,2048]{1,0:T(8,128)(2,1)S(1)}, bf16[128,2048]{1,0:T(8,128)(2,1)}, u32[]{:S(2)}, u32[]{:S(2)}) collective-permute-start(bf16[128,2048]{1,0:T(8,128)(2,1)S(1)} %collective-permute-done.2.refs_2_), channel_id=1, source_target_pairs={{0,1},{1,0},{2,3},{3,2},{4,5},{5,4},{6,7},{7,6},{8,9},{9,8},{10,11... | collective-permute-start | bytes 1572872 | tf_op jit(solution)/shard_map/swap_cores/ppermute | solution.py:313
  36.7 11.8 %collective-permute-start.14 = (bf16[128,2048]{1,0:T(8,128)(2,1)}, bf16[128,2048]{1,0:T(8,128)(2,1)S(1)}, u32[]{:S(2)}, u32[]{:S(2)}) collective-permute-start(bf16[128,2048]{1,0:T(8,128)(2,1)} %collective-permute-done.10.refs_6_), channel_id=1, source_target_pairs={{0,4},{1,5},{4,8},{5,9},{8,12},{9,13},{12,14},{13,15},{14,10},{15,... | collective-permute-start | bytes 1572872 | tf_op jit(solution)/shard_map/weight_3_up/ppermute | solution.py:308
  37.8 11.6 %collective-permute-start.16 = (bf16[128,2048]{1,0:T(8,128)(2,1)}, bf16[128,2048]{1,0:T(8,128)(2,1)S(1)}, u32[]{:S(2)}, u32[]{:S(2)}) collective-permute-start(bf16[128,2048]{1,0:T(8,128)(2,1)} %collective-permute-done.12.refs_8_), channel_id=1, source_target_pairs={{0,2},{1,3},{4,0},{5,1},{8,4},{9,5},{12,8},{13,9},{14,12},{15,13},... | collective-permute-start | bytes 1572872 | tf_op jit(solution)/shard_map/weight_3_down/ppermute | solution.py:308
  38.7 10.7 %collective-permute-start.9 = (bf16[128,2048]{1,0:T(8,128)(2,1)S(1)}, bf16[128,2048]{1,0:T(8,128)(2,1)}, u32[]{:S(2)}, u32[]{:S(2)}) collective-permute-start(bf16[128,2048]{1,0:T(8,128)(2,1)S(1)} %collective-permute-done.3.refs_4_), channel_id=1, source_target_pairs={{0,1},{1,0},{2,3},{3,2},{4,5},{5,4},{6,7},{7,6},{8,9},{9,8},{10,11... | collective-permute-start | bytes 1572872 | tf_op jit(solution)/shard_map/swap_cores/ppermute | solution.py:313
  38.7 11.6 %collective-permute-start.11 = (bf16[128,2048]{1,0:T(8,128)(2,1)}, bf16[128,2048]{1,0:T(8,128)(2,1)}, u32[]{:S(2)}, u32[]{:S(2)}) collective-permute-start(bf16[128,2048]{1,0:T(8,128)(2,1)} %collective-permute-done.10.refs_6_), channel_id=1, source_target_pairs={{0,1},{1,0},{2,3},{3,2},{4,5},{5,4},{6,7},{7,6},{8,9},{9,8},{10,11... | collective-permute-start | bytes 1572872 | tf_op jit(solution)/shard_map/swap_cores/ppermute | solution.py:313
  39.9 11.6 %collective-permute-start.13 = (bf16[128,2048]{1,0:T(8,128)(2,1)}, bf16[128,2048]{1,0:T(8,128)(2,1)S(1)}, u32[]{:S(2)}, u32[]{:S(2)}) collective-permute-start(bf16[128,2048]{1,0:T(8,128)(2,1)} %collective-permute-done.12.refs_8_), channel_id=1, source_target_pairs={{0,1},{1,0},{2,3},{3,2},{4,5},{5,4},{6,7},{7,6},{8,9},{9,8},{10,11... | collective-permute-start | bytes 1572872 | tf_op jit(solution)/shard_map/swap_cores/ppermute | solution.py:313
  48.5 3.1 %collective-permute-start.15 = (bf16[128,2048]{1,0:T(8,128)(2,1)S(1)}, bf16[128,2048]{1,0:T(8,128)(2,1)S(1)}, u32[]{:S(2)}, u32[]{:S(2)}) collective-permute-start(bf16[128,2048]{1,0:T(8,128)(2,1)S(1)} %collective-permute-done.14.refs_10_), channel_id=1, source_target_pairs={{0,1},{1,0},{2,3},{3,2},{4,5},{5,4},{6,7},{7,6},{8,9},{9,8},{10,11... | collective-permute-start | bytes 1572872 | tf_op jit(solution)/shard_map/swap_cores/ppermute | solution.py:313
  49.3 2.2 %collective-permute-start.17 = (bf16[128,2048]{1,0:T(8,128)(2,1)S(1)}, bf16[128,2048]{1,0:T(8,128)(2,1)S(1)}, u32[]{:S(2)}, u32[]{:S(2)}) collective-permute-start(bf16[128,2048]{1,0:T(8,128)(2,1)S(1)} %collective-permute-done.16.refs_12_), channel_id=1, source_target_pairs={{0,1},{1,0},{2,3},{3,2},{4,5},{5,4},{6,7},{7,6},{8,9},{9,8},{10,11... | collective-permute-start | bytes 1572872 | tf_op jit(solution)/shard_map/swap_cores/ppermute | solution.py:313
  49.4 8.8 %collective-permute-start.19 = (bf16[64,2048]{1,0:T(8,128)(2,1)S(1)}, bf16[64,2048]{1,0:T(8,128)(2,1)S(1)}, u32[]{:S(2)}, u32[]{:S(2)}) collective-permute-start(bf16[64,2048]{1,0:T(8,128)(2,1)S(1)} %slice.69), channel_id=1, source_target_pairs={{0,2},{1,3},{4,0},{5,1},{8,4},{9,5},{12,8},{13,9},{14,12},{15,13},... | collective-permute-start | bytes 786440 | tf_op jit(solution)/shard_map/weight_far_down/ppermute | solution.py:308
  50.4 8.4 %collective-permute-start.18 = (bf16[64,2048]{1,0:T(8,128)(2,1)S(1)}, bf16[64,2048]{1,0:T(8,128)(2,1)S(1)}, u32[]{:S(2)}, u32[]{:S(2)}) collective-permute-start(bf16[64,2048]{1,0:T(8,128)(2,1)S(1)} %slice.65), channel_id=1, source_target_pairs={{0,4},{1,5},{4,8},{5,9},{8,12},{9,13},{12,14},{13,15},{14,10},{15,... | collective-permute-start | bytes 786440 | tf_op jit(solution)/shard_map/weight_far_up/ppermute | solution.py:308
  62.1 2.2 %collective-permute-start.22 = (bf16[128,2048]{1,0:T(8,128)(2,1)S(1)}, bf16[128,2048]{1,0:T(8,128)(2,1)S(1)}, u32[]{:S(2)}, u32[]{:S(2)}) collective-permute-start(bf16[128,2048]{1,0:T(8,128)(2,1)S(1)} %get-tuple-element.44.refs_0_), channel_id=1, source_target_pairs={{0,1},{1,0},{2,3},{3,2},{4,5},{5,4},{6,7},{7,6},{8,9},{9,8},{10,11... | collective-permute-start | bytes 1572872 | tf_op jit(solution)/shard_map/swap_cores/ppermute | solution.py:313
  62.2 14.2 %collective-permute-start.25 = (bf16[128,2048]{1,0:T(8,128)(2,1)S(1)}, bf16[128,2048]{1,0:T(8,128)(2,1)S(1)}, u32[]{:S(2)}, u32[]{:S(2)}) collective-permute-start(bf16[128,2048]{1,0:T(8,128)(2,1)S(1)} %get-tuple-element.44.refs_0_), channel_id=1, source_target_pairs={{0,2},{1,3},{4,0},{5,1},{8,4},{9,5},{12,8},{13,9},{14,12},{15,13},... | collective-permute-start | bytes 1572872 | tf_op jit(solution)/shard_map/token_1_down/ppermute | solution.py:308
  62.9 13.9 %collective-permute-start.24 = (bf16[128,2048]{1,0:T(8,128)(2,1)S(1)}, bf16[128,2048]{1,0:T(8,128)(2,1)S(1)}, u32[]{:S(2)}, u32[]{:S(2)}) collective-permute-start(bf16[128,2048]{1,0:T(8,128)(2,1)S(1)} %get-tuple-element.44.refs_0_), channel_id=1, source_target_pairs={{0,4},{1,5},{4,8},{5,9},{8,12},{9,13},{12,14},{13,15},{14,10},{15,... | collective-permute-start | bytes 1572872 | tf_op jit(solution)/shard_map/token_1_up/ppermute | solution.py:308
  76.4 2.6 %collective-permute-start.27 = (bf16[128,2048]{1,0:T(8,128)(2,1)S(1)}, bf16[128,2048]{1,0:T(8,128)(2,1)S(1)}, u32[]{:S(2)}, u32[]{:S(2)}) collective-permute-start(bf16[128,2048]{1,0:T(8,128)(2,1)S(1)} %collective-permute-done.25.refs_1_), channel_id=1, source_target_pairs={{0,1},{1,0},{2,3},{3,2},{4,5},{5,4},{6,7},{7,6},{8,9},{9,8},{10,11... | collective-permute-start | bytes 1572872 | tf_op jit(solution)/shard_map/swap_cores/ppermute | solution.py:313
  76.8 2.3 %collective-permute-start.26 = (bf16[128,2048]{1,0:T(8,128)(2,1)S(1)}, bf16[128,2048]{1,0:T(8,128)(2,1)S(1)}, u32[]{:S(2)}, u32[]{:S(2)}) collective-permute-start(bf16[128,2048]{1,0:T(8,128)(2,1)S(1)} %collective-permute-done.24.refs_0_), channel_id=1, source_target_pairs={{0,1},{1,0},{2,3},{3,2},{4,5},{5,4},{6,7},{7,6},{8,9},{9,8},{10,11... | collective-permute-start | bytes 1572872 | tf_op jit(solution)/shard_map/swap_cores/ppermute | solution.py:313
  76.9 14.2 %collective-permute-start.29 = (bf16[128,2048]{1,0:T(8,128)(2,1)S(1)}, bf16[128,2048]{1,0:T(8,128)(2,1)S(1)}, u32[]{:S(2)}, u32[]{:S(2)}) collective-permute-start(bf16[128,2048]{1,0:T(8,128)(2,1)S(1)} %collective-permute-done.25.refs_1_), channel_id=1, source_target_pairs={{0,2},{1,3},{4,0},{5,1},{8,4},{9,5},{12,8},{13,9},{14,12},{15,13},... | collective-permute-start | bytes 1572872 | tf_op jit(solution)/shard_map/token_2_down/ppermute | solution.py:308
  77.6 13.6 %collective-permute-start.28 = (bf16[128,2048]{1,0:T(8,128)(2,1)S(1)}, bf16[128,2048]{1,0:T(8,128)(2,1)S(1)}, u32[]{:S(2)}, u32[]{:S(2)}) collective-permute-start(bf16[128,2048]{1,0:T(8,128)(2,1)S(1)} %collective-permute-done.24.refs_0_), channel_id=1, source_target_pairs={{0,4},{1,5},{4,8},{5,9},{8,12},{9,13},{12,14},{13,15},{14,10},{15,... | collective-permute-start | bytes 1572872 | tf_op jit(solution)/shard_map/token_2_up/ppermute | solution.py:308
  91.1 2.5 %collective-permute-start.31 = (bf16[128,2048]{1,0:T(8,128)(2,1)S(1)}, bf16[128,2048]{1,0:T(8,128)(2,1)S(1)}, u32[]{:S(2)}, u32[]{:S(2)}) collective-permute-start(bf16[128,2048]{1,0:T(8,128)(2,1)S(1)} %collective-permute-done.29.refs_1_), channel_id=1, source_target_pairs={{0,1},{1,0},{2,3},{3,2},{4,5},{5,4},{6,7},{7,6},{8,9},{9,8},{10,11... | collective-permute-start | bytes 1572872 | tf_op jit(solution)/shard_map/swap_cores/ppermute | solution.py:313
  91.1 2.7 %collective-permute-start.30 = (bf16[128,2048]{1,0:T(8,128)(2,1)S(1)}, bf16[128,2048]{1,0:T(8,128)(2,1)S(1)}, u32[]{:S(2)}, u32[]{:S(2)}) collective-permute-start(bf16[128,2048]{1,0:T(8,128)(2,1)S(1)} %collective-permute-done.28.refs_0_), channel_id=1, source_target_pairs={{0,1},{1,0},{2,3},{3,2},{4,5},{5,4},{6,7},{7,6},{8,9},{9,8},{10,11... | collective-permute-start | bytes 1572872 | tf_op jit(solution)/shard_map/swap_cores/ppermute | solution.py:313
  91.7 13.8 %collective-permute-start.33 = (bf16[128,2048]{1,0:T(8,128)(2,1)S(1)}, bf16[128,2048]{1,0:T(8,128)(2,1)S(1)}, u32[]{:S(2)}, u32[]{:S(2)}) collective-permute-start(bf16[128,2048]{1,0:T(8,128)(2,1)S(1)} %collective-permute-done.29.refs_1_), channel_id=1, source_target_pairs={{0,2},{1,3},{4,0},{5,1},{8,4},{9,5},{12,8},{13,9},{14,12},{15,13},... | collective-permute-start | bytes 1572872 | tf_op jit(solution)/shard_map/token_3_down/ppermute | solution.py:308
  92.5 14.1 %collective-permute-start.32 = (bf16[128,2048]{1,0:T(8,128)(2,1)S(1)}, bf16[128,2048]{1,0:T(8,128)(2,1)S(1)}, u32[]{:S(2)}, u32[]{:S(2)}) collective-permute-start(bf16[128,2048]{1,0:T(8,128)(2,1)S(1)} %collective-permute-done.28.refs_0_), channel_id=1, source_target_pairs={{0,4},{1,5},{4,8},{5,9},{8,12},{9,13},{12,14},{13,15},{14,10},{15,... | collective-permute-start | bytes 1572872 | tf_op jit(solution)/shard_map/token_3_up/ppermute | solution.py:308
  93.7 22.1 %collective-permute-start.37 = (bf16[256,2048]{1,0:T(8,128)(2,1)S(1)}, bf16[256,2048]{1,0:T(8,128)(2,1)S(1)}, u32[]{:S(2)}, u32[]{:S(2)}) collective-permute-start(bf16[256,2048]{1,0:T(8,128)(2,1)S(1)} %get-tuple-element.59), channel_id=1, source_target_pairs={{0,1},{1,0},{2,3},{3,2},{4,5},{5,4},{6,7},{7,6},{8,9},{9,8},{10,11... | collective-permute-start | bytes 3145736 | tf_op jit(solution)/shard_map/swap_cores/ppermute | solution.py:313
  99.4 16.3 %collective-permute-start.38 = (bf16[256,2048]{1,0:T(8,128)(2,1)S(1)}, bf16[256,2048]{1,0:T(8,128)(2,1)S(1)}, u32[]{:S(2)}, u32[]{:S(2)}) collective-permute-start(bf16[256,2048]{1,0:T(8,128)(2,1)S(1)} %get-tuple-element.60), channel_id=1, source_target_pairs={{0,1},{1,0},{2,3},{3,2},{4,5},{5,4},{6,7},{7,6},{8,9},{9,8},{10,11... | collective-permute-start | bytes 3145736 | tf_op jit(solution)/shard_map/swap_cores/ppermute | solution.py:313
  105.5 1.9 %collective-permute-start.35 = (bf16[128,2048]{1,0:T(8,128)(2,1)S(1)}, bf16[128,2048]{1,0:T(8,128)(2,1)S(1)}, u32[]{:S(2)}, u32[]{:S(2)}) collective-permute-start(bf16[128,2048]{1,0:T(8,128)(2,1)S(1)} %collective-permute-done.33.refs_1_), channel_id=1, source_target_pairs={{0,1},{1,0},{2,3},{3,2},{4,5},{5,4},{6,7},{7,6},{8,9},{9,8},{10,11... | collective-permute-start | bytes 1572872 | tf_op jit(solution)/shard_map/swap_cores/ppermute | solution.py:313
  106.6 2.2 %collective-permute-start.34 = (bf16[128,2048]{1,0:T(8,128)(2,1)S(1)}, bf16[128,2048]{1,0:T(8,128)(2,1)S(1)}, u32[]{:S(2)}, u32[]{:S(2)}) collective-permute-start(bf16[128,2048]{1,0:T(8,128)(2,1)S(1)} %collective-permute-done.32.refs_0_), channel_id=1, source_target_pairs={{0,1},{1,0},{2,3},{3,2},{4,5},{5,4},{6,7},{7,6},{8,9},{9,8},{10,11... | collective-permute-start | bytes 1572872 | tf_op jit(solution)/shard_map/swap_cores/ppermute | solution.py:313
  106.6 9.0 %collective-permute-start.23 = (bf16[128,2048]{1,0:T(8,128)(2,1)S(1)}, bf16[128,2048]{1,0:T(8,128)(2,1)S(1)}, u32[]{:S(2)}, u32[]{:S(2)}) collective-permute-start(bf16[128,2048]{1,0:T(8,128)(2,1)S(1)} %get-tuple-element.46), channel_id=1, source_target_pairs={{0,1},{1,0},{2,3},{3,2},{4,5},{5,4},{6,7},{7,6},{8,9},{9,8},{10,11... | collective-permute-start | bytes 1572872 | tf_op jit(solution)/shard_map/swap_cores/ppermute | solution.py:313
  107.4 8.3 %collective-permute-start.39 = (bf16[64,2048]{1,0:T(8,128)(2,1)S(1)}, bf16[64,2048]{1,0:T(8,128)(2,1)S(1)}, u32[]{:S(2)}, u32[]{:S(2)}) collective-permute-start(bf16[64,2048]{1,0:T(8,128)(2,1)S(1)} %slice.55), channel_id=1, source_target_pairs={{0,2},{1,3},{4,0},{5,1},{8,4},{9,5},{12,8},{13,9},{14,12},{15,13},... | collective-permute-start | bytes 786440 | tf_op jit(solution)/shard_map/token_far_down/ppermute | solution.py:308
  108.8 8.1 %collective-permute-start.36 = (bf16[64,2048]{1,0:T(8,128)(2,1)S(1)}, bf16[64,2048]{1,0:T(8,128)(2,1)S(1)}, u32[]{:S(2)}, u32[]{:S(2)}) collective-permute-start(bf16[64,2048]{1,0:T(8,128)(2,1)S(1)} %slice.54), channel_id=1, source_target_pairs={{0,4},{1,5},{4,8},{5,9},{8,12},{9,13},{12,14},{13,15},{14,10},{15,... | collective-permute-start | bytes 786440 | tf_op jit(solution)/shard_map/token_far_up/ppermute | solution.py:308
  117.0 2.0 %collective-permute-start.40 = (bf16[128,2048]{1,0:T(8,128)(2,1)S(1)}, bf16[128,2048]{1,0:T(8,128)(2,1)S(1)}, u32[]{:S(2)}, u32[]{:S(2)}) collective-permute-start(bf16[128,2048]{1,0:T(8,128)(2,1)S(1)} %constant_dynamic-update-slice_fusion.4.refs_0_), channel_id=1, source_target_pairs={{0,1},{1,0},{2,3},{3,2},{4,5},{5,4},{6,7},{7,6},{8,9},{9,8},{10,11... | collective-permute-start | bytes 1572872 | tf_op jit(solution)/shard_map/swap_cores/ppermute | solution.py:313
  122.1 2.0 %collective-permute-start.41 = (bf16[128,2048]{1,0:T(8,128)(2,1)S(1)}, bf16[128,2048]{1,0:T(8,128)(2,1)S(1)}, u32[]{:S(2)}, u32[]{:S(2)}) collective-permute-start(bf16[128,2048]{1,0:T(8,128)(2,1)S(1)} %get-tuple-element.64), channel_id=1, source_target_pairs={{0,1},{1,0},{2,3},{3,2},{4,5},{5,4},{6,7},{7,6},{8,9},{9,8},{10,11... | collective-permute-start | bytes 1572872 | tf_op jit(solution)/shard_map/swap_cores/ppermute | solution.py:313
  122.3 4.0 %collective-permute-start.42 = (bf16[256,2048]{1,0:T(8,128)(2,1)S(1)}, bf16[256,2048]{1,0:T(8,128)(2,1)S(1)}, u32[]{:S(2)}, u32[]{:S(2)}) collective-permute-start(bf16[256,2048]{1,0:T(8,128)(2,1)S(1)} %get-tuple-element.66), channel_id=1, source_target_pairs={{0,1},{1,0},{2,3},{3,2},{4,5},{5,4},{6,7},{7,6},{8,9},{9,8},{10,11... | collective-permute-start | bytes 3145736 | tf_op jit(solution)/shard_map/swap_cores/ppermute | solution.py:313
  124.3 8.4 %collective-permute-start.43 = (bf16[64,2048]{1,0:T(8,128)(2,1)S(1)}, bf16[64,2048]{1,0:T(8,128)(2,1)S(1)}, u32[]{:S(2)}, u32[]{:S(2)}) collective-permute-start(bf16[64,2048]{1,0:T(8,128)(2,1)S(1)} %get-tuple-element.73), channel_id=1, source_target_pairs={{0,4},{1,5},{4,8},{5,9},{8,12},{9,13},{12,14},{13,15},{14,10},{15,... | collective-permute-start | bytes 786440 | tf_op jit(solution)/shard_map/sum_far_up/ppermute | solution.py:308
  125.7 8.6 %collective-permute-start.44 = (bf16[64,2048]{1,0:T(8,128)(2,1)S(1)}, bf16[64,2048]{1,0:T(8,128)(2,1)S(1)}, u32[]{:S(2)}, u32[]{:S(2)}) collective-permute-start(bf16[64,2048]{1,0:T(8,128)(2,1)S(1)} %get-tuple-element.72), channel_id=1, source_target_pairs={{0,2},{1,3},{4,0},{5,1},{8,4},{9,5},{12,8},{13,9},{14,12},{15,13},... | collective-permute-start | bytes 786440 | tf_op jit(solution)/shard_map/sum_far_down/ppermute | solution.py:308
  132.9 13.2 %collective-permute-start.45 = (bf16[128,2048]{1,0:T(8,128)(2,1)S(1)}, bf16[128,2048]{1,0:T(8,128)(2,1)S(1)}, u32[]{:S(2)}, u32[]{:S(2)}) collective-permute-start(bf16[128,2048]{1,0:T(8,128)(2,1)S(1)} %add_convert_fusion.6), channel_id=1, source_target_pairs={{0,4},{1,5},{4,8},{5,9},{8,12},{9,13},{12,14},{13,15},{14,10},{15,... | collective-permute-start | bytes 1572872 | tf_op jit(solution)/shard_map/sum_3_up/ppermute | solution.py:308
  134.4 13.2 %collective-permute-start.46 = (bf16[128,2048]{1,0:T(8,128)(2,1)S(1)}, bf16[128,2048]{1,0:T(8,128)(2,1)S(1)}, u32[]{:S(2)}, u32[]{:S(2)}) collective-permute-start(bf16[128,2048]{1,0:T(8,128)(2,1)S(1)} %add_convert_fusion.5), channel_id=1, source_target_pairs={{0,2},{1,3},{4,0},{5,1},{8,4},{9,5},{12,8},{13,9},{14,12},{15,13},... | collective-permute-start | bytes 1572872 | tf_op jit(solution)/shard_map/sum_3_down/ppermute | solution.py:308
  146.3 12.3 %collective-permute-start.47 = (bf16[128,2048]{1,0:T(8,128)(2,1)S(1)}, bf16[128,2048]{1,0:T(8,128)(2,1)S(1)}, u32[]{:S(2)}, u32[]{:S(2)}) collective-permute-start(bf16[128,2048]{1,0:T(8,128)(2,1)S(1)} %add_convert_fusion.4), channel_id=1, source_target_pairs={{0,4},{1,5},{4,8},{5,9},{8,12},{9,13},{12,14},{13,15},{14,10},{15,... | collective-permute-start | bytes 1572872 | tf_op jit(solution)/shard_map/sum_2_up/ppermute | solution.py:308
  147.9 12.0 %collective-permute-start.49 = (bf16[128,2048]{1,0:T(8,128)(2,1)S(1)}, bf16[128,2048]{1,0:T(8,128)(2,1)S(1)}, u32[]{:S(2)}, u32[]{:S(2)}) collective-permute-start(bf16[128,2048]{1,0:T(8,128)(2,1)S(1)} %add_convert_fusion.3), channel_id=1, source_target_pairs={{0,2},{1,3},{4,0},{5,1},{8,4},{9,5},{12,8},{13,9},{14,12},{15,13},... | collective-permute-start | bytes 1572872 | tf_op jit(solution)/shard_map/sum_2_down/ppermute | solution.py:308
  160.2 11.1 %collective-permute-start.50 = (bf16[128,2048]{1,0:T(8,128)(2,1)S(1)}, bf16[128,2048]{1,0:T(8,128)(2,1)S(1)}, u32[]{:S(2)}, u32[]{:S(2)}) collective-permute-start(bf16[128,2048]{1,0:T(8,128)(2,1)S(1)} %add_convert_fusion.1), channel_id=1, source_target_pairs={{0,2},{1,3},{4,0},{5,1},{8,4},{9,5},{12,8},{13,9},{14,12},{15,13},... | collective-permute-start | bytes 1572872 | tf_op jit(solution)/shard_map/sum_1_down/ppermute | solution.py:308
  160.9 10.7 %collective-permute-start.48 = (bf16[128,2048]{1,0:T(8,128)(2,1)S(1)}, bf16[128,2048]{1,0:T(8,128)(2,1)S(1)}, u32[]{:S(2)}, u32[]{:S(2)}) collective-permute-start(bf16[128,2048]{1,0:T(8,128)(2,1)S(1)} %add_convert_fusion.2), channel_id=1, source_target_pairs={{0,4},{1,5},{4,8},{5,9},{8,12},{9,13},{12,14},{13,15},{14,10},{15,... | collective-permute-start | bytes 1572872 | tf_op jit(solution)/shard_map/sum_1_up/ppermute | solution.py:308
  (9 other events, 100.3 us)

commit v5 on v4

--- a/solution.py
+++ b/solution.py
@@ -253,9 +253,9 @@
     tile = 256
     for i in range(count):
         tokens[i * rows : (i + 1) * rows, :] = blocks[i][...]
-        weight = table[pl.ds(here[places[i]], 1), :]
+        weight = table[pl.ds(here[places[i][0]], 1), :]
         weight = jnp.transpose(jnp.broadcast_to(weight, (lanes, lanes)))
-        scale[i * rows : (i + 1) * rows, :] = weight
+        scale[i * rows : (i + 1) * rows, :] = weight[places[i][1] : places[i][1] + rows]
     for f in range(0, ff, tile):
         cols = slice(f, f + tile)
         g = jnp.dot(tokens[...], gate[0, :, cols], preferred_element_type=F32)
@@ -404,29 +404,33 @@
         ring.chips, here, attended, acc, norm_gain, [*pair, *(ring.swap(x) for x in pair)]
     )
 
-    def experts(level, chips):
+    def experts(level, chips, firsts=(0, 0)):
         others = [ring.swap(x) for x in level]
-        places = [1 + ring.chips + c for c in chips] + [1 + 2 * ring.chips + c for c in chips]
+        places = [(1 + ring.chips + c, first) for c, first in zip(chips, firsts)]
+        places += [(1 + 2 * ring.chips + c, first) for c, first in zip(chips, firsts)]
         *kept, sent = expert_blocks(
             tuple(places), here, table, [*level, *others], expert_gate, expert_up, expert_down
         )
         return [*kept, ring.swap(sent)]
 
     pair = forward([normed, normed], "token_1")
-    results = [experts([normed], [0])]
+    results = [[normed]]
     for k in range(1, ring.far):
-        pair = both(pair, results[-1][0])
+        if k > 1:
+            pair = both(pair, results[-1][0])
         level = pair
         if k < ring.far - 1:
             pair = forward(pair, "token_" + str(k + 1))
         else:
             pair = forward_far(pair, "token_far")
         results.append(experts(level, [2 * k - 1, 2 * k]))
-    pair = both(pair, *(r[-1] for r in results[:-1]), results[-1][0])
-    far = experts([jnp.concatenate(pair, axis=0)], [ring.chips - 1])
-
-    total = add(*far)
-    pair = forward_far([total, total], "sum_far")
+    pair = both(pair, *(r[-1] for r in results[1:-1]), results[-1][0])
+    far_up, far_down, back = experts(pair, [ring.chips - 1] * 2, (0, half))
+
+    up = add(far_up, back[:half])
+    total = add(after(far_down, up), back[half:])
+    pair = forward([up, total], "sum_far")
+    results[0] = experts([after(normed, total)], [0])
     rows = queries.shape[0]
     for k in range(ring.far - 1, 0, -1):
         behind, ahead, back = results[k]

time: 173 us -> 172 us (level)
    ppermute x22 -> x23, starting transfers between devices: 3.52 us -> 2.46 us  [swap(): return lax.ppermute(x, 'ctx', [(i, i ^ 1) for i in range(n)])]
    ppermute x22 -> x23, waiting for transfers between devices: 5.39 us -> 5.18 us  [swap(): return lax.ppermute(x, 'ctx', [(i, i ^ 1) for i in range(n)])]
  transfers between devices with their start and end apart: 51 -> 52, of which waited for: 29 -> 29; matrix products, arithmetic and copies ran while one was open for 3% -> 3% of each run, Pallas kernels for 17% -> 17%
where the time goes in v5:
time: 172 us
  waiting for transfers between devices  93.7 us (54%)
  Pallas kernels  34.8 us (20%)
  starting transfers between devices  34.5 us (20%)
  other arithmetic  4.75 us (3%)
  local copies, waits for them, and re-layouts  3.31 us (2%)
    ppermute x24, waiting for transfers between devices, step(): return lax.ppermute(x, 'ctx', pairs)  77.9 us
    ppermute x24, starting transfers between devices, step(): return lax.ppermute(x, 'ctx', pairs)  25.4 us
    pallas_call x5, Pallas kernels, expert_blocks(): pl.pallas_call(functools.partial(expert_kernel, places), in_specs=[smem()...  23.3 us
    ppermute x5, waiting for transfers between devices, xor_round(): lax.ppermute(x, 'ctx', [(i, i ^ mask) for i in range(n)])  10.7 us
    ppermute x5, starting transfers between devices, xor_round(): lax.ppermute(x, 'ctx', [(i, i ^ mask) for i in range(n)])  6.65 us
    ppermute x23, waiting for transfers between devices, swap(): return lax.ppermute(x, 'ctx', [(i, i ^ 1) for i in range(n)])  5.18 us
    pallas_call x1, Pallas kernels, attend(): pl.pallas_call(attention_kernel, in_specs=[smem(), vmem(), vmem()] + [hbm...  4.4 us
    pallas_call x1, Pallas kernels, project_first(): pl.pallas_call(functools.partial(project_first_kernel, levels), in_specs=...  3.44 us
  transfers between devices with their start and end apart: 52, of which 29 were waited for; matrix products, arithmetic and copies ran while one was open for 3% of the time, Pallas kernels for 17%

profile of v5, /device:TPU:0, one launch (start us, length us, event | category | flops | bytes accessed | tf_op | source)
XLA Modules:
  0.0 172.0 jit_solution(13829602066154113942)
XLA Ops:
  0.6 3.1 %collective-permute-start.2 = (bf16[128,2048]{1,0:T(8,128)(2,1)}, bf16[128,2048]{1,0:T(8,128)(2,1)S(1)}, u32[]{:S(2)}, u32[]{:S(2)}) collective-permute-start(bf16[128,2048]{1,0:T(8,128)(2,1)} %refs_0_.3), channel_id=1, source_target_pairs={{0,4},{1,5},{4,8},{5,9},{8,12},{9,13},{12,14},{13,15},{14,10},{15,... | collective-permute-start | bytes 1572872 | tf_op jit(solution)/shard_map/weight_1_up/ppermute | solution.py:308
  3.7 1.9 %summaries.1 = bf16[64,128]{1,0:T(8,128)(2,1)} custom-call(s32[1,128]{1,0:T(1,128)} %bitcast.24, bf16[128,512]{1,0:T(8,128)(2,1)} %refs_1_.3, bf16[128,512]{1,0:T(8,128)(2,1)} %refs_2_.4, f32[1,128]{1,0:T(1,128)} %bitcast.25, s32[8,128]{1,0:T(8,128)} %bitcast.22, f32[8,128]{1,0:T(8,128)} %bitcast.23), custom_call_target="tpu_custom_call" | custom-call | tf_op jit(solution)/shard_map/summaries/pallas_call | solution.py:93
  7.8 3.0 %collective-permute-start.1 = (bf16[2,64,128]{2,1,0:T(8,128)(2,1)S(1)}, bf16[2,64,128]{2,1,0:T(8,128)(2,1)S(1)}, u32[]{:S(2)}, u32[]{:S(2)}) collective-permute-start(bf16[2,64,128]{2,1,0:T(8,128)(2,1)S(1)} %pad_maximum_fusion.1), channel_id=1, source_target_pairs={{0,8},{1,9},{2,10},{3,11},{4,12},{5,13},{6,14},{7,15},{8,0},{9,1},... | collective-permute-start | bytes 98312 | tf_op jit(solution)/shard_map/summary_round/ppermute | solution.py:332
  12.2 7.1 %collective-permute-done.1 = bf16[2,64,128]{2,1,0:T(8,128)(2,1)S(1)} collective-permute-done((bf16[2,64,128]{2,1,0:T(8,128)(2,1)S(1)}, bf16[2,64,128]{2,1,0:T(8,128)(2,1)S(1)}, u32[]{:S(2)}, u32[]{:S(2)}) %collective-permute-start.1) | collective-permute-done | bytes 32800 | tf_op jit(solution)/shard_map/summary_round/ppermute | solution.py:332
  20.4 1.2 collective-permute-start.5
  21.6 2.0 %collective-permute-start.6 = (bf16[4,64,128]{2,1,0:T(8,128)(2,1)S(1)}, bf16[4,64,128]{2,1,0:T(8,128)(2,1)S(1)}, u32[]{:S(2)}, u32[]{:S(2)}) collective-permute-start(bf16[4,64,128]{2,1,0:T(8,128)(2,1)S(1)} %pad_maximum_fusion), channel_id=1, source_target_pairs={{0,6},{1,7},{2,4},{3,5},{4,2},{5,3},{6,0},{7,1},{8,14},{9,15},{10,... | collective-permute-start | bytes 196616 | tf_op jit(solution)/shard_map/summary_round/ppermute | solution.py:332
  23.7 1.2 collective-permute-start.10
  25.9 2.2 %collective-permute-done.6 = bf16[4,64,128]{2,1,0:T(8,128)(2,1)S(1)} collective-permute-done((bf16[4,64,128]{2,1,0:T(8,128)(2,1)S(1)}, bf16[4,64,128]{2,1,0:T(8,128)(2,1)S(1)}, u32[]{:S(2)}, u32[]{:S(2)}) %collective-permute-start.6) | collective-permute-done | bytes 65568 | tf_op jit(solution)/shard_map/summary_round/ppermute | solution.py:332
  28.8 4.4 %attention.1.tokens = bf16[128,2048]{1,0:T(8,128)(2,1)} custom-call(s32[1]{0:T(128)} %bitcast.1.me, s32[1,128]{1,0:T(1,128)} %reshape_reshape.3.owners, bf16[16,32,128]{2,1,0:T(8,128)(2,1)} %get-tuple-element.75.gathered, bf16[128,2048]{1,0:T(8,128)(2,1)} %refs_0_.2, bf16[128,512]{1,0:T(8,128)(2,1)} %refs_1_.3, bf16[128,512]{1,0:T(8,128)(2,1)} %refs_2_.4), custom_call_target="tpu_custom_call" | custom-call | flops 268435456 | bytes 2097152 | tf_op jit(solution)/shard_map/attention/pallas_call | solution.py:151
  33.2 3.5 %collective-permute-done.10.refs_6_ = bf16[128,2048]{1,0:T(8,128)(2,1)} collective-permute-done((bf16[128,2048]{1,0:T(8,128)(2,1)S(1)}, bf16[128,2048]{1,0:T(8,128)(2,1)}, u32[]{:S(2)}, u32[]{:S(2)}) %collective-permute-start.10) | collective-permute-done | bytes 524320 | tf_op jit(solution)/shard_map/weight_2_up/ppermute | solution.py:308
  36.7 1.1 collective-permute-start.14
  37.8 1.0 collective-permute-start.16
  39.9 8.5 %collective-permute-done.14.refs_10_ = bf16[128,2048]{1,0:T(8,128)(2,1)S(1)} collective-permute-done((bf16[128,2048]{1,0:T(8,128)(2,1)}, bf16[128,2048]{1,0:T(8,128)(2,1)S(1)}, u32[]{:S(2)}, u32[]{:S(2)}) %collective-permute-start.14) | collective-permute-done | bytes 524320 | tf_op jit(solution)/shard_map/weight_3_up/ppermute | solution.py:308
  50.4 1.2 collective-permute-start.18
  51.6 1.0 copy-done.3
  52.6 3.4 %project_first.1.acc = f32[128,2048]{1,0:T(8,128)S(1)} custom-call(s32[25]{0:T(128)S(1)} %dynamic-slice_bitcast_fusion.here, bf16[128,2048]{1,0:T(8,128)(2,1)S(1)} %copy-done.3, bf16[128,2048]{1,0:T(8,128)(2,1)S(1)} %copy-done.4, bf16[128,2048]{1,0:T(8,128)(2,1)S(1)} %collective-permute-done.7.refs_1_, bf16[128,2048]{1,0:T(8,128)(2,1)S(1)} %collective-permute-done.2.refs_2_, ...), custom_call_target="tpu_custom_call" | custom-call | flops 939524096 | bytes 7340032 | tf_op jit(solution)/shard_map/project_first/pallas_call | solution.py:196
  56.1 2.1 %collective-permute-done.19.b = bf16[64,2048]{1,0:T(8,128)(2,1)S(1)} collective-permute-done((bf16[64,2048]{1,0:T(8,128)(2,1)S(1)}, bf16[64,2048]{1,0:T(8,128)(2,1)S(1)}, u32[]{:S(2)}, u32[]{:S(2)}) %collective-permute-start.19) | collective-permute-done | bytes 262176 | tf_op jit(solution)/shard_map/weight_far_down/ppermute | solution.py:308
  58.8 0.9 collective-permute-done.21.d
  60.3 1.7 %project_last.1 = (f32[128,2048]{1,0:T(8,128)S(1)}, bf16[128,2048]{1,0:T(8,128)(2,1)}, bf16[128,2048]{1,0:T(8,128)(2,1)S(1)}) custom-call(s32[25]{0:T(128)S(1)} %dynamic-slice_bitcast_fusion.here, bf16[128,2048]{1,0:T(8,128)(2,1)S(1)} %copy-done.3, f32[128,2048]{1,0:T(8,128)S(1)} %project_first.1.acc, f32[1,2048]{1,0:T(1,128)S(1)} %bitcast.17, ...), custom_call_target="tpu_custom_call" | custom-call | flops 134217728 | bytes 3145728 | tf_op jit(solution)/shard_map/project_last/pallas_call | solution.py:225
  62.1 1.2 collective-permute-start.22
  64.1 11.9 %collective-permute-done.22.refs_0_ = bf16[128,2048]{1,0:T(8,128)(2,1)S(1)} collective-permute-done((bf16[128,2048]{1,0:T(8,128)(2,1)S(1)}, bf16[128,2048]{1,0:T(8,128)(2,1)S(1)}, u32[]{:S(2)}, u32[]{:S(2)}) %collective-permute-start.22) | collective-permute-done | bytes 524320 | tf_op jit(solution)/shard_map/token_1_up/ppermute | solution.py:308
  77.8 1.1 collective-permute-start.23
  79.0 5.6 %experts.5 = (bf16[128,2048]{1,0:T(8,128)(2,1)S(1)}, bf16[128,2048]{1,0:T(8,128)(2,1)S(1)}, bf16[256,2048]{1,0:T(8,128)(2,1)S(1)}) custom-call(s32[25]{0:T(128)S(1)} %dynamic-slice_bitcast_fusion.here, f32[16,128]{1,0:T(8,128)S(1)} %fusion.table, bf16[128,2048]{1,0:T(8,128)(2,1)S(1)} %collective-permute-done.22.refs_0_, ...), custom_call_target="tpu_custom_call" | custom-call | tf_op jit(solution)/shard_map/experts/pallas_call | solution.py:279
  84.6 6.6 %collective-permute-done.28.refs_1_ = bf16[128,2048]{1,0:T(8,128)(2,1)S(1)} collective-permute-done((bf16[128,2048]{1,0:T(8,128)(2,1)S(1)}, bf16[128,2048]{1,0:T(8,128)(2,1)S(1)}, u32[]{:S(2)}, u32[]{:S(2)}) %collective-permute-start.28) | collective-permute-done | bytes 524320 | tf_op jit(solution)/shard_map/token_2_down/ppermute | solution.py:308
  92.7 1.2 collective-permute-start.27
  93.9 5.6 %experts.6 = (bf16[128,2048]{1,0:T(8,128)(2,1)S(1)}, bf16[128,2048]{1,0:T(8,128)(2,1)S(1)}, bf16[256,2048]{1,0:T(8,128)(2,1)S(1)}) custom-call(s32[25]{0:T(128)S(1)} %dynamic-slice_bitcast_fusion.here, f32[16,128]{1,0:T(8,128)S(1)} %fusion.table, bf16[128,2048]{1,0:T(8,128)(2,1)S(1)} %collective-permute-done.23.refs_0_, ...), custom_call_target="tpu_custom_call" | custom-call | tf_op jit(solution)/shard_map/experts/pallas_call | solution.py:279
  100.1 6.1 %collective-permute-done.34.refs_1_ = bf16[128,2048]{1,0:T(8,128)(2,1)S(1)} collective-permute-done((bf16[128,2048]{1,0:T(8,128)(2,1)S(1)}, bf16[128,2048]{1,0:T(8,128)(2,1)S(1)}, u32[]{:S(2)}, u32[]{:S(2)}) %collective-permute-start.34) | collective-permute-done | bytes 524320 | tf_op jit(solution)/shard_map/token_3_down/ppermute | solution.py:308
  108.1 1.1 collective-permute-start.31
  109.3 5.6 %experts.7 = (bf16[128,2048]{1,0:T(8,128)(2,1)S(1)}, bf16[128,2048]{1,0:T(8,128)(2,1)S(1)}, bf16[256,2048]{1,0:T(8,128)(2,1)S(1)}) custom-call(s32[25]{0:T(128)S(1)} %dynamic-slice_bitcast_fusion.here, f32[16,128]{1,0:T(8,128)S(1)} %fusion.table, bf16[128,2048]{1,0:T(8,128)(2,1)S(1)} %collective-permute-done.27.refs_0_, ...), custom_call_target="tpu_custom_call" | custom-call | tf_op jit(solution)/shard_map/experts/pallas_call | solution.py:279
  115.4 1.1 collective-permute-done.31.refs_0_
  116.9 1.1 collective-permute-done.38.refs_2_
  118.0 3.2 %experts.8 = (bf16[64,2048]{1,0:T(8,128)(2,1)S(1)}, bf16[64,2048]{1,0:T(8,128)(2,1)S(1)}, bf16[128,2048]{1,0:T(8,128)(2,1)S(1)}) custom-call(s32[25]{0:T(128)S(1)} %dynamic-slice_bitcast_fusion.here, f32[16,128]{1,0:T(8,128)S(1)} %fusion.table, bf16[64,2048]{1,0:T(8,128)(2,1)S(1)} %collective-permute-done.31.refs_0_, ...), custom_call_target="tpu_custom_call" | custom-call | tf_op jit(solution)/shard_map/experts/pallas_call | solution.py:279
  121.8 1.4 collective-permute-done.40
  123.2 1.2 collective-permute-start.44
  124.5 0.9 collective-permute-start.45
  125.4 6.2 %collective-permute-done.44 = bf16[64,2048]{1,0:T(8,128)(2,1)S(1)} collective-permute-done((bf16[64,2048]{1,0:T(8,128)(2,1)S(1)}, bf16[64,2048]{1,0:T(8,128)(2,1)S(1)}, u32[]{:S(2)}, u32[]{:S(2)}) %collective-permute-start.44) | collective-permute-done | bytes 262176 | tf_op jit(solution)/shard_map/sum_far_up/ppermute | solution.py:308
  131.8 1.2 collective-permute-start.46
  133.2 0.9 collective-permute-start.47
  134.2 10.9 %collective-permute-done.46 = bf16[128,2048]{1,0:T(8,128)(2,1)S(1)} collective-permute-done((bf16[128,2048]{1,0:T(8,128)(2,1)S(1)}, bf16[128,2048]{1,0:T(8,128)(2,1)S(1)}, u32[]{:S(2)}, u32[]{:S(2)}) %collective-permute-start.46) | collective-permute-done | bytes 524320 | tf_op jit(solution)/shard_map/sum_3_up/ppermute | solution.py:308
  145.3 1.2 collective-permute-start.48
  146.7 1.1 collective-permute-start.50
  147.9 3.2 %experts.9 = (bf16[128,2048]{1,0:T(8,128)(2,1)S(1)}, bf16[128,2048]{1,0:T(8,128)(2,1)S(1)}) custom-call(s32[25]{0:T(128)S(1)} %dynamic-slice_bitcast_fusion.here, f32[16,128]{1,0:T(8,128)S(1)} %fusion.table, bf16[128,2048]{1,0:T(8,128)(2,1)S(1)} %get-tuple-element.61.refs_0_, bf16[128,2048]{1,0:T(8,128)(2,1)S(1)} %collective-permute-done.41.refs_1_, ...), custom_call_target="tpu_custom_call" | custom-call | tf_op jit(solution)/shard_map/experts/pallas_call | solution.py:279
  151.2 6.4 %collective-permute-done.48 = bf16[128,2048]{1,0:T(8,128)(2,1)S(1)} collective-permute-done((bf16[128,2048]{1,0:T(8,128)(2,1)S(1)}, bf16[128,2048]{1,0:T(8,128)(2,1)S(1)}, u32[]{:S(2)}, u32[]{:S(2)}) %collective-permute-start.48) | collective-permute-done | bytes 524320 | tf_op jit(solution)/shard_map/sum_2_up/ppermute | solution.py:308
  157.8 1.1 collective-permute-done.50
  159.2 0.9 collective-permute-start.51
  160.1 1.1 collective-permute-start.49
  161.3 9.0 %collective-permute-done.51 = bf16[128,2048]{1,0:T(8,128)(2,1)S(1)} collective-permute-done((bf16[128,2048]{1,0:T(8,128)(2,1)S(1)}, bf16[128,2048]{1,0:T(8,128)(2,1)S(1)}, u32[]{:S(2)}, u32[]{:S(2)}) %collective-permute-start.51) | collective-permute-done | bytes 524320 | tf_op jit(solution)/shard_map/sum_1_down/ppermute | solution.py:308
  170.8 1.2 add_convert_fusion
  (104 shorter events, 20.7 us)
Async XLA Ops:
  0.6 19.5 %collective-permute-start.2 = (bf16[128,2048]{1,0:T(8,128)(2,1)}, bf16[128,2048]{1,0:T(8,128)(2,1)S(1)}, u32[]{:S(2)}, u32[]{:S(2)}) collective-permute-start(bf16[128,2048]{1,0:T(8,128)(2,1)} %refs_0_.3), channel_id=1, source_target_pairs={{0,4},{1,5},{4,8},{5,9},{8,12},{9,13},{12,14},{13,15},{14,10},{15,... | collective-permute-start | bytes 1572872 | tf_op jit(solution)/shard_map/weight_1_up/ppermute | solution.py:308
  3.7 16.4 %collective-permute-start.3 = (bf16[128,2048]{1,0:T(8,128)(2,1)}, bf16[128,2048]{1,0:T(8,128)(2,1)S(1)}, u32[]{:S(2)}, u32[]{:S(2)}) collective-permute-start(bf16[128,2048]{1,0:T(8,128)(2,1)} %refs_0_.3), channel_id=1, source_target_pairs={{0,2},{1,3},{4,0},{5,1},{8,4},{9,5},{12,8},{13,9},{14,12},{15,13},... | collective-permute-start | bytes 1572872 | tf_op jit(solution)/shard_map/weight_1_down/ppermute | solution.py:308
  5.7 33.0 %collective-permute-start.7 = (bf16[128,2048]{1,0:T(8,128)(2,1)}, bf16[128,2048]{1,0:T(8,128)(2,1)S(1)}, u32[]{:S(2)}, u32[]{:S(2)}) collective-permute-start(bf16[128,2048]{1,0:T(8,128)(2,1)} %refs_0_.3), channel_id=1, source_target_pairs={{0,1},{1,0},{2,3},{3,2},{4,5},{5,4},{6,7},{7,6},{8,9},{9,8},{10,11... | collective-permute-start | bytes 1572872 | tf_op jit(solution)/shard_map/swap_cores/ppermute | solution.py:313
  7.8 11.6 %collective-permute-start.1 = (bf16[2,64,128]{2,1,0:T(8,128)(2,1)S(1)}, bf16[2,64,128]{2,1,0:T(8,128)(2,1)S(1)}, u32[]{:S(2)}, u32[]{:S(2)}) collective-permute-start(bf16[2,64,128]{2,1,0:T(8,128)(2,1)S(1)} %pad_maximum_fusion.1), channel_id=1, source_target_pairs={{0,8},{1,9},{2,10},{3,11},{4,12},{5,13},{6,14},{7,15},{8,0},{9,1},... | collective-permute-start | bytes 98312 | tf_op jit(solution)/shard_map/summary_round/ppermute | solution.py:332
  20.1 5.2 %collective-permute-start.4 = (bf16[4,64,128]{2,1,0:T(8,128)(2,1)S(1)}, bf16[4,64,128]{2,1,0:T(8,128)(2,1)S(1)}, u32[]{:S(2)}, u32[]{:S(2)}) collective-permute-start(bf16[4,64,128]{2,1,0:T(8,128)(2,1)S(1)} %pad_maximum_fusion), channel_id=1, source_target_pairs={{0,2},{1,3},{2,0},{3,1},{4,6},{5,7},{6,4},{7,5},{8,10},{9,11},{10,... | collective-permute-start | bytes 196616 | tf_op jit(solution)/shard_map/summary_round/ppermute | solution.py:332
  20.4 5.4 %collective-permute-start.5 = (bf16[4,64,128]{2,1,0:T(8,128)(2,1)S(1)}, bf16[4,64,128]{2,1,0:T(8,128)(2,1)S(1)}, u32[]{:S(2)}, u32[]{:S(2)}) collective-permute-start(bf16[4,64,128]{2,1,0:T(8,128)(2,1)S(1)} %pad_maximum_fusion), channel_id=1, source_target_pairs={{0,4},{1,5},{2,6},{3,7},{4,0},{5,1},{6,2},{7,3},{8,12},{9,13},{10,... | collective-permute-start | bytes 196616 | tf_op jit(solution)/shard_map/summary_round/ppermute | solution.py:332
  21.6 6.4 %collective-permute-start.6 = (bf16[4,64,128]{2,1,0:T(8,128)(2,1)S(1)}, bf16[4,64,128]{2,1,0:T(8,128)(2,1)S(1)}, u32[]{:S(2)}, u32[]{:S(2)}) collective-permute-start(bf16[4,64,128]{2,1,0:T(8,128)(2,1)S(1)} %pad_maximum_fusion), channel_id=1, source_target_pairs={{0,6},{1,7},{2,4},{3,5},{4,2},{5,3},{6,0},{7,1},{8,14},{9,15},{10,... | collective-permute-start | bytes 196616 | tf_op jit(solution)/shard_map/summary_round/ppermute | solution.py:332
  23.7 13.0 %collective-permute-start.10 = (bf16[128,2048]{1,0:T(8,128)(2,1)S(1)}, bf16[128,2048]{1,0:T(8,128)(2,1)}, u32[]{:S(2)}, u32[]{:S(2)}) collective-permute-start(bf16[128,2048]{1,0:T(8,128)(2,1)S(1)} %collective-permute-done.2.refs_2_), channel_id=1, source_target_pairs={{0,4},{1,5},{4,8},{5,9},{8,12},{9,13},{12,14},{13,15},{14,10},{15,... | collective-permute-start | bytes 1572872 | tf_op jit(solution)/shard_map/weight_2_up/ppermute | solution.py:308
  25.4 12.4 %collective-permute-start.12 = (bf16[128,2048]{1,0:T(8,128)(2,1)S(1)}, bf16[128,2048]{1,0:T(8,128)(2,1)}, u32[]{:S(2)}, u32[]{:S(2)}) collective-permute-start(bf16[128,2048]{1,0:T(8,128)(2,1)S(1)} %collective-permute-done.3.refs_4_), channel_id=1, source_target_pairs={{0,2},{1,3},{4,0},{5,1},{8,4},{9,5},{12,8},{13,9},{14,12},{15,13},... | collective-permute-start | bytes 1572872 | tf_op jit(solution)/shard_map/weight_2_down/ppermute | solution.py:308
  25.8 14.1 %collective-permute-start.8 = (bf16[128,2048]{1,0:T(8,128)(2,1)S(1)}, bf16[128,2048]{1,0:T(8,128)(2,1)}, u32[]{:S(2)}, u32[]{:S(2)}) collective-permute-start(bf16[128,2048]{1,0:T(8,128)(2,1)S(1)} %collective-permute-done.2.refs_2_), channel_id=1, source_target_pairs={{0,1},{1,0},{2,3},{3,2},{4,5},{5,4},{6,7},{7,6},{8,9},{9,8},{10,11... | collective-permute-start | bytes 1572872 | tf_op jit(solution)/shard_map/swap_cores/ppermute | solution.py:313
  36.7 11.8 %collective-permute-start.14 = (bf16[128,2048]{1,0:T(8,128)(2,1)}, bf16[128,2048]{1,0:T(8,128)(2,1)S(1)}, u32[]{:S(2)}, u32[]{:S(2)}) collective-permute-start(bf16[128,2048]{1,0:T(8,128)(2,1)} %collective-permute-done.10.refs_6_), channel_id=1, source_target_pairs={{0,4},{1,5},{4,8},{5,9},{8,12},{9,13},{12,14},{13,15},{14,10},{15,... | collective-permute-start | bytes 1572872 | tf_op jit(solution)/shard_map/weight_3_up/ppermute | solution.py:308
  37.8 11.6 %collective-permute-start.16 = (bf16[128,2048]{1,0:T(8,128)(2,1)}, bf16[128,2048]{1,0:T(8,128)(2,1)S(1)}, u32[]{:S(2)}, u32[]{:S(2)}) collective-permute-start(bf16[128,2048]{1,0:T(8,128)(2,1)} %collective-permute-done.12.refs_8_), channel_id=1, source_target_pairs={{0,2},{1,3},{4,0},{5,1},{8,4},{9,5},{12,8},{13,9},{14,12},{15,13},... | collective-permute-start | bytes 1572872 | tf_op jit(solution)/shard_map/weight_3_down/ppermute | solution.py:308
  38.7 10.7 %collective-permute-start.9 = (bf16[128,2048]{1,0:T(8,128)(2,1)S(1)}, bf16[128,2048]{1,0:T(8,128)(2,1)}, u32[]{:S(2)}, u32[]{:S(2)}) collective-permute-start(bf16[128,2048]{1,0:T(8,128)(2,1)S(1)} %collective-permute-done.3.refs_4_), channel_id=1, source_target_pairs={{0,1},{1,0},{2,3},{3,2},{4,5},{5,4},{6,7},{7,6},{8,9},{9,8},{10,11... | collective-permute-start | bytes 1572872 | tf_op jit(solution)/shard_map/swap_cores/ppermute | solution.py:313
  38.7 11.6 %collective-permute-start.11 = (bf16[128,2048]{1,0:T(8,128)(2,1)}, bf16[128,2048]{1,0:T(8,128)(2,1)}, u32[]{:S(2)}, u32[]{:S(2)}) collective-permute-start(bf16[128,2048]{1,0:T(8,128)(2,1)} %collective-permute-done.10.refs_6_), channel_id=1, source_target_pairs={{0,1},{1,0},{2,3},{3,2},{4,5},{5,4},{6,7},{7,6},{8,9},{9,8},{10,11... | collective-permute-start | bytes 1572872 | tf_op jit(solution)/shard_map/swap_cores/ppermute | solution.py:313
  39.9 11.6 %collective-permute-start.13 = (bf16[128,2048]{1,0:T(8,128)(2,1)}, bf16[128,2048]{1,0:T(8,128)(2,1)S(1)}, u32[]{:S(2)}, u32[]{:S(2)}) collective-permute-start(bf16[128,2048]{1,0:T(8,128)(2,1)} %collective-permute-done.12.refs_8_), channel_id=1, source_target_pairs={{0,1},{1,0},{2,3},{3,2},{4,5},{5,4},{6,7},{7,6},{8,9},{9,8},{10,11... | collective-permute-start | bytes 1572872 | tf_op jit(solution)/shard_map/swap_cores/ppermute | solution.py:313
  48.5 3.1 %collective-permute-start.15 = (bf16[128,2048]{1,0:T(8,128)(2,1)S(1)}, bf16[128,2048]{1,0:T(8,128)(2,1)S(1)}, u32[]{:S(2)}, u32[]{:S(2)}) collective-permute-start(bf16[128,2048]{1,0:T(8,128)(2,1)S(1)} %collective-permute-done.14.refs_10_), channel_id=1, source_target_pairs={{0,1},{1,0},{2,3},{3,2},{4,5},{5,4},{6,7},{7,6},{8,9},{9,8},{10,11... | collective-permute-start | bytes 1572872 | tf_op jit(solution)/shard_map/swap_cores/ppermute | solution.py:313
  49.3 2.2 %collective-permute-start.17 = (bf16[128,2048]{1,0:T(8,128)(2,1)S(1)}, bf16[128,2048]{1,0:T(8,128)(2,1)S(1)}, u32[]{:S(2)}, u32[]{:S(2)}) collective-permute-start(bf16[128,2048]{1,0:T(8,128)(2,1)S(1)} %collective-permute-done.16.refs_12_), channel_id=1, source_target_pairs={{0,1},{1,0},{2,3},{3,2},{4,5},{5,4},{6,7},{7,6},{8,9},{9,8},{10,11... | collective-permute-start | bytes 1572872 | tf_op jit(solution)/shard_map/swap_cores/ppermute | solution.py:313
  49.4 8.8 %collective-permute-start.19 = (bf16[64,2048]{1,0:T(8,128)(2,1)S(1)}, bf16[64,2048]{1,0:T(8,128)(2,1)S(1)}, u32[]{:S(2)}, u32[]{:S(2)}) collective-permute-start(bf16[64,2048]{1,0:T(8,128)(2,1)S(1)} %slice.69), channel_id=1, source_target_pairs={{0,2},{1,3},{4,0},{5,1},{8,4},{9,5},{12,8},{13,9},{14,12},{15,13},... | collective-permute-start | bytes 786440 | tf_op jit(solution)/shard_map/weight_far_down/ppermute | solution.py:308
  50.4 8.4 %collective-permute-start.18 = (bf16[64,2048]{1,0:T(8,128)(2,1)S(1)}, bf16[64,2048]{1,0:T(8,128)(2,1)S(1)}, u32[]{:S(2)}, u32[]{:S(2)}) collective-permute-start(bf16[64,2048]{1,0:T(8,128)(2,1)S(1)} %slice.65), channel_id=1, source_target_pairs={{0,4},{1,5},{4,8},{5,9},{8,12},{9,13},{12,14},{13,15},{14,10},{15,... | collective-permute-start | bytes 786440 | tf_op jit(solution)/shard_map/weight_far_up/ppermute | solution.py:308
  62.1 14.0 %collective-permute-start.22 = (bf16[128,2048]{1,0:T(8,128)(2,1)S(1)}, bf16[128,2048]{1,0:T(8,128)(2,1)S(1)}, u32[]{:S(2)}, u32[]{:S(2)}) collective-permute-start(bf16[128,2048]{1,0:T(8,128)(2,1)S(1)} %get-tuple-element.61.refs_0_), channel_id=1, source_target_pairs={{0,4},{1,5},{4,8},{5,9},{8,12},{9,13},{12,14},{13,15},{14,10},{15,... | collective-permute-start | bytes 1572872 | tf_op jit(solution)/shard_map/token_1_up/ppermute | solution.py:308
  63.2 13.7 %collective-permute-start.24 = (bf16[128,2048]{1,0:T(8,128)(2,1)S(1)}, bf16[128,2048]{1,0:T(8,128)(2,1)S(1)}, u32[]{:S(2)}, u32[]{:S(2)}) collective-permute-start(bf16[128,2048]{1,0:T(8,128)(2,1)S(1)} %get-tuple-element.61.refs_0_), channel_id=1, source_target_pairs={{0,2},{1,3},{4,0},{5,1},{8,4},{9,5},{12,8},{13,9},{14,12},{15,13},... | collective-permute-start | bytes 1572872 | tf_op jit(solution)/shard_map/token_1_down/ppermute | solution.py:308
  76.1 2.9 %collective-permute-start.25 = (bf16[128,2048]{1,0:T(8,128)(2,1)S(1)}, bf16[128,2048]{1,0:T(8,128)(2,1)S(1)}, u32[]{:S(2)}, u32[]{:S(2)}) collective-permute-start(bf16[128,2048]{1,0:T(8,128)(2,1)S(1)} %collective-permute-done.22.refs_0_), channel_id=1, source_target_pairs={{0,1},{1,0},{2,3},{3,2},{4,5},{5,4},{6,7},{7,6},{8,9},{9,8},{10,11... | collective-permute-start | bytes 1572872 | tf_op jit(solution)/shard_map/swap_cores/ppermute | solution.py:313
  76.9 2.0 %collective-permute-start.26 = (bf16[128,2048]{1,0:T(8,128)(2,1)S(1)}, bf16[128,2048]{1,0:T(8,128)(2,1)S(1)}, u32[]{:S(2)}, u32[]{:S(2)}) collective-permute-start(bf16[128,2048]{1,0:T(8,128)(2,1)S(1)} %collective-permute-done.24.refs_1_), channel_id=1, source_target_pairs={{0,1},{1,0},{2,3},{3,2},{4,5},{5,4},{6,7},{7,6},{8,9},{9,8},{10,11... | collective-permute-start | bytes 1572872 | tf_op jit(solution)/shard_map/swap_cores/ppermute | solution.py:313
  76.9 14.3 %collective-permute-start.28 = (bf16[128,2048]{1,0:T(8,128)(2,1)S(1)}, bf16[128,2048]{1,0:T(8,128)(2,1)S(1)}, u32[]{:S(2)}, u32[]{:S(2)}) collective-permute-start(bf16[128,2048]{1,0:T(8,128)(2,1)S(1)} %collective-permute-done.24.refs_1_), channel_id=1, source_target_pairs={{0,2},{1,3},{4,0},{5,1},{8,4},{9,5},{12,8},{13,9},{14,12},{15,13},... | collective-permute-start | bytes 1572872 | tf_op jit(solution)/shard_map/token_2_down/ppermute | solution.py:308
  77.8 14.1 %collective-permute-start.23 = (bf16[128,2048]{1,0:T(8,128)(2,1)S(1)}, bf16[128,2048]{1,0:T(8,128)(2,1)S(1)}, u32[]{:S(2)}, u32[]{:S(2)}) collective-permute-start(bf16[128,2048]{1,0:T(8,128)(2,1)S(1)} %collective-permute-done.22.refs_0_), channel_id=1, source_target_pairs={{0,4},{1,5},{4,8},{5,9},{8,12},{9,13},{12,14},{13,15},{14,10},{15,... | collective-permute-start | bytes 1572872 | tf_op jit(solution)/shard_map/token_2_up/ppermute | solution.py:308
  91.3 2.6 %collective-permute-start.30 = (bf16[128,2048]{1,0:T(8,128)(2,1)S(1)}, bf16[128,2048]{1,0:T(8,128)(2,1)S(1)}, u32[]{:S(2)}, u32[]{:S(2)}) collective-permute-start(bf16[128,2048]{1,0:T(8,128)(2,1)S(1)} %collective-permute-done.28.refs_1_), channel_id=1, source_target_pairs={{0,1},{1,0},{2,3},{3,2},{4,5},{5,4},{6,7},{7,6},{8,9},{9,8},{10,11... | collective-permute-start | bytes 1572872 | tf_op jit(solution)/shard_map/swap_cores/ppermute | solution.py:313
  91.9 2.1 %collective-permute-start.29 = (bf16[128,2048]{1,0:T(8,128)(2,1)S(1)}, bf16[128,2048]{1,0:T(8,128)(2,1)S(1)}, u32[]{:S(2)}, u32[]{:S(2)}) collective-permute-start(bf16[128,2048]{1,0:T(8,128)(2,1)S(1)} %collective-permute-done.23.refs_0_), channel_id=1, source_target_pairs={{0,1},{1,0},{2,3},{3,2},{4,5},{5,4},{6,7},{7,6},{8,9},{9,8},{10,11... | collective-permute-start | bytes 1572872 | tf_op jit(solution)/shard_map/swap_cores/ppermute | solution.py:313
  91.9 14.3 %collective-permute-start.34 = (bf16[128,2048]{1,0:T(8,128)(2,1)S(1)}, bf16[128,2048]{1,0:T(8,128)(2,1)S(1)}, u32[]{:S(2)}, u32[]{:S(2)}) collective-permute-start(bf16[128,2048]{1,0:T(8,128)(2,1)S(1)} %collective-permute-done.28.refs_1_), channel_id=1, source_target_pairs={{0,2},{1,3},{4,0},{5,1},{8,4},{9,5},{12,8},{13,9},{14,12},{15,13},... | collective-permute-start | bytes 1572872 | tf_op jit(solution)/shard_map/token_3_down/ppermute | solution.py:308
  92.7 13.9 %collective-permute-start.27 = (bf16[128,2048]{1,0:T(8,128)(2,1)S(1)}, bf16[128,2048]{1,0:T(8,128)(2,1)S(1)}, u32[]{:S(2)}, u32[]{:S(2)}) collective-permute-start(bf16[128,2048]{1,0:T(8,128)(2,1)S(1)} %collective-permute-done.23.refs_0_), channel_id=1, source_target_pairs={{0,4},{1,5},{4,8},{5,9},{8,12},{9,13},{12,14},{13,15},{14,10},{15,... | collective-permute-start | bytes 1572872 | tf_op jit(solution)/shard_map/token_3_up/ppermute | solution.py:308
  93.9 21.5 %collective-permute-start.32 = (bf16[256,2048]{1,0:T(8,128)(2,1)S(1)}, bf16[256,2048]{1,0:T(8,128)(2,1)S(1)}, u32[]{:S(2)}, u32[]{:S(2)}) collective-permute-start(bf16[256,2048]{1,0:T(8,128)(2,1)S(1)} %get-tuple-element.51), channel_id=1, source_target_pairs={{0,1},{1,0},{2,3},{3,2},{4,5},{5,4},{6,7},{7,6},{8,9},{9,8},{10,11... | collective-permute-start | bytes 3145736 | tf_op jit(solution)/shard_map/swap_cores/ppermute | solution.py:313
  99.6 15.8 %collective-permute-start.33 = (bf16[256,2048]{1,0:T(8,128)(2,1)S(1)}, bf16[256,2048]{1,0:T(8,128)(2,1)S(1)}, u32[]{:S(2)}, u32[]{:S(2)}) collective-permute-start(bf16[256,2048]{1,0:T(8,128)(2,1)S(1)} %get-tuple-element.52), channel_id=1, source_target_pairs={{0,1},{1,0},{2,3},{3,2},{4,5},{5,4},{6,7},{7,6},{8,9},{9,8},{10,11... | collective-permute-start | bytes 3145736 | tf_op jit(solution)/shard_map/swap_cores/ppermute | solution.py:313
  106.2 1.9 %collective-permute-start.36 = (bf16[128,2048]{1,0:T(8,128)(2,1)S(1)}, bf16[128,2048]{1,0:T(8,128)(2,1)S(1)}, u32[]{:S(2)}, u32[]{:S(2)}) collective-permute-start(bf16[128,2048]{1,0:T(8,128)(2,1)S(1)} %collective-permute-done.34.refs_1_), channel_id=1, source_target_pairs={{0,1},{1,0},{2,3},{3,2},{4,5},{5,4},{6,7},{7,6},{8,9},{9,8},{10,11... | collective-permute-start | bytes 1572872 | tf_op jit(solution)/shard_map/swap_cores/ppermute | solution.py:313
  106.6 2.7 %collective-permute-start.35 = (bf16[128,2048]{1,0:T(8,128)(2,1)S(1)}, bf16[128,2048]{1,0:T(8,128)(2,1)S(1)}, u32[]{:S(2)}, u32[]{:S(2)}) collective-permute-start(bf16[128,2048]{1,0:T(8,128)(2,1)S(1)} %collective-permute-done.27.refs_0_), channel_id=1, source_target_pairs={{0,1},{1,0},{2,3},{3,2},{4,5},{5,4},{6,7},{7,6},{8,9},{9,8},{10,11... | collective-permute-start | bytes 1572872 | tf_op jit(solution)/shard_map/swap_cores/ppermute | solution.py:313
  106.7 8.6 %collective-permute-start.37 = (bf16[64,2048]{1,0:T(8,128)(2,1)S(1)}, bf16[64,2048]{1,0:T(8,128)(2,1)S(1)}, u32[]{:S(2)}, u32[]{:S(2)}) collective-permute-start(bf16[64,2048]{1,0:T(8,128)(2,1)S(1)} %slice.55), channel_id=1, source_target_pairs={{0,2},{1,3},{4,0},{5,1},{8,4},{9,5},{12,8},{13,9},{14,12},{15,13},... | collective-permute-start | bytes 786440 | tf_op jit(solution)/shard_map/token_far_down/ppermute | solution.py:308
  108.1 8.3 %collective-permute-start.31 = (bf16[64,2048]{1,0:T(8,128)(2,1)S(1)}, bf16[64,2048]{1,0:T(8,128)(2,1)S(1)}, u32[]{:S(2)}, u32[]{:S(2)}) collective-permute-start(bf16[64,2048]{1,0:T(8,128)(2,1)S(1)} %slice.54), channel_id=1, source_target_pairs={{0,4},{1,5},{4,8},{5,9},{8,12},{9,13},{12,14},{13,15},{14,10},{15,... | collective-permute-start | bytes 786440 | tf_op jit(solution)/shard_map/token_far_up/ppermute | solution.py:308
  115.4 1.5 collective-permute-start.39
  121.2 2.0 %collective-permute-start.40 = (bf16[128,2048]{1,0:T(8,128)(2,1)S(1)}, bf16[128,2048]{1,0:T(8,128)(2,1)S(1)}, u32[]{:S(2)}, u32[]{:S(2)}) collective-permute-start(bf16[128,2048]{1,0:T(8,128)(2,1)S(1)} %get-tuple-element.59), channel_id=1, source_target_pairs={{0,1},{1,0},{2,3},{3,2},{4,5},{5,4},{6,7},{7,6},{8,9},{9,8},{10,11... | collective-permute-start | bytes 1572872 | tf_op jit(solution)/shard_map/swap_cores/ppermute | solution.py:313
  121.4 4.0 %collective-permute-start.43 = (bf16[256,2048]{1,0:T(8,128)(2,1)S(1)}, bf16[256,2048]{1,0:T(8,128)(2,1)S(1)}, u32[]{:S(2)}, u32[]{:S(2)}) collective-permute-start(bf16[256,2048]{1,0:T(8,128)(2,1)S(1)} %get-tuple-element.68), channel_id=1, source_target_pairs={{0,1},{1,0},{2,3},{3,2},{4,5},{5,4},{6,7},{7,6},{8,9},{9,8},{10,11... | collective-permute-start | bytes 3145736 | tf_op jit(solution)/shard_map/swap_cores/ppermute | solution.py:313
  123.2 8.4 %collective-permute-start.44 = (bf16[64,2048]{1,0:T(8,128)(2,1)S(1)}, bf16[64,2048]{1,0:T(8,128)(2,1)S(1)}, u32[]{:S(2)}, u32[]{:S(2)}) collective-permute-start(bf16[64,2048]{1,0:T(8,128)(2,1)S(1)} %add_convert_fusion.8), channel_id=1, source_target_pairs={{0,4},{1,5},{4,8},{5,9},{8,12},{9,13},{12,14},{13,15},{14,10},{15,... | collective-permute-start | bytes 786440 | tf_op jit(solution)/shard_map/sum_far_up/ppermute | solution.py:308
  124.5 8.5 %collective-permute-start.45 = (bf16[64,2048]{1,0:T(8,128)(2,1)S(1)}, bf16[64,2048]{1,0:T(8,128)(2,1)S(1)}, u32[]{:S(2)}, u32[]{:S(2)}) collective-permute-start(bf16[64,2048]{1,0:T(8,128)(2,1)S(1)} %add_convert_fusion.7), channel_id=1, source_target_pairs={{0,2},{1,3},{4,0},{5,1},{8,4},{9,5},{12,8},{13,9},{14,12},{15,13},... | collective-permute-start | bytes 786440 | tf_op jit(solution)/shard_map/sum_far_down/ppermute | solution.py:308
  131.8 13.2 %collective-permute-start.46 = (bf16[128,2048]{1,0:T(8,128)(2,1)S(1)}, bf16[128,2048]{1,0:T(8,128)(2,1)S(1)}, u32[]{:S(2)}, u32[]{:S(2)}) collective-permute-start(bf16[128,2048]{1,0:T(8,128)(2,1)S(1)} %add_convert_fusion.6), channel_id=1, source_target_pairs={{0,4},{1,5},{4,8},{5,9},{8,12},{9,13},{12,14},{13,15},{14,10},{15,... | collective-permute-start | bytes 1572872 | tf_op jit(solution)/shard_map/sum_3_up/ppermute | solution.py:308
  133.2 13.3 %collective-permute-start.47 = (bf16[128,2048]{1,0:T(8,128)(2,1)S(1)}, bf16[128,2048]{1,0:T(8,128)(2,1)S(1)}, u32[]{:S(2)}, u32[]{:S(2)}) collective-permute-start(bf16[128,2048]{1,0:T(8,128)(2,1)S(1)} %add_convert_fusion.5), channel_id=1, source_target_pairs={{0,2},{1,3},{4,0},{5,1},{8,4},{9,5},{12,8},{13,9},{14,12},{15,13},... | collective-permute-start | bytes 1572872 | tf_op jit(solution)/shard_map/sum_3_down/ppermute | solution.py:308
  134.1 13.7 %collective-permute-start.41 = (bf16[128,2048]{1,0:T(8,128)(2,1)S(1)}, bf16[128,2048]{1,0:T(8,128)(2,1)S(1)}, u32[]{:S(2)}, u32[]{:S(2)}) collective-permute-start(bf16[128,2048]{1,0:T(8,128)(2,1)S(1)} %get-tuple-element.61.refs_0_), channel_id=1, source_target_pairs={{0,1},{1,0},{2,3},{3,2},{4,5},{5,4},{6,7},{7,6},{8,9},{9,8},{10,11... | collective-permute-start | bytes 1572872 | tf_op jit(solution)/shard_map/swap_cores/ppermute | solution.py:313
  145.3 12.3 %collective-permute-start.48 = (bf16[128,2048]{1,0:T(8,128)(2,1)S(1)}, bf16[128,2048]{1,0:T(8,128)(2,1)S(1)}, u32[]{:S(2)}, u32[]{:S(2)}) collective-permute-start(bf16[128,2048]{1,0:T(8,128)(2,1)S(1)} %add_convert_fusion.4), channel_id=1, source_target_pairs={{0,4},{1,5},{4,8},{5,9},{8,12},{9,13},{12,14},{13,15},{14,10},{15,... | collective-permute-start | bytes 1572872 | tf_op jit(solution)/shard_map/sum_2_up/ppermute | solution.py:308
  146.7 12.2 %collective-permute-start.50 = (bf16[128,2048]{1,0:T(8,128)(2,1)S(1)}, bf16[128,2048]{1,0:T(8,128)(2,1)S(1)}, u32[]{:S(2)}, u32[]{:S(2)}) collective-permute-start(bf16[128,2048]{1,0:T(8,128)(2,1)S(1)} %add_convert_fusion.3), channel_id=1, source_target_pairs={{0,2},{1,3},{4,0},{5,1},{8,4},{9,5},{12,8},{13,9},{14,12},{15,13},... | collective-permute-start | bytes 1572872 | tf_op jit(solution)/shard_map/sum_2_down/ppermute | solution.py:308
  151.1 10.2 %collective-permute-start.42 = (bf16[128,2048]{1,0:T(8,128)(2,1)S(1)}, bf16[128,2048]{1,0:T(8,128)(2,1)S(1)}, u32[]{:S(2)}, u32[]{:S(2)}) collective-permute-start(bf16[128,2048]{1,0:T(8,128)(2,1)S(1)} %get-tuple-element.63), channel_id=1, source_target_pairs={{0,1},{1,0},{2,3},{3,2},{4,5},{5,4},{6,7},{7,6},{8,9},{9,8},{10,11... | collective-permute-start | bytes 1572872 | tf_op jit(solution)/shard_map/swap_cores/ppermute | solution.py:313
  159.2 11.1 %collective-permute-start.51 = (bf16[128,2048]{1,0:T(8,128)(2,1)S(1)}, bf16[128,2048]{1,0:T(8,128)(2,1)S(1)}, u32[]{:S(2)}, u32[]{:S(2)}) collective-permute-start(bf16[128,2048]{1,0:T(8,128)(2,1)S(1)} %add_convert_fusion.1), channel_id=1, source_target_pairs={{0,2},{1,3},{4,0},{5,1},{8,4},{9,5},{12,8},{13,9},{14,12},{15,13},... | collective-permute-start | bytes 1572872 | tf_op jit(solution)/shard_map/sum_1_down/ppermute | solution.py:308
  160.1 10.7 %collective-permute-start.49 = (bf16[128,2048]{1,0:T(8,128)(2,1)S(1)}, bf16[128,2048]{1,0:T(8,128)(2,1)S(1)}, u32[]{:S(2)}, u32[]{:S(2)}) collective-permute-start(bf16[128,2048]{1,0:T(8,128)(2,1)S(1)} %add_convert_fusion.2), channel_id=1, source_target_pairs={{0,4},{1,5},{4,8},{5,9},{8,12},{9,13},{12,14},{13,15},{14,10},{15,... | collective-permute-start | bytes 1572872 | tf_op jit(solution)/shard_map/sum_1_up/ppermute | solution.py:308
  (10 other events, 145.9 us)
